TPU v7x, 32 devices: a whole 2x2x4 slice. The times are simulated.
32 devices in a mesh: outer: 4 (over x, core), inner: 8 (over z, y).
Axes of the slice: x: 2, y: 2, z: 4, core: 2. Of those that a mesh axis runs over, the one named last changes fastest.
Arguments:
- inputs: bfloat16 [128, 16, 16, 512], P(('outer', 'inner')), may hold values from -12 to 12
- cotangent: bfloat16 [128, 16, 16, 2048], P(('outer', 'inner')), may hold values from -12 to 12
- conv_weight: bfloat16 [4608, 512], replicated, may hold values from -1 to 1
- expand_weight: bfloat16 [512, 2048], replicated, may hold values from -2 to 2
- conv_momentum: float32 [32, 73728], P(('outer', 'inner')), may hold values from -6 to 6
- expand_momentum: float32 [32, 32768], P(('outer', 'inner')), may hold values from -6 to 6
Outputs:
- input_grad: bfloat16 [128, 16, 16, 512], P(('outer', 'inner'))
- conv_new: float32 [32, 73728], P(('outer', 'inner'))
- expand_new: float32 [32, 32768], P(('outer', 'inner'))
All inputs are finite; a program needn't handle non-finite values.
Results may differ from a plain program's by a relative error of at most 0.01.
Values may be sent and summed in bfloat16 or wider, within the bound.
No kernel may reach another device: no remote copies, remote signals or barrier semaphores. Data moves between devices by JAX's collectives and lax.ppermute only.
A program may use at most 128 MiB of HBM per device.

v0:
```python
import jax
import jax.numpy as jnp
from jax import lax
from jax.sharding import PartitionSpec as P

EPS = 1e-06
MOMENTUM = 0.9


def from_partner(block, axis, stride):
    count = lax.axis_size(axis)
    route = []
    for low in range(count):
        high = low | 1 << stride
        if high != low and high < count:
            route += [(low, high), (high, low)]
    return lax.ppermute(block, axis, route)


def patches(image):
    images, height, across, channels = image.shape
    padded = jnp.pad(image, ((0, 0), (1, 1), (1, 1), (0, 0)))
    pieces = [
        padded[:, shift_y : shift_y + height, shift_x : shift_x + across, :]
        for shift_y in range(3)
        for shift_x in range(3)
    ]
    return jnp.concatenate(pieces, axis=-1).reshape(images * height * across, 9 * channels)


def local_step(inputs, cotangent, conv_weight, expand_weight):
    images, height, across, channels = inputs.shape
    row_count = images * height * across
    relu_in = jnp.maximum(inputs, jnp.zeros((), inputs.dtype))
    columns = patches(relu_in)
    hidden_pre = jnp.dot(columns, conv_weight, preferred_element_type=jnp.float32).astype(
        jnp.bfloat16
    )
    hidden_act = jnp.maximum(hidden_pre, jnp.zeros((), hidden_pre.dtype))
    grad_rows = cotangent.reshape(row_count, cotangent.shape[-1])
    expand_grad = (
        lax.dot_general(
            hidden_act, grad_rows, (((0,), (0,)), ((), ())), preferred_element_type=jnp.float32
        )
        / row_count
    ).astype(jnp.bfloat16)
    hidden_back = lax.dot_general(
        grad_rows, expand_weight, (((1,), (1,)), ((), ())), preferred_element_type=jnp.float32
    )
    hidden_grad = jnp.where(hidden_pre > 0, hidden_back, 0.0).astype(jnp.bfloat16)
    conv_grad = (
        lax.dot_general(
            hidden_grad, columns, (((0,), (0,)), ((), ())), preferred_element_type=jnp.float32
        )
        / row_count
    ).astype(jnp.bfloat16)
    flipped = (
        conv_weight.reshape(3, 3, channels, channels)[::-1, ::-1]
        .transpose(0, 1, 3, 2)
        .reshape(9 * channels, channels)
    )
    back_cols = patches(hidden_grad.reshape(images, height, across, channels))
    input_back = jnp.dot(back_cols, flipped, preferred_element_type=jnp.float32)
    input_grad = jnp.where(inputs.reshape(row_count, channels) > 0, input_back, 0.0).astype(
        jnp.bfloat16
    )
    return (input_grad.reshape(inputs.shape), conv_grad, expand_grad)


def layer_stats(first, second, conv_len):
    conv_first = first[:, :conv_len]
    conv_second = second[:, :conv_len]
    expand_first = first[:, conv_len:]
    expand_second = second[:, conv_len:]
    return jnp.stack(
        [
            jnp.sum(conv_first * conv_first),
            jnp.sum(conv_second * conv_second),
            jnp.sum(conv_first * conv_second),
            jnp.sum(expand_first * expand_first),
            jnp.sum(expand_second * expand_second),
            jnp.sum(expand_first * expand_second),
        ]
    )


def coef_rows(stats, conv_len, expand_len):
    first_conv = 1.0 - stats[2] / (2.0 * (stats[0] + EPS))
    second_conv = 1.0 - stats[2] / (2.0 * (stats[1] + EPS))
    first_expand = 1.0 - stats[5] / (2.0 * (stats[3] + EPS))
    second_expand = 1.0 - stats[5] / (2.0 * (stats[4] + EPS))
    first_row = jnp.concatenate(
        [
            jnp.full((conv_len,), first_conv, jnp.float32),
            jnp.full((expand_len,), first_expand, jnp.float32),
        ]
    )
    second_row = jnp.concatenate(
        [
            jnp.full((conv_len,), second_conv, jnp.float32),
            jnp.full((expand_len,), second_expand, jnp.float32),
        ]
    )
    return (first_row, second_row)


def body(inputs, cotangent, conv_weight, expand_weight, conv_momentum, expand_momentum):
    input_grad, conv_grad, expand_grad = local_step(inputs, cotangent, conv_weight, expand_weight)
    outer_count = lax.axis_size("outer")
    inner_count = lax.axis_size("inner")
    conv_len = conv_momentum.shape[1]
    expand_len = expand_momentum.shape[1]
    conv_parts = conv_grad.astype(jnp.float32).reshape(outer_count, inner_count, conv_len)
    expand_parts = expand_grad.astype(jnp.float32).reshape(outer_count, inner_count, expand_len)
    joined = jnp.concatenate([conv_parts, expand_parts], axis=2)
    summed = lax.psum_scatter(
        joined.astype(jnp.bfloat16), "inner", scatter_dimension=1, tiled=True
    ).astype(jnp.float32)
    total_len = conv_len + expand_len
    holding = summed.reshape(outer_count, total_len)
    outer_pos = lax.axis_index("outer")
    levels = outer_count.bit_length() - 1
    for step_bit in range(levels):
        partner = from_partner(holding.astype(jnp.bfloat16), "outer", step_bit).astype(
            holding.dtype
        )
        stats = lax.psum(layer_stats(holding, partner, conv_len), "inner")
        mine_coef, partner_coef = coef_rows(stats, conv_len, expand_len)
        holding = mine_coef * holding + partner_coef * partner
    final = lax.dynamic_slice_in_dim(holding, outer_pos, 1, 0)
    conv_new = MOMENTUM * conv_momentum + final[:, :conv_len]
    expand_new = MOMENTUM * expand_momentum + final[:, conv_len:]
    return (input_grad, conv_new, expand_new)


def solution(mesh):
    return jax.shard_map(
        body,
        mesh=mesh,
        in_specs=(
            P(("outer", "inner"), None, None, None),
            P(("outer", "inner"), None, None, None),
            P(),
            P(),
            P(("outer", "inner"), None),
            P(("outer", "inner"), None),
        ),
        out_specs=(
            P(("outer", "inner"), None, None, None),
            P(("outer", "inner"), None),
            P(("outer", "inner"), None),
        ),
        check_vma=False,
    )
```

profile of v0, /device:TPU:0, one launch (start us, length us, event | category | flops | bytes accessed | tf_op | source)
XLA Modules:
  0.0 401.3 jit_solution(18277517635371770999)
XLA Ops:
  11.6 5.0 %convolution_convert_fusion = bf16[1024,512]{1,0:T(8,128)(2,1)S(1)} fusion(bf16[1024,4608]{1,0:T(8,128)(2,1)S(1)} %bitcast.64, bf16[4608,512]{1,0:T(8,128)(2,1)S(1)} %bitcast.53), kind=kOutput, calls=%fused_computation.23 | convolution fusion | flops 4832362496 | bytes 15204352 | tf_op jit(solution)/shard_map/dot_general | solution.py:36
  16.6 3.7 multiply_convert_fusion.1
  20.3 2.4 select_convert_fusion.1
  23.7 7.0 %multiply_convert_fusion = bf16[512,4608]{1,0:T(8,128)(2,1)} fusion(bf16[1024,512]{1,0:T(8,128)(2,1)S(1)} %select_convert_fusion.1, bf16[1024,4608]{1,0:T(8,128)(2,1)S(1)} %bitcast.65), kind=kOutput, calls=%fused_computation | convolution fusion | flops 4836556800 | bytes 15204352 | tf_op jit(solution)/shard_map/dot_general | solution.py:52
  30.6 6.1 %reshape.118 = bf16[4,8,73728]{2,1,0:T(8,128)(2,1)} reshape(bf16[512,4608]{1,0:T(8,128)(2,1)} %multiply_convert_fusion) | data formatting | bytes 9437184 | tf_op jit(solution)/shard_map/reshape | solution.py:113
  36.7 8.1 %copy.17 = bf16[4,8,73728]{2,0,1:T(4,128)(2,1)} copy(bf16[4,8,73728]{2,1,0:T(8,128)(2,1)} %reshape.118) | data formatting | bytes 9437184 | tf_op jit(solution)/shard_map/reshape | solution.py:113
  44.8 2.9 reshape.119
  47.7 1.6 copy.18
  49.4 9.9 %pad_maximum_fusion = bf16[4,8,106496]{2,0,1:T(4,128)(2,1)} fusion(bf16[4,8,32768]{2,0,1:T(4,128)(2,1)S(1)} %copy.18, bf16[4,8,73728]{2,0,1:T(4,128)(2,1)} %copy.17), kind=kLoop, calls=%fused_computation.1 | loop fusion | flops 13631488 | bytes 13631488 | tf_op jit(solution)/shard_map/concatenate | solution.py:115
  60.5 3.4 pad_slice_fusion
  70.6 219.1 %all-reduce.9.cloned.1.call-done = bf16[4,8,106496]{2,0,1:T(4,128)(2,1)} async-done(((bf16[4,8,106496]{2,0,1:T(4,128)(2,1)}), bf16[4,8,106496]{2,0,1:T(4,128)(2,1)}) %all-reduce.9.cloned.1.call-update) | async-done | bytes 6815760
  289.7 2.2 fusion.13
  292.0 2.5 constant_dynamic-update-slice_fusion.3
  296.6 4.8 %reverse_bitcast_fusion = bf16[3,3,512,512]{2,3,1,0:T(8,128)(2,1)} fusion(bf16[3,3,512,512]{3,2,1,0:T(8,128)(2,1)} %bitcast.51), kind=kLoop, calls=%fused_computation.2 | loop fusion | bytes 9437184 | tf_op jit(solution)/shard_map/transpose | solution.py:59
  303.8 1.6 multiply_reduce_fusion.3
  305.4 4.0 stack.48
  309.4 6.8 %copy.16 = bf16[3,3,512,512]{3,2,1,0:T(8,128)(2,1)} copy(bf16[3,3,512,512]{2,3,1,0:T(8,128)(2,1)} %reverse_bitcast_fusion) | data formatting | bytes 9437184 | tf_op jit(solution)/shard_map/transpose | solution.py:59
  316.1 19.1 %psum.14 = f32[6]{0:T(128)S(1)} all-reduce(f32[6]{0:T(128)S(1)} %stack.48), channel_id=1, replica_groups=mesh['outer'=4,'inner'=8] {'inner'}, use_global_device_ids=true, to_apply=%region_7.8 | all-reduce | flops 6 | bytes 48 | tf_op jit(solution)/shard_map/psum | solution.py:127
  342.2 1.5 collective-permute-start.1
  343.8 8.8 %select_convert_fusion = bf16[1024,512]{1,0:T(8,128)(2,1)} fusion(pred[4,16,16,512]{3,2,1,0:T(8,128)(4,1)S(1)} %copy-done.13, bf16[1024,4608]{1,0:T(8,128)(2,1)} %constant_dynamic-update-slice_fusion.1, bf16[4608,512]{1,0:T(8,128)(2,1)S(1)} %bitcast.54), kind=kOutput, calls=%fused_computation.20 | convolution fusion | flops 4832886784 | bytes 15728640 | tf_op jit(solution)/shard_map/dot_general | solution.py:63
  352.6 7.2 %collective-permute-done.1 = bf16[4,106496]{1,0:T(4,128)(2,1)S(1)} collective-permute-done((bf16[4,106496]{1,0:T(4,128)(2,1)S(1)}, bf16[4,106496]{1,0:T(4,128)(2,1)S(1)}, u32[]{:S(2)}, u32[]{:S(2)}) %collective-permute-start.1) | collective-permute-done | bytes 852000 | tf_op jit(solution)/shard_map/ppermute | solution.py:17
  362.5 3.9 stack.55
  366.4 17.1 %psum.15 = f32[6]{0:T(128)S(1)} all-reduce(f32[6]{0:T(128)S(1)} %stack.55), channel_id=1, replica_groups=mesh['outer'=4,'inner'=8] {'inner'}, use_global_device_ids=true, to_apply=%region_14.15 | all-reduce | flops 6 | bytes 48 | tf_op jit(solution)/shard_map/psum | solution.py:127
  389.4 3.0 fusion.10
  (83 shorter events, 24.9 us)
Async XLA Ops:
  7.2 13.2 %copy-start = (bf16[512,2048]{1,0:T(8,128)(2,1)S(1)}, bf16[512,2048]{1,0:T(8,128)(2,1)}, u32[]{:S(2)}) copy-start(bf16[512,2048]{1,0:T(8,128)(2,1)} %param.9) | copy-start | bytes 6291460
  7.2 2.7 copy-start.2
  7.2 282.5 %all-reduce.9.cloned.1.call-start = ((), (), s32[]{:S(2)}) async-start(), calls=%async_computation | async-start | bytes 13631488
  9.1 2.3 slice-start
  10.1 1.4 slice-start.1
  11.6 5.0 %copy-start.16 = (bf16[4,16,16,2048]{3,2,1,0:T(8,128)(2,1)S(1)}, bf16[4,16,16,2048]{3,2,1,0:T(8,128)(2,1)}, u32[]{:S(2)}) copy-start(bf16[4,16,16,2048]{3,2,1,0:T(8,128)(2,1)} %param.7) | copy-start | bytes 12582916
  22.7 1.0 copy-start.6
  59.2 0.7 copy-start.17
  59.2 1.2 copy-start.7
  69.4 225.1 %copy-start.8 = (bf16[4,16,16,512]{3,2,1,0:T(8,128)(2,1)S(1)}, bf16[4,16,16,512]{3,2,1,0:T(8,128)(2,1)}, u32[]{:S(2)}) copy-start(bf16[4,16,16,512]{3,2,1,0:T(8,128)(2,1)} %get-tuple-element.25) | copy-start | bytes 3145732
  291.9 9.5 %copy-start.11 = (bf16[4,106496]{1,0:T(4,128)(2,1)}, bf16[4,106496]{1,0:T(4,128)(2,1)S(1)}, u32[]{:S(2)}) copy-start(bf16[4,106496]{1,0:T(4,128)(2,1)S(1)} %get-tuple-element.18) | copy-start | bytes 2555908
  291.9 10.6 %collective-permute-start = (bf16[4,106496]{1,0:T(4,128)(2,1)S(1)}, bf16[4,106496]{1,0:T(4,128)(2,1)S(1)}, u32[]{:S(2)}, u32[]{:S(2)}) collective-permute-start(bf16[4,106496]{1,0:T(4,128)(2,1)S(1)} %get-tuple-element.18), channel_id=1, source_target_pairs={{0,8},{8,0},{16,24},{24,16},{1,9},{9,1},{17,25},{25,17},{2,10},{10... | collective-permute-start | bytes 2555912 | tf_op jit(solution)/shard_map/ppermute | solution.py:17
  302.5 2.9 copy-start.9
  309.4 31.9 %copy-start.10 = (bf16[4,106496]{1,0:T(4,128)(2,1)S(1)}, bf16[4,106496]{1,0:T(4,128)(2,1)}, u32[]{:S(2)}) copy-start(bf16[4,106496]{1,0:T(4,128)(2,1)} %copy-done.9) | copy-start | bytes 2555908
  309.4 31.9 %copy-start.12 = (bf16[4,106496]{1,0:T(4,128)(2,1)S(1)}, bf16[4,106496]{1,0:T(4,128)(2,1)}, u32[]{:S(2)}) copy-start(bf16[4,106496]{1,0:T(4,128)(2,1)} %copy-done.11) | copy-start | bytes 2555908
  316.1 27.7 %copy-start.13 = (pred[4,16,16,512]{3,2,1,0:T(8,128)(4,1)S(1)}, pred[4,16,16,512]{3,2,1,0:T(8,128)(4,1)}, u32[]{:S(2)}) copy-start(pred[4,16,16,512]{3,2,1,0:T(8,128)(4,1)} %broadcast_compare_fusion) | copy-start | bytes 1572868
  335.2 8.6 %copy-start.5 = (bf16[3,3,512,512]{3,2,1,0:T(8,128)(2,1)S(1)}, bf16[3,3,512,512]{3,2,1,0:T(8,128)(2,1)}, u32[]{:S(2)}) copy-start(bf16[3,3,512,512]{3,2,1,0:T(8,128)(2,1)} %copy.16) | copy-start | bytes 14155780
  342.2 18.8 %copy-start.3 = (f32[4,106496]{1,0:T(4,128)}, f32[4,106496]{1,0:T(4,128)S(1)}, u32[]{:S(2)}) copy-start(f32[4,106496]{1,0:T(4,128)S(1)} %get-tuple-element.16) | copy-start | bytes 5111812
  342.2 17.6 %collective-permute-start.1 = (bf16[4,106496]{1,0:T(4,128)(2,1)S(1)}, bf16[4,106496]{1,0:T(4,128)(2,1)S(1)}, u32[]{:S(2)}, u32[]{:S(2)}) collective-permute-start(bf16[4,106496]{1,0:T(4,128)(2,1)S(1)} %get-tuple-element.15), channel_id=1, source_target_pairs={{0,16},{16,0},{8,24},{24,8},{1,17},{17,1},{9,25},{25,9},{2,18},{18... | collective-permute-start | bytes 2555912 | tf_op jit(solution)/shard_map/ppermute | solution.py:17
  352.6 39.9 %copy-start.14 = (f32[1,73728]{1,0:T(1,128)S(1)}, f32[1,73728]{1,0:T(1,128)}, u32[]{:S(2)}) copy-start(f32[1,73728]{1,0:T(1,128)} %param.10) | copy-start | bytes 884740
  359.8 34.6 %copy-start.1 = (bf16[512,2048]{1,0:T(8,128)(2,1)S(1)}, bf16[512,2048]{1,0:T(8,128)(2,1)}, u32[]{:S(2)}) copy-start(bf16[512,2048]{1,0:T(8,128)(2,1)} %param.9) | copy-start | bytes 6291460
  360.0 2.5 copy-start.4
  360.0 33.6 %copy-start.15 = (f32[1,32768]{1,0:T(1,128)S(1)}, f32[1,32768]{1,0:T(1,128)}, u32[]{:S(2)}) copy-start(f32[1,32768]{1,0:T(1,128)} %param.11) | copy-start | bytes 393220
Sparse Core Ops, SparseCore 0:
  59.4 230.2 all-reduce.8
where the time goes:
time: 402 us; the launch traced here: 401 us
  waiting for transfers between devices  226 us (56%)
  local copies, waits for them, and re-layouts  59.2 us (15%)
  blocking collectives  36.2 us (9%)
  matrix products  26.8 us (7%)
  other arithmetic  26.4 us (7%)
  between operations  24.7 us (6%)
    unnamed x2, waiting for transfers between devices  219 us
    psum x2, blocking collectives, body(): stats = lax.psum(layer_stats(holding, partner, conv_len), 'inner')  36.2 us
    unnamed x56, local copies, waits for them, and re-layouts  14.7 us
    reshape x2, local copies, waits for them, and re-layouts, body(): conv_grad.astype(jnp.float32).reshape(outer_count, inner_count, conv_len)  14.2 us
    transpose x2, local copies, waits for them, and re-layouts, local_step(): flipped = conv_weight.reshape(3, 3, channels, channels)[::-1, ::-1].trans...  11.5 us
    concatenate x1, other arithmetic, body(): joined = jnp.concatenate([conv_parts, expand_parts], axis=2)  9.87 us
    dot_general x1, matrix products, local_step(): input_back = jnp.dot(back_cols, flipped, preferred_element_type=jnp.float32)  8.81 us
  transfers between devices with their start and end apart: 3, of which 2 were waited for; matrix products, arithmetic and copies ran while one was open for 7% of the time, Pallas kernels for 0%

commit v1 on v0

v1 whole, which is shorter than its diff:
```python
import functools

import jax
import jax.numpy as jnp
from jax import lax
from jax.experimental import pallas as pl
from jax.experimental.pallas import tpu as pltpu
from jax.sharding import PartitionSpec as P

EPS = 1e-06
MOMENTUM = 0.9
LANES = 128
VMEM = 48 * 1024 * 1024


def params(**more):
    return pltpu.CompilerParams(vmem_limit_bytes=VMEM, **more)


def cost(macs, moved):
    return pl.CostEstimate(flops=2 * macs, bytes_accessed=moved, transcendentals=0)


def exchange(block, axis, bit):
    count = lax.axis_size(axis)
    return lax.ppermute(block, axis, [(i, i ^ (1 << bit)) for i in range(count)])


def my_bit(axis, bit):
    return (lax.axis_index(axis) >> bit) & 1


def fill_row_taps(source_ref, taps_ref, images, height, across, relu):
    channels = source_ref.shape[1]
    area = height * across
    for image in range(images):
        base = image * area
        block = source_ref[base : base + area, :]
        if relu:
            block = jnp.maximum(block, jnp.zeros((), block.dtype))
        blank = jnp.zeros((across, channels), block.dtype)
        taps_ref[base : base + across, 0:channels] = blank
        taps_ref[base + across : base + area, 0:channels] = block[: area - across]
        taps_ref[base : base + area, channels : 2 * channels] = block
        taps_ref[base : base + area - across, 2 * channels : 3 * channels] = block[across:]
        taps_ref[base + area - across : base + area, 2 * channels : 3 * channels] = blank


def shifted_sum(product, across):
    rows, width = product(1).shape
    place = lax.rem(lax.broadcasted_iota(jnp.int32, (rows, width), 0), across)
    total = product(1)
    total += jnp.where(place > 0, pltpu.roll(product(0), 1, 0), 0.0)
    total += jnp.where(place < across - 1, pltpu.roll(product(2), rows - 1, 0), 0.0)
    return total


def forward_kernel(images, height, across, x_ref, w_ref, out_ref, taps_ref):
    channels = x_ref.shape[1]

    @pl.when(pl.program_id(0) == 0)
    def _():
        fill_row_taps(x_ref, taps_ref, images, height, across, True)

    @functools.cache
    def product(tap_x):
        weight = jnp.concatenate(
            [w_ref[(3 * tap_y + tap_x) * channels : (3 * tap_y + tap_x + 1) * channels, :] for tap_y in range(3)],
            axis=0,
        )
        return jnp.dot(taps_ref[...], weight, preferred_element_type=jnp.float32)

    out_ref[...] = shifted_sum(product, across).astype(out_ref.dtype)


def forward(x, weight, shape):
    images, height, across, channels = shape
    rows = images * height * across
    wide = weight.shape[1]
    block = wide // 2
    return pl.pallas_call(
        functools.partial(forward_kernel, images, height, across),
        out_shape=jax.ShapeDtypeStruct((rows, wide), jnp.bfloat16),
        grid=(2,),
        in_specs=[
            pl.BlockSpec((rows, channels), lambda n: (0, 0)),
            pl.BlockSpec((9 * channels, block), lambda n: (0, n)),
        ],
        out_specs=pl.BlockSpec((rows, block), lambda n: (0, n)),
        scratch_shapes=[pltpu.VMEM((rows, 3 * channels), jnp.bfloat16)],
        compiler_params=params(),
        cost_estimate=cost(rows * 9 * channels * wide, 2 * (weight.size + 2 * rows * channels)),
        name="conv_forward",
    )(x, weight)


def backward_kernel(images, height, across, d_ref, w_ref, x_ref, out_ref, taps_ref):
    @pl.when(pl.program_id(0) == 0)
    def _():
        fill_row_taps(d_ref, taps_ref, images, height, across, False)

    @functools.cache
    def product(tap_x):
        weight = jnp.concatenate([w_ref[3 * (2 - tap_y) + 2 - tap_x] for tap_y in range(3)], axis=1)
        return lax.dot_general(
            taps_ref[...], weight, (((1,), (1,)), ((), ())), preferred_element_type=jnp.float32
        )

    total = shifted_sum(product, across)
    keep = x_ref[...].astype(jnp.float32) > 0
    out_ref[...] = jnp.where(keep, total, 0.0).astype(out_ref.dtype)


def backward(hidden_grad, weight, x, shape):
    images, height, across, channels = shape
    rows = images * height * across
    wide = weight.shape[1]
    block = channels // 2
    return pl.pallas_call(
        functools.partial(backward_kernel, images, height, across),
        out_shape=jax.ShapeDtypeStruct((rows, channels), jnp.bfloat16),
        grid=(2,),
        in_specs=[
            pl.BlockSpec((rows, wide), lambda n: (0, 0)),
            pl.BlockSpec((9, block, wide), lambda n: (0, n, 0)),
            pl.BlockSpec((rows, block), lambda n: (0, n)),
        ],
        out_specs=pl.BlockSpec((rows, block), lambda n: (0, n)),
        scratch_shapes=[pltpu.VMEM((rows, 3 * wide), jnp.bfloat16)],
        compiler_params=params(),
        cost_estimate=cost(rows * 9 * channels * wide, 2 * (weight.size + 3 * rows * channels)),
        name="conv_backward",
    )(hidden_grad, weight.reshape(9, channels, wide), x)


def kernel_grad_kernel(images, height, across, tap_y, xa_ref, xb_ref, da_ref, db_ref, out_ref, x_ref, d_ref):
    rows, channels = xa_ref.shape
    area = height * across
    for source, ref in enumerate((xa_ref, xb_ref)):
        for image in range(images):
            base = image * area
            block = ref[base : base + area, :]
            block = jnp.maximum(block, jnp.zeros((), block.dtype))
            blank = jnp.zeros((across, channels), block.dtype)
            base += source * rows
            if tap_y == 0:
                x_ref[base : base + across, :] = blank
                x_ref[base + across : base + area, :] = block[: area - across]
            elif tap_y == 1:
                x_ref[base : base + area, :] = block
            else:
                x_ref[base : base + area - across, :] = block[across:]
                x_ref[base + area - across : base + area, :] = blank
    place = lax.rem(lax.broadcasted_iota(jnp.int32, da_ref.shape, 1), across)
    for tap_x in range(3):
        for source, ref in enumerate((da_ref, db_ref)):
            block = ref[...]
            if tap_x != 1:
                wide = pltpu.roll(block.astype(jnp.float32), (tap_x - 1) % rows, 1)
                valid = place < across - 1 if tap_x == 0 else place > 0
                block = jnp.where(valid, wide, 0.0).astype(block.dtype)
            d_ref[:, source * rows : (source + 1) * rows] = block
        total = jnp.dot(d_ref[...], x_ref[...], preferred_element_type=jnp.float32)
        out_ref[:, tap_x * channels : (tap_x + 1) * channels] = (total / rows).astype(out_ref.dtype)


def kernel_grad(tap_y, x_own, x_other, d_own, d_other, shape):
    images, height, across, channels = shape
    rows = images * height * across
    half = d_own.shape[0]
    return pl.pallas_call(
        functools.partial(kernel_grad_kernel, images, height, across, tap_y),
        out_shape=jax.ShapeDtypeStruct((half, 3 * channels), jnp.bfloat16),
        scratch_shapes=[
            pltpu.VMEM((2 * rows, channels), jnp.bfloat16),
            pltpu.VMEM((half, 2 * rows), jnp.bfloat16),
        ],
        compiler_params=params(),
        cost_estimate=cost(2 * rows * 3 * channels * half, 4 * rows * (channels + half) + 6 * half * channels),
        name=f"conv_grad_rows{tap_y}",
    )(x_own, x_other, d_own, d_other)


def pairs_of(count):
    return [(a, b) for a in range(count) for b in range(a, count)]


def stat_rows(count):
    return -(-len(pairs_of(count)) // 8) * 8


def gram_kernel(offset, *refs):
    v_ref, out_ref = refs[0], refs[-1]
    count, rows, width = v_ref.shape
    if len(refs) == 3:
        out_ref[...] = refs[1][...]
    else:
        out_ref[...] = jnp.zeros(out_ref.shape, jnp.float32)
    vectors = [v_ref[o].astype(jnp.float32) for o in range(count)]
    for index, (a, b) in enumerate(pairs_of(count)):
        product = vectors[a] * vectors[b]
        folded = sum(product[:, g : g + LANES] for g in range(0, width, LANES))
        row = offset + index
        out_ref[row : row + 1, :] += jnp.sum(folded, axis=0, keepdims=True)


def gram(vectors, offset, before):
    count = vectors.shape[0]
    args = (vectors,) if before is None else (vectors, before)
    return pl.pallas_call(
        functools.partial(gram_kernel, offset),
        out_shape=jax.ShapeDtypeStruct((2 * stat_rows(count), LANES), jnp.float32),
        compiler_params=params(),
        name="gram",
    )(*args)


def adasum_coefs(table, count):
    def dot(first, second):
        total = 0.0
        for i, u in first.items():
            for j, v in second.items():
                total = total + u * v * table[min(i, j), max(i, j)]
        return total

    held = [{o: jnp.ones((1, LANES), jnp.float32)} for o in range(count)]
    while len(held) > 1:
        merged = []
        for low, high in zip(held[::2], held[1::2]):
            cross = dot(low, high)
            low_coef = 1.0 - cross / (2.0 * (jnp.maximum(dot(low, low), 0.0) + EPS))
            high_coef = 1.0 - cross / (2.0 * (jnp.maximum(dot(high, high), 0.0) + EPS))
            both = {o: low_coef * u for o, u in low.items()}
            both.update({o: high_coef * u for o, u in high.items()})
            merged.append(both)
        held = merged
    return held[0]


def finish_kernel(pieces, *refs):
    stats_ref = refs[0]
    conv_refs = refs[1 : 1 + pieces]
    expand_ref, conv_m_ref, expand_m_ref, conv_out, expand_out = refs[1 + pieces :]
    count, rows, _ = expand_ref.shape

    def apply(offset, v_refs, m_ref, out_ref):
        table = {}
        for index, pair in enumerate(pairs_of(count)):
            lane = stats_ref[offset + index : offset + index + 1, :]
            table[pair] = jnp.broadcast_to(jnp.sum(lane, axis=1, keepdims=True), (1, LANES))
        coefs = adasum_coefs(table, count)
        stride = sum(ref.shape[2] for ref in v_refs) // LANES
        group = 0
        for ref in v_refs:
            for start in range(0, ref.shape[2], LANES):
                total = sum(
                    coefs[o] * ref[o, :, start : start + LANES].astype(jnp.float32) for o in range(count)
                )
                place = pl.ds(group, rows, stride=stride)
                out_ref[place, :] = MOMENTUM * m_ref[place, :] + total
                group += 1

    apply(0, conv_refs, conv_m_ref, conv_out)
    apply(stat_rows(count), (expand_ref,), expand_m_ref, expand_out)


def finish(stats, conv_pieces, expand, conv_momentum, expand_momentum):
    conv_m = conv_momentum.reshape(-1, LANES)
    expand_m = expand_momentum.reshape(-1, LANES)
    conv_new, expand_new = pl.pallas_call(
        functools.partial(finish_kernel, len(conv_pieces)),
        out_shape=(
            jax.ShapeDtypeStruct(conv_m.shape, jnp.float32),
            jax.ShapeDtypeStruct(expand_m.shape, jnp.float32),
        ),
        compiler_params=params(),
        name="finish",
    )(stats, *conv_pieces, expand, conv_m, expand_m)
    return conv_new.reshape(conv_momentum.shape), expand_new.reshape(expand_momentum.shape)


def halve(block, dim, bit):
    mine = my_bit("inner", bit)
    send = lax.dynamic_index_in_dim(block, 1 - mine, dim, keepdims=False)
    keep = lax.dynamic_index_in_dim(block, mine, dim, keepdims=False)
    got = exchange(send, "inner", bit)
    return (keep.astype(jnp.float32) + got.astype(jnp.float32)).astype(jnp.bfloat16)


def reduce_over_inner(block, order, bits):
    left = sorted(bits, reverse=True)
    for bit in order:
        block = halve(block, 1 + left.index(bit), bit)
        left.remove(bit)
    return block


def all_to_all_outer(block):
    count = lax.axis_size("outer")
    levels = count.bit_length() - 1
    tail = block.shape[1:]
    block = block.reshape((2,) * levels + tail)
    for bit in reversed(range(levels)):
        dim = levels - 1 - bit
        mine = my_bit("outer", bit)
        send = lax.dynamic_index_in_dim(block, 1 - mine, dim, keepdims=False)
        keep = lax.dynamic_index_in_dim(block, mine, dim, keepdims=False)
        got = exchange(send, "outer", bit)
        low = jnp.where(mine == 0, keep, got)
        high = jnp.where(mine == 0, got, keep)
        block = jnp.stack([low, high], axis=dim)
    return block.reshape((count,) + tail)


def body(inputs, cotangent, conv_weight, expand_weight, conv_momentum, expand_momentum):
    shape = inputs.shape
    images, height, across, channels = shape
    rows = images * height * across
    wide = cotangent.shape[-1]
    outer_count = lax.axis_size("outer")
    inner_count = lax.axis_size("inner")
    inner_bits = inner_count.bit_length() - 1
    outer_bits = outer_count.bit_length() - 1
    hidden = conv_weight.shape[1]
    own = hidden // (outer_count * inner_count)

    x_own = inputs.reshape(rows, channels)
    x_other = exchange(x_own, "inner", 0)
    hidden_pre = forward(x_own, conv_weight, shape)
    hidden_act = jnp.maximum(hidden_pre, jnp.zeros((), hidden_pre.dtype))
    grad_rows = cotangent.reshape(rows, wide)
    expand_grad = (
        lax.dot_general(
            hidden_act, grad_rows, (((0,), (0,)), ((), ())), preferred_element_type=jnp.float32
        )
        / rows
    ).astype(jnp.bfloat16)
    hidden_back = lax.dot_general(
        grad_rows, expand_weight, (((1,), (1,)), ((), ())), preferred_element_type=jnp.float32
    )
    hidden_grad = jnp.where(hidden_pre > 0, hidden_back, 0.0).astype(jnp.bfloat16)

    twos = (2,) * inner_bits
    expand_order = list(range(1, inner_bits))
    expand_order.insert(1, 0)
    expand_own = reduce_over_inner(
        expand_grad.reshape((outer_count,) + twos + (own, wide)), expand_order, range(inner_bits)
    )

    grad_t = hidden_grad.T.reshape((outer_count * inner_count // 2, 2, own, rows))
    side = my_bit("inner", 0)
    d_own = lax.dynamic_index_in_dim(grad_t, side, 1, keepdims=False).reshape(hidden // 2, rows)
    d_send = lax.dynamic_index_in_dim(grad_t, 1 - side, 1, keepdims=False).reshape(hidden // 2, rows)
    d_other = exchange(d_send, "inner", 0)

    input_grad = backward(hidden_grad, conv_weight, x_own, shape).reshape(shape)

    conv_owns = []
    for tap_y in range(3):
        piece = kernel_grad(tap_y, x_own, x_other, d_own, d_other, shape)
        piece = piece.reshape((outer_count,) + twos[1:] + (own, 3 * channels))
        conv_owns.append(reduce_over_inner(piece, range(1, inner_bits), range(1, inner_bits)))

    expand_all = all_to_all_outer(expand_own)
    stats = gram(expand_all, stat_rows(outer_count), None)
    conv_alls = []
    for piece in conv_owns:
        conv_alls.append(all_to_all_outer(piece))
        stats = gram(conv_alls[-1], 0, stats)
    for axis, bits in (("inner", inner_bits), ("outer", outer_bits)):
        for bit in range(bits):
            stats = stats + exchange(stats, axis, bit)
    conv_new, expand_new = finish(stats, conv_alls, expand_all, conv_momentum, expand_momentum)
    return (input_grad, conv_new, expand_new)


def solution(mesh):
    split = P(("outer", "inner"))
    return jax.shard_map(
        body,
        mesh=mesh,
        in_specs=(split, split, P(), P(), split, split),
        out_specs=(split, split, split),
        check_vma=False,
    )
```

time: 402 us -> 147 us (0.37)
  waiting for transfers between devices: 226 us -> 81.4 us
  local copies, waits for them, and re-layouts: 59.2 us -> 5.18 us
  blocking collectives: 36.2 us -> 0 us
  Pallas kernels: 0 us -> 27.9 us
  between operations: 24.7 us -> 1.1 us
  other arithmetic: 26.4 us -> 2.94 us
  starting transfers between devices: 1.64 us -> 23.9 us
  matrix products: 26.8 us -> 4.75 us
    unnamed x2 -> x0, waiting for transfers between devices: 219 us -> none
    ppermute x2 -> x24, waiting for transfers between devices: 7.22 us -> 81.4 us  [exchange(): return lax.ppermute(block, axis, [(i, i ^ 1 << bit) for i in range(count)])]
    psum x2 -> x0, blocking collectives: 36.2 us -> none  [body(): stats = lax.psum(layer_stats(holding, partner, conv_len), 'inner')]
    pallas_call x0 -> x10, Pallas kernels: none -> 27.9 us  [the longest x3 10.6 us: kernel_grad(): pl.pallas_call(functools.partial(kernel_grad_kernel, images, height, acro...]
    ppermute x2 -> x24, starting transfers between devices: 1.6 us -> 23.9 us  [exchange(): return lax.ppermute(block, axis, [(i, i ^ 1 << bit) for i in range(count)])]
    dot_general x5 -> x2, matrix products: 26.8 us -> 4.75 us  [the longest x1 2.39 us: body(): lax.dot_general(hidden_act, grad_rows, (((0,), (0,)), ((), ())), preferre...]
    reshape x4 -> x0, local copies, waits for them, and re-layouts: 18.7 us -> none  [the longest x2 14.2 us: body(): conv_grad.astype(jnp.float32).reshape(outer_count, inner_count, conv_len)]
    unnamed x56 -> x12, local copies, waits for them, and re-layouts: 14.7 us -> 0.03 us
  transfers between devices with their start and end apart: 3 -> 24, of which waited for: 2 -> 14; matrix products, arithmetic and copies ran while one was open for 7% -> 6% of each run, Pallas kernels for 0% -> 13%
where the time goes in v1:
time: 147 us
  waiting for transfers between devices  81.4 us (55%)
  Pallas kernels  27.9 us (19%)
  starting transfers between devices  23.9 us (16%)
  local copies, waits for them, and re-layouts  5.18 us (4%)
  matrix products  4.75 us (3%)
  other arithmetic  2.94 us (2%)
    ppermute x24, waiting for transfers between devices, exchange(): return lax.ppermute(block, axis, [(i, i ^ 1 << bit) for i in range(count)])  81.4 us
    ppermute x24, starting transfers between devices, exchange(): return lax.ppermute(block, axis, [(i, i ^ 1 << bit) for i in range(count)])  23.9 us
    pallas_call x3, Pallas kernels, kernel_grad(): pl.pallas_call(functools.partial(kernel_grad_kernel, images, height, acro...  10.6 us
    pallas_call x1, Pallas kernels, backward(): pl.pallas_call(functools.partial(backward_kernel, images, height, across)...  8.24 us
    pallas_call x1, Pallas kernels, forward(): pl.pallas_call(functools.partial(forward_kernel, images, height, across),...  7.61 us
  transfers between devices with their start and end apart: 24, of which 14 were waited for; matrix products, arithmetic and copies ran while one was open for 6% of the time, Pallas kernels for 13%

profile of v1, /device:TPU:0, one launch (start us, length us, event | category | flops | bytes accessed | tf_op | source)
XLA Modules:
  0.0 147.1 jit_solution(1509931739589150250)
XLA Ops:
  0.7 7.6 %conv_forward.1 = bf16[1024,512]{1,0:T(8,128)(2,1)S(1)} custom-call(bf16[1024,512]{1,0:T(8,128)(2,1)} %bitcast.x_ref.xa_ref, bf16[4608,512]{1,0:T(8,128)(2,1)} %w_ref.1), custom_call_target="tpu_custom_call" | custom-call | flops 4831838208 | bytes 6815744 | tf_op jit(solution)/shard_map/conv_forward/pallas_call | solution.py:81
  8.3 2.4 %multiply_convert_fusion = bf16[512,2048]{1,0:T(8,128)(2,1)S(1)} fusion(bf16[1024,2048]{1,0:T(8,128)(2,1)S(1)} %bitcast.212, bf16[1024,512]{1,0:T(8,128)(2,1)S(1)} %conv_forward.1), kind=kOutput, calls=%fused_computation | convolution fusion | flops 2150105088 | bytes 7340032 | tf_op jit(solution)/shard_map/dot_general | solution.py:333
  11.9 3.0 %collective-permute-start.14 = (bf16[4,2,2,16,2048]{4,3,2,1,0:T(8,128)(2,1)}, bf16[4,2,2,16,2048]{4,3,2,1,0:T(8,128)(2,1)}, u32[]{:S(2)}, u32[]{:S(2)}) collective-permute-start(bf16[4,2,2,16,2048]{4,3,2,1,0:T(8,128)(2,1)} %dynamic-slice_bitcast_fusion), channel_id=1, source_target_pairs={{0,2},{1,3},{2,0},{3,1},{4,6},{5,7},{6,4},{7,5},{8,10},{9,11},{10,... | collective-permute-start | bytes 3145736 | tf_op jit(solution)/shard_map/ppermute | solution.py:26
  16.4 2.4 %select_convert_fusion.d_ref = bf16[1024,512]{1,0:T(8,128)(2,1)S(1)} fusion(bf16[1024,512]{1,0:T(8,128)(2,1)S(1)} %conv_forward.1, bf16[1024,2048]{1,0:T(8,128)(2,1)S(1)} %bitcast.213, bf16[512,2048]{1,0:T(8,128)(2,1)S(1)} %copy-done), kind=kOutput, calls=%fused_computation.3 | convolution fusion | flops 2149056512 | bytes 8388608 | tf_op jit(solution)/shard_map/dot_general | solution.py:338
  20.1 2.3 %constant_dynamic-slice_fusion = (bf16[16,1,16,1024]{3,2,1,0:T(8,128)(2,1)}, bf16[16,1,16,1024]{3,2,1,0:T(8,128)(2,1)}) fusion(bf16[16,2,16,1024]{3,2,1,0:T(8,128)(2,1)} %bitcast.200, s32[]{:T(128)S(6)} %select_n.150, s32[]{:T(128)S(6)} %select_n.149), kind=kLoop, calls=%fused_computation.95 | loop fusion | bytes 2097160 | tf_op jit(solution)/shard_map/jit(dynamic_index_in_dim)/dynamic_slice | solution.py:353
  22.9 15.4 %collective-permute-done.14 = bf16[4,2,2,16,2048]{4,3,2,1,0:T(8,128)(2,1)} collective-permute-done((bf16[4,2,2,16,2048]{4,3,2,1,0:T(8,128)(2,1)}, bf16[4,2,2,16,2048]{4,3,2,1,0:T(8,128)(2,1)}, u32[]{:S(2)}, u32[]{:S(2)}) %collective-permute-start.14) | collective-permute-done | bytes 1048608 | tf_op jit(solution)/shard_map/ppermute | solution.py:26
  38.4 1.9 %fusion = bf16[4,2,2,16,2048]{4,3,2,1,0:T(8,128)(2,1)S(1)} fusion(bf16[4,2,2,16,2048]{4,3,2,1,0:T(8,128)(2,1)} %collective-permute-done.14, bf16[4,2,2,2,16,2048]{5,4,3,2,1,0:T(8,128)(2,1)} %bitcast.202, s32[]{:T(128)S(6)} %select_n.151), kind=kLoop, calls=%fused_computation.2 | loop fusion | flops 2097152 | bytes 3145732 | tf_op jit(solution)/shard_map/convert_element_type | solution.py:287
  40.4 1.7 %collective-permute-start.15 = (bf16[4,2,16,2048]{3,2,1,0:T(8,128)(2,1)S(1)}, bf16[4,2,16,2048]{3,2,1,0:T(8,128)(2,1)S(1)}, u32[]{:S(2)}, u32[]{:S(2)}) collective-permute-start(bf16[4,2,16,2048]{3,2,1,0:T(8,128)(2,1)S(1)} %dynamic-slice_bitcast_fusion.1), channel_id=1, source_target_pairs={{0,1},{1,0},{2,3},{3,2},{4,5},{5,4},{6,7},{7,6},{8,9},{9,8},{10,11... | collective-permute-start | bytes 1572872 | tf_op jit(solution)/shard_map/ppermute | solution.py:26
  42.1 10.4 %collective-permute-done.1.db_ref = bf16[256,1024]{1,0:T(8,128)(2,1)} collective-permute-done((bf16[256,1024]{1,0:T(8,128)(2,1)}, bf16[256,1024]{1,0:T(8,128)(2,1)}, u32[]{:S(2)}, u32[]{:S(2)}) %collective-permute-start.1) | collective-permute-done | bytes 524320 | tf_op jit(solution)/shard_map/ppermute | solution.py:26
  52.6 3.5 %conv_grad_rows0.1 = bf16[256,1536]{1,0:T(8,128)(2,1)S(1)} custom-call(bf16[1024,512]{1,0:T(8,128)(2,1)} %bitcast.x_ref.xa_ref, bf16[1024,512]{1,0:T(8,128)(2,1)} %collective-permute-done.xb_ref, bf16[256,1024]{1,0:T(8,128)(2,1)S(1)} %bitcast.195, bf16[256,1024]{1,0:T(8,128)(2,1)} %collective-permute-done.1.db_ref), custom_call_target="tpu_custom_call" | custom-call | flops 1610612736 | bytes 3932160 | tf_op jit(solution)/shard_map/conv_grad_rows0/pallas_call | solution.py:171
  56.6 3.5 %conv_grad_rows1.1 = bf16[256,1536]{1,0:T(8,128)(2,1)S(1)} custom-call(bf16[1024,512]{1,0:T(8,128)(2,1)} %bitcast.x_ref.xa_ref, bf16[1024,512]{1,0:T(8,128)(2,1)} %collective-permute-done.xb_ref, bf16[256,1024]{1,0:T(8,128)(2,1)S(1)} %bitcast.196, bf16[256,1024]{1,0:T(8,128)(2,1)} %collective-permute-done.1.db_ref), custom_call_target="tpu_custom_call" | custom-call | flops 1610612736 | bytes 3932160 | tf_op jit(solution)/shard_map/conv_grad_rows1/pallas_call | solution.py:171
  61.9 3.5 %conv_grad_rows2.1 = bf16[256,1536]{1,0:T(8,128)(2,1)S(1)} custom-call(bf16[1024,512]{1,0:T(8,128)(2,1)} %bitcast.x_ref.xa_ref, bf16[1024,512]{1,0:T(8,128)(2,1)} %collective-permute-done.xb_ref, bf16[256,1024]{1,0:T(8,128)(2,1)S(1)} %bitcast.197, bf16[256,1024]{1,0:T(8,128)(2,1)} %collective-permute-done.1.db_ref), custom_call_target="tpu_custom_call" | custom-call | flops 1610612736 | bytes 3932160 | tf_op jit(solution)/shard_map/conv_grad_rows2/pallas_call | solution.py:171
  66.0 4.4 %collective-permute-done.10 = bf16[4,2,16,1536]{3,2,1,0:T(8,128)(2,1)S(1)} collective-permute-done((bf16[4,2,16,1536]{3,2,1,0:T(8,128)(2,1)S(1)}, bf16[4,2,16,1536]{3,2,1,0:T(8,128)(2,1)S(1)}, u32[]{:S(2)}, u32[]{:S(2)}) %collective-permute-start.10) | collective-permute-done | bytes 393248 | tf_op jit(solution)/shard_map/ppermute | solution.py:26
  71.1 11.9 %collective-permute-done.6 = bf16[4,2,16,1536]{3,2,1,0:T(8,128)(2,1)S(1)} collective-permute-done((bf16[4,2,16,1536]{3,2,1,0:T(8,128)(2,1)S(1)}, bf16[4,2,16,1536]{3,2,1,0:T(8,128)(2,1)S(1)}, u32[]{:S(2)}, u32[]{:S(2)}) %collective-permute-start.6) | collective-permute-done | bytes 393248 | tf_op jit(solution)/shard_map/ppermute | solution.py:26
  83.7 3.8 %collective-permute-done.2 = bf16[4,2,16,1536]{3,2,1,0:T(8,128)(2,1)S(1)} collective-permute-done((bf16[4,2,16,1536]{3,2,1,0:T(8,128)(2,1)S(1)}, bf16[4,2,16,1536]{3,2,1,0:T(8,128)(2,1)S(1)}, u32[]{:S(2)}, u32[]{:S(2)}) %collective-permute-start.2) | collective-permute-done | bytes 393248 | tf_op jit(solution)/shard_map/ppermute | solution.py:26
  89.2 1.7 %collective-permute-start.16 = (bf16[4,16,2048]{2,1,0:T(8,128)(2,1)S(1)}, bf16[4,16,2048]{2,1,0:T(8,128)(2,1)S(1)}, u32[]{:S(2)}, u32[]{:S(2)}) collective-permute-start(bf16[4,16,2048]{2,1,0:T(8,128)(2,1)S(1)} %dynamic-slice_bitcast_fusion.5), channel_id=1, source_target_pairs={{0,4},{1,5},{2,6},{3,7},{4,0},{5,1},{6,2},{7,3},{8,12},{9,13},{10,... | collective-permute-start | bytes 786440 | tf_op jit(solution)/shard_map/ppermute | solution.py:26
  92.6 13.2 %collective-permute-done.7 = bf16[4,16,1536]{2,1,0:T(8,128)(2,1)S(1)} collective-permute-done((bf16[4,16,1536]{2,1,0:T(8,128)(2,1)S(1)}, bf16[4,16,1536]{2,1,0:T(8,128)(2,1)S(1)}, u32[]{:S(2)}, u32[]{:S(2)}) %collective-permute-start.7) | collective-permute-done | bytes 196640 | tf_op jit(solution)/shard_map/ppermute | solution.py:26
  107.4 2.6 %collective-permute-done.3 = bf16[4,16,1536]{2,1,0:T(8,128)(2,1)S(1)} collective-permute-done((bf16[4,16,1536]{2,1,0:T(8,128)(2,1)S(1)}, bf16[4,16,1536]{2,1,0:T(8,128)(2,1)S(1)}, u32[]{:S(2)}, u32[]{:S(2)}) %collective-permute-start.3) | collective-permute-done | bytes 196640 | tf_op jit(solution)/shard_map/ppermute | solution.py:26
  112.4 2.4 %collective-permute-done.4 = bf16[2,16,1536]{2,1,0:T(8,128)(2,1)S(1)} collective-permute-done((bf16[2,16,1536]{2,1,0:T(8,128)(2,1)S(1)}, bf16[2,16,1536]{2,1,0:T(8,128)(2,1)S(1)}, u32[]{:S(2)}, u32[]{:S(2)}) %collective-permute-start.4) | collective-permute-done | bytes 98336 | tf_op jit(solution)/shard_map/ppermute | solution.py:26
  116.7 4.2 %collective-permute-done.17 = bf16[2,16,2048]{2,1,0:T(8,128)(2,1)S(1)} collective-permute-done((bf16[2,16,2048]{2,1,0:T(8,128)(2,1)S(1)}, bf16[2,16,2048]{2,1,0:T(8,128)(2,1)S(1)}, u32[]{:S(2)}, u32[]{:S(2)}) %collective-permute-start.17) | collective-permute-done | bytes 131104 | tf_op jit(solution)/shard_map/ppermute | solution.py:26
  124.5 2.2 %collective-permute-done.19 = f32[32,128]{1,0:T(8,128)S(1)} collective-permute-done((f32[32,128]{1,0:T(8,128)S(1)}, f32[32,128]{1,0:T(8,128)S(1)}, u32[]{:S(2)}, u32[]{:S(2)}) %collective-permute-start.19) | collective-permute-done | bytes 16416 | tf_op jit(solution)/shard_map/ppermute | solution.py:26
  126.7 3.7 %collective-permute-done.20 = f32[32,128]{1,0:T(8,128)S(1)} collective-permute-done((f32[32,128]{1,0:T(8,128)S(1)}, f32[32,128]{1,0:T(8,128)S(1)}, u32[]{:S(2)}, u32[]{:S(2)}) %collective-permute-start.20) | collective-permute-done | bytes 16416 | tf_op jit(solution)/shard_map/ppermute | solution.py:26
  130.5 4.6 %collective-permute-done.21 = f32[32,128]{1,0:T(8,128)S(1)} collective-permute-done((f32[32,128]{1,0:T(8,128)S(1)}, f32[32,128]{1,0:T(8,128)S(1)}, u32[]{:S(2)}, u32[]{:S(2)}) %collective-permute-start.21) | collective-permute-done | bytes 16416 | tf_op jit(solution)/shard_map/ppermute | solution.py:26
  137.8 8.2 %conv_backward.1 = bf16[1024,512]{1,0:T(8,128)(2,1)} custom-call(bf16[1024,512]{1,0:T(8,128)(2,1)S(1)} %select_convert_fusion.d_ref, bf16[9,512,512]{2,1,0:T(8,128)(2,1)} %bitcast.211, bf16[1024,512]{1,0:T(8,128)(2,1)} %bitcast.x_ref.xa_ref), custom_call_target="tpu_custom_call" | custom-call | flops 4831838208 | bytes 7864320 | tf_op jit(solution)/shard_map/conv_backward/pallas_call | solution.py:119
  (95 shorter events, 25.2 us)
Async XLA Ops:
  11.9 26.5 %collective-permute-start.14 = (bf16[4,2,2,16,2048]{4,3,2,1,0:T(8,128)(2,1)}, bf16[4,2,2,16,2048]{4,3,2,1,0:T(8,128)(2,1)}, u32[]{:S(2)}, u32[]{:S(2)}) collective-permute-start(bf16[4,2,2,16,2048]{4,3,2,1,0:T(8,128)(2,1)} %dynamic-slice_bitcast_fusion), channel_id=1, source_target_pairs={{0,2},{1,3},{2,0},{3,1},{4,6},{5,7},{6,4},{7,5},{8,10},{9,11},{10,... | collective-permute-start | bytes 3145736 | tf_op jit(solution)/shard_map/ppermute | solution.py:26
  14.9 37.6 %collective-permute-start = (bf16[1024,512]{1,0:T(8,128)(2,1)}, bf16[1024,512]{1,0:T(8,128)(2,1)}, u32[]{:S(2)}, u32[]{:S(2)}) collective-permute-start(bf16[1024,512]{1,0:T(8,128)(2,1)} %bitcast.x_ref.xa_ref), channel_id=1, source_target_pairs={{0,1},{1,0},{2,3},{3,2},{4,5},{5,4},{6,7},{7,6},{8,9},{9,8},{10,11... | collective-permute-start | bytes 3145736 | tf_op jit(solution)/shard_map/ppermute | solution.py:26
  22.4 30.1 %collective-permute-start.1 = (bf16[256,1024]{1,0:T(8,128)(2,1)}, bf16[256,1024]{1,0:T(8,128)(2,1)}, u32[]{:S(2)}, u32[]{:S(2)}) collective-permute-start(bf16[256,1024]{1,0:T(8,128)(2,1)} %bitcast.7), channel_id=1, source_target_pairs={{0,1},{1,0},{2,3},{3,2},{4,5},{5,4},{6,7},{7,6},{8,9},{9,8},{10,11... | collective-permute-start | bytes 1572872 | tf_op jit(solution)/shard_map/ppermute | solution.py:26
  40.4 48.6 %collective-permute-start.15 = (bf16[4,2,16,2048]{3,2,1,0:T(8,128)(2,1)S(1)}, bf16[4,2,16,2048]{3,2,1,0:T(8,128)(2,1)S(1)}, u32[]{:S(2)}, u32[]{:S(2)}) collective-permute-start(bf16[4,2,16,2048]{3,2,1,0:T(8,128)(2,1)S(1)} %dynamic-slice_bitcast_fusion.1), channel_id=1, source_target_pairs={{0,1},{1,0},{2,3},{3,2},{4,5},{5,4},{6,7},{7,6},{8,9},{9,8},{10,11... | collective-permute-start | bytes 1572872 | tf_op jit(solution)/shard_map/ppermute | solution.py:26
  56.1 14.2 %collective-permute-start.10 = (bf16[4,2,16,1536]{3,2,1,0:T(8,128)(2,1)S(1)}, bf16[4,2,16,1536]{3,2,1,0:T(8,128)(2,1)S(1)}, u32[]{:S(2)}, u32[]{:S(2)}) collective-permute-start(bf16[4,2,16,1536]{3,2,1,0:T(8,128)(2,1)S(1)} %dynamic-slice_bitcast_fusion.2), channel_id=1, source_target_pairs={{0,2},{1,3},{2,0},{3,1},{4,6},{5,7},{6,4},{7,5},{8,10},{9,11},{10,... | collective-permute-start | bytes 1179656 | tf_op jit(solution)/shard_map/ppermute | solution.py:26
  60.2 22.8 %collective-permute-start.6 = (bf16[4,2,16,1536]{3,2,1,0:T(8,128)(2,1)S(1)}, bf16[4,2,16,1536]{3,2,1,0:T(8,128)(2,1)S(1)}, u32[]{:S(2)}, u32[]{:S(2)}) collective-permute-start(bf16[4,2,16,1536]{3,2,1,0:T(8,128)(2,1)S(1)} %dynamic-slice_bitcast_fusion.3), channel_id=1, source_target_pairs={{0,2},{1,3},{2,0},{3,1},{4,6},{5,7},{6,4},{7,5},{8,10},{9,11},{10,... | collective-permute-start | bytes 1179656 | tf_op jit(solution)/shard_map/ppermute | solution.py:26
  65.4 22.1 %collective-permute-start.2 = (bf16[4,2,16,1536]{3,2,1,0:T(8,128)(2,1)S(1)}, bf16[4,2,16,1536]{3,2,1,0:T(8,128)(2,1)S(1)}, u32[]{:S(2)}, u32[]{:S(2)}) collective-permute-start(bf16[4,2,16,1536]{3,2,1,0:T(8,128)(2,1)S(1)} %dynamic-slice_bitcast_fusion.4), channel_id=1, source_target_pairs={{0,2},{1,3},{2,0},{3,1},{4,6},{5,7},{6,4},{7,5},{8,10},{9,11},{10,... | collective-permute-start | bytes 1179656 | tf_op jit(solution)/shard_map/ppermute | solution.py:26
  70.5 20.4 %collective-permute-start.11 = (bf16[4,16,1536]{2,1,0:T(8,128)(2,1)S(1)}, bf16[4,16,1536]{2,1,0:T(8,128)(2,1)S(1)}, u32[]{:S(2)}, u32[]{:S(2)}) collective-permute-start(bf16[4,16,1536]{2,1,0:T(8,128)(2,1)S(1)} %dynamic-slice_bitcast_fusion.6), channel_id=1, source_target_pairs={{0,4},{1,5},{2,6},{3,7},{4,0},{5,1},{6,2},{7,3},{8,12},{9,13},{10,... | collective-permute-start | bytes 589832 | tf_op jit(solution)/shard_map/ppermute | solution.py:26
  83.1 22.6 %collective-permute-start.7 = (bf16[4,16,1536]{2,1,0:T(8,128)(2,1)S(1)}, bf16[4,16,1536]{2,1,0:T(8,128)(2,1)S(1)}, u32[]{:S(2)}, u32[]{:S(2)}) collective-permute-start(bf16[4,16,1536]{2,1,0:T(8,128)(2,1)S(1)} %dynamic-slice_bitcast_fusion.7), channel_id=1, source_target_pairs={{0,4},{1,5},{2,6},{3,7},{4,0},{5,1},{6,2},{7,3},{8,12},{9,13},{10,... | collective-permute-start | bytes 589832 | tf_op jit(solution)/shard_map/ppermute | solution.py:26
  87.7 22.3 %collective-permute-start.3 = (bf16[4,16,1536]{2,1,0:T(8,128)(2,1)S(1)}, bf16[4,16,1536]{2,1,0:T(8,128)(2,1)S(1)}, u32[]{:S(2)}, u32[]{:S(2)}) collective-permute-start(bf16[4,16,1536]{2,1,0:T(8,128)(2,1)S(1)} %dynamic-slice_bitcast_fusion.8), channel_id=1, source_target_pairs={{0,4},{1,5},{2,6},{3,7},{4,0},{5,1},{6,2},{7,3},{8,12},{9,13},{10,... | collective-permute-start | bytes 589832 | tf_op jit(solution)/shard_map/ppermute | solution.py:26
  89.2 25.7 %collective-permute-start.16 = (bf16[4,16,2048]{2,1,0:T(8,128)(2,1)S(1)}, bf16[4,16,2048]{2,1,0:T(8,128)(2,1)S(1)}, u32[]{:S(2)}, u32[]{:S(2)}) collective-permute-start(bf16[4,16,2048]{2,1,0:T(8,128)(2,1)S(1)} %dynamic-slice_bitcast_fusion.5), channel_id=1, source_target_pairs={{0,4},{1,5},{2,6},{3,7},{4,0},{5,1},{6,2},{7,3},{8,12},{9,13},{10,... | collective-permute-start | bytes 786440 | tf_op jit(solution)/shard_map/ppermute | solution.py:26
  91.0 20.6 %collective-permute-start.12 = (bf16[2,16,1536]{2,1,0:T(8,128)(2,1)S(1)}, bf16[2,16,1536]{2,1,0:T(8,128)(2,1)S(1)}, u32[]{:S(2)}, u32[]{:S(2)}) collective-permute-start(bf16[2,16,1536]{2,1,0:T(8,128)(2,1)S(1)} %dynamic-slice_bitcast_fusion.10), channel_id=1, source_target_pairs={{0,16},{8,24},{16,0},{24,8},{1,17},{9,25},{17,1},{25,9},{2,18},{10... | collective-permute-start | bytes 294920 | tf_op jit(solution)/shard_map/ppermute | solution.py:26
  105.8 5.9 %collective-permute-start.8 = (bf16[2,16,1536]{2,1,0:T(8,128)(2,1)S(1)}, bf16[2,16,1536]{2,1,0:T(8,128)(2,1)S(1)}, u32[]{:S(2)}, u32[]{:S(2)}) collective-permute-start(bf16[2,16,1536]{2,1,0:T(8,128)(2,1)S(1)} %dynamic-slice_bitcast_fusion.11), channel_id=1, source_target_pairs={{0,16},{8,24},{16,0},{24,8},{1,17},{9,25},{17,1},{25,9},{2,18},{10... | collective-permute-start | bytes 294920 | tf_op jit(solution)/shard_map/ppermute | solution.py:26
  110.0 4.7 %collective-permute-start.4 = (bf16[2,16,1536]{2,1,0:T(8,128)(2,1)S(1)}, bf16[2,16,1536]{2,1,0:T(8,128)(2,1)S(1)}, u32[]{:S(2)}, u32[]{:S(2)}) collective-permute-start(bf16[2,16,1536]{2,1,0:T(8,128)(2,1)S(1)} %dynamic-slice_bitcast_fusion.12), channel_id=1, source_target_pairs={{0,16},{8,24},{16,0},{24,8},{1,17},{9,25},{17,1},{25,9},{2,18},{10... | collective-permute-start | bytes 294920 | tf_op jit(solution)/shard_map/ppermute | solution.py:26
  111.7 4.9 %collective-permute-start.13 = (bf16[2,16,1536]{2,1,0:T(8,128)(2,1)S(1)}, bf16[2,16,1536]{2,1,0:T(8,128)(2,1)S(1)}, u32[]{:S(2)}, u32[]{:S(2)}) collective-permute-start(bf16[2,16,1536]{2,1,0:T(8,128)(2,1)S(1)} %fusion.18), channel_id=1, source_target_pairs={{0,8},{8,0},{16,24},{24,16},{1,9},{9,1},{17,25},{25,17},{2,10},{10... | collective-permute-start | bytes 294920 | tf_op jit(solution)/shard_map/ppermute | solution.py:26
  111.8 4.8 %collective-permute-start.9 = (bf16[2,16,1536]{2,1,0:T(8,128)(2,1)S(1)}, bf16[2,16,1536]{2,1,0:T(8,128)(2,1)S(1)}, u32[]{:S(2)}, u32[]{:S(2)}) collective-permute-start(bf16[2,16,1536]{2,1,0:T(8,128)(2,1)S(1)} %fusion.22), channel_id=1, source_target_pairs={{0,8},{8,0},{16,24},{24,16},{1,9},{9,1},{17,25},{25,17},{2,10},{10... | collective-permute-start | bytes 294920 | tf_op jit(solution)/shard_map/ppermute | solution.py:26
  114.8 1.9 %collective-permute-start.5 = (bf16[2,16,1536]{2,1,0:T(8,128)(2,1)S(1)}, bf16[2,16,1536]{2,1,0:T(8,128)(2,1)S(1)}, u32[]{:S(2)}, u32[]{:S(2)}) collective-permute-start(bf16[2,16,1536]{2,1,0:T(8,128)(2,1)S(1)} %fusion.26), channel_id=1, source_target_pairs={{0,8},{8,0},{16,24},{24,16},{1,9},{9,1},{17,25},{25,17},{2,10},{10... | collective-permute-start | bytes 294920 | tf_op jit(solution)/shard_map/ppermute | solution.py:26
  115.0 6.0 %collective-permute-start.17 = (bf16[2,16,2048]{2,1,0:T(8,128)(2,1)S(1)}, bf16[2,16,2048]{2,1,0:T(8,128)(2,1)S(1)}, u32[]{:S(2)}, u32[]{:S(2)}) collective-permute-start(bf16[2,16,2048]{2,1,0:T(8,128)(2,1)S(1)} %dynamic-slice_bitcast_fusion.9), channel_id=1, source_target_pairs={{0,16},{8,24},{16,0},{24,8},{1,17},{9,25},{17,1},{25,9},{2,18},{10... | collective-permute-start | bytes 393224 | tf_op jit(solution)/shard_map/ppermute | solution.py:26
  121.0 1.4 collective-permute-start.18
  122.9 3.8 %collective-permute-start.19 = (f32[32,128]{1,0:T(8,128)S(1)}, f32[32,128]{1,0:T(8,128)S(1)}, u32[]{:S(2)}, u32[]{:S(2)}) collective-permute-start(f32[32,128]{1,0:T(8,128)S(1)} %gram.7), channel_id=1, source_target_pairs={{0,1},{1,0},{2,3},{3,2},{4,5},{5,4},{6,7},{7,6},{8,9},{9,8},{10,11... | collective-permute-start | bytes 49160 | tf_op jit(solution)/shard_map/ppermute | solution.py:26
  126.7 3.7 %collective-permute-start.20 = (f32[32,128]{1,0:T(8,128)S(1)}, f32[32,128]{1,0:T(8,128)S(1)}, u32[]{:S(2)}, u32[]{:S(2)}) collective-permute-start(f32[32,128]{1,0:T(8,128)S(1)} %add.132), channel_id=1, source_target_pairs={{0,2},{1,3},{2,0},{3,1},{4,6},{5,7},{6,4},{7,5},{8,10},{9,11},{10,... | collective-permute-start | bytes 49160 | tf_op jit(solution)/shard_map/ppermute | solution.py:26
  130.5 4.6 %collective-permute-start.21 = (f32[32,128]{1,0:T(8,128)S(1)}, f32[32,128]{1,0:T(8,128)S(1)}, u32[]{:S(2)}, u32[]{:S(2)}) collective-permute-start(f32[32,128]{1,0:T(8,128)S(1)} %add.133), channel_id=1, source_target_pairs={{0,4},{1,5},{2,6},{3,7},{4,0},{5,1},{6,2},{7,3},{8,12},{9,13},{10,... | collective-permute-start | bytes 49160 | tf_op jit(solution)/shard_map/ppermute | solution.py:26
  135.1 1.2 collective-permute-start.22
  136.3 9.7 %collective-permute-start.23 = (f32[32,128]{1,0:T(8,128)S(1)}, f32[32,128]{1,0:T(8,128)S(1)}, u32[]{:S(2)}, u32[]{:S(2)}) collective-permute-start(f32[32,128]{1,0:T(8,128)S(1)} %add.135), channel_id=1, source_target_pairs={{0,16},{8,24},{16,0},{24,8},{1,17},{9,25},{17,1},{25,9},{2,18},{10... | collective-permute-start | bytes 49160 | tf_op jit(solution)/shard_map/ppermute | solution.py:26
  (6 other events, 73.8 us)

commit v2 on v1

v2 whole, which is shorter than its diff:
```python
import functools

import jax
import jax.numpy as jnp
from jax import lax
from jax.experimental import pallas as pl
from jax.experimental.pallas import tpu as pltpu
from jax.sharding import PartitionSpec as P

EPS = 1e-06
MOMENTUM = 0.9
LANES = 128
VMEM = 48 * 1024 * 1024


def params(**more):
    return pltpu.CompilerParams(vmem_limit_bytes=VMEM, **more)


def call(kernel, name, out_shape, args, after=(), scratch=(), in_specs=None):
    count = len(args)

    def run(*refs):
        kernel(*refs[:count], *refs[count + len(after) :])

    if in_specs is None:
        in_specs = [pl.BlockSpec(memory_space=pltpu.VMEM)] * count
    return pl.pallas_call(
        run,
        out_shape=out_shape,
        in_specs=list(in_specs) + [pl.BlockSpec(memory_space=pl.ANY)] * len(after),
        scratch_shapes=list(scratch),
        compiler_params=params(),
        cost_estimate=pl.CostEstimate(flops=1, bytes_accessed=1, transcendentals=0),
        name=name,
    )(*args, *after)


def half(shape):
    return jax.ShapeDtypeStruct(shape, jnp.bfloat16)


def exchange(block, axis, bit):
    count = lax.axis_size(axis)
    return lax.ppermute(block, axis, [(i, i ^ (1 << bit)) for i in range(count)])


def my_bit(axis, bit):
    return (lax.axis_index(axis) >> bit) & 1


def fill_row_taps(source_ref, taps_ref, images, height, across, relu):
    channels = source_ref.shape[1]
    area = height * across
    for image in range(images):
        base = image * area
        block = source_ref[base : base + area, :]
        if relu:
            block = jnp.maximum(block, jnp.zeros((), block.dtype))
        blank = jnp.zeros((across, channels), block.dtype)
        taps_ref[base : base + across, 0:channels] = blank
        taps_ref[base + across : base + area, 0:channels] = block[: area - across]
        taps_ref[base : base + area, channels : 2 * channels] = block
        taps_ref[base : base + area - across, 2 * channels : 3 * channels] = block[across:]
        taps_ref[base + area - across : base + area, 2 * channels : 3 * channels] = blank


def shifted_sum(product, across):
    rows, width = product(1).shape
    place = lax.rem(lax.broadcasted_iota(jnp.int32, (rows, width), 0), across)
    total = product(1)
    total += jnp.where(place > 0, pltpu.roll(product(0), 1, 0), 0.0)
    total += jnp.where(place < across - 1, pltpu.roll(product(2), rows - 1, 0), 0.0)
    return total


def store_split(value, bit, step, send_ref, keep_ref, first, columns):
    mine = my_bit("inner", bit)
    for pair in range(value.shape[0] // (2 * step)):
        zero = value[2 * pair * step : (2 * pair + 1) * step]
        one = value[(2 * pair + 1) * step : (2 * pair + 2) * step]
        place = slice(first + pair * step, first + (pair + 1) * step)
        keep_ref[place, columns] = jnp.where(mine == 0, zero, one).astype(keep_ref.dtype)
        send_ref[place, columns] = jnp.where(mine == 0, one, zero).astype(send_ref.dtype)


def split_rows(block, bit, step):
    mine = my_bit("inner", bit)
    parts = block.reshape(block.shape[0] // (2 * step), 2, step, block.shape[1])
    send = lax.dynamic_index_in_dim(parts, 1 - mine, 1, keepdims=False)
    keep = lax.dynamic_index_in_dim(parts, mine, 1, keepdims=False)
    return [part.reshape(block.shape[0] // 2, block.shape[1]) for part in (send, keep)]


def fused_split(own):
    return own % 16 == 0


def front_kernel(index, bit, own, shape, x_hbm, w_hbm, cot_hbm, *refs):
    images, height, across, channels = shape
    hid_ref, *out_refs = refs[:-5]
    x_ref, w_ref, cot_ref, taps_ref, sems = refs[-5:]
    rows, block = hid_ref.shape
    x_copy = pltpu.make_async_copy(x_hbm, x_ref, sems.at[0])
    cot_copy = pltpu.make_async_copy(cot_hbm, cot_ref, sems.at[1])
    w_copies = {}
    for tap_x in (1, 0, 2):
        for tap_y in range(3):
            tap = 3 * tap_y + tap_x
            w_copies[tap] = pltpu.make_async_copy(
                w_hbm.at[pl.ds(tap * channels, channels), pl.ds(index * block, block)],
                w_ref.at[pl.ds(tap * channels, channels), :],
                sems.at[2 + tap],
            )
    x_copy.start()
    for copy in w_copies.values():
        copy.start()
    cot_copy.start()
    x_copy.wait()
    fill_row_taps(x_ref, taps_ref, images, height, across, True)

    @functools.cache
    def product(tap_x):
        for tap_y in range(3):
            w_copies[3 * tap_y + tap_x].wait()
        weight = jnp.concatenate(
            [w_ref[(3 * tap_y + tap_x) * channels : (3 * tap_y + tap_x + 1) * channels, :] for tap_y in range(3)],
            axis=0,
        )
        return jnp.dot(taps_ref[...], weight, preferred_element_type=jnp.float32)

    hidden = shifted_sum(product, across).astype(hid_ref.dtype)
    hid_ref[...] = hidden
    act = jnp.maximum(hidden, jnp.zeros((), hidden.dtype))
    cot_copy.wait()
    wide = cot_ref.shape[1]
    piece = min(wide, 512)
    for start in range(0, wide, piece):
        columns = slice(start, start + piece)
        grad = lax.dot_general(
            act, cot_ref[:, columns], (((0,), (0,)), ((), ())), preferred_element_type=jnp.float32
        )
        grad = grad / rows
        if len(out_refs) == 2:
            store_split(grad, bit, own << bit, *out_refs, 0, columns)
        else:
            out_refs[0][:, columns] = grad.astype(jnp.bfloat16)


def front(index, x, weight, cot, shape, bit, own):
    rows, channels = x.shape
    wide = cot.shape[1]
    block = weight.shape[1] // 2
    parts = 2 if fused_split(own) else 1
    hidden, *grads = call(
        functools.partial(front_kernel, index, bit, own, shape),
        f"forward_expand{index}",
        [half((rows, block))] + [half((block // parts, wide))] * parts,
        (x, weight, cot),
        in_specs=[pl.BlockSpec(memory_space=pl.ANY)] * 3,
        scratch=[
            pltpu.VMEM((rows, channels), jnp.bfloat16),
            pltpu.VMEM((9 * channels, block), jnp.bfloat16),
            pltpu.VMEM((rows, wide), jnp.bfloat16),
            pltpu.VMEM((rows, 3 * channels), jnp.bfloat16),
            pltpu.SemaphoreType.DMA((11,)),
        ],
    )
    if parts == 1:
        grads = split_rows(grads[0], bit, own << bit)
    return hidden, *grads


def hidden_grad_kernel(own, *refs):
    blocks = refs[:2]
    cot_ref, w_ref, out_ref, *t_refs = refs[2:]
    wide = blocks[0].shape[1]
    for index, hid_ref in enumerate(blocks):
        place = slice(index * wide, (index + 1) * wide)
        back = lax.dot_general(
            cot_ref[...], w_ref[place, :], (((1,), (1,)), ((), ())), preferred_element_type=jnp.float32
        )
        grad = jnp.where(hid_ref[...].astype(jnp.float32) > 0, back, 0.0)
        out_ref[:, place] = grad.astype(out_ref.dtype)
        turned = grad.T
        if len(t_refs) == 2:
            store_split(turned, 0, own, *t_refs, index * wide // 2, slice(None))
        else:
            t_refs[0][place, :] = turned.astype(jnp.bfloat16)


def hidden_gradient(hidden, cot, weight, own, after):
    rows, block = hidden[0].shape
    wide = 2 * block
    parts = 2 if fused_split(own) else 1
    grad, *turned = call(
        functools.partial(hidden_grad_kernel, own),
        "hidden_grad",
        [half((rows, wide))] + [half((wide // parts, rows))] * parts,
        (*hidden, cot, weight),
        after,
    )
    if parts == 1:
        turned = split_rows(turned[0], 0, own)
    return grad, *turned


def backward_kernel(shape, d_ref, w_ref, x_ref, out_ref, taps_ref):
    images, height, across, channels = shape
    fill_row_taps(d_ref, taps_ref, images, height, across, False)
    block = channels // 2
    for start in range(0, channels, block):
        columns = slice(start, start + block)

        @functools.cache
        def product(tap_x):
            weight = jnp.concatenate(
                [w_ref[3 * (2 - tap_y) + 2 - tap_x, columns, :] for tap_y in range(3)], axis=1
            )
            return lax.dot_general(
                taps_ref[...], weight, (((1,), (1,)), ((), ())), preferred_element_type=jnp.float32
            )

        total = shifted_sum(product, across)
        keep = x_ref[:, columns].astype(jnp.float32) > 0
        out_ref[:, columns] = jnp.where(keep, total, 0.0).astype(out_ref.dtype)


def backward(hidden_grad, weight, x, shape):
    rows, channels = x.shape
    wide = weight.shape[1]
    return call(
        functools.partial(backward_kernel, shape),
        "conv_backward",
        half((rows, channels)),
        (hidden_grad, weight.reshape(9, channels, wide), x),
        scratch=[pltpu.VMEM((rows, 3 * wide), jnp.bfloat16)],
    )


def kernel_grad_kernel(tap_y, bit, step, shape, x_count, *refs):
    images, height, across, channels = shape
    area = height * across
    x_refs = refs[:x_count]
    d_refs = refs[x_count : x_count + 2]
    out_refs = refs[x_count + 2 : -2]
    x_ref, d_ref = refs[-2:]
    rows = d_refs[0].shape[1]
    first = 0
    for ref in x_refs:
        for image in range(ref.shape[0] // area):
            block = ref[image * area : (image + 1) * area, :]
            block = jnp.maximum(block, jnp.zeros((), block.dtype))
            blank = jnp.zeros((across, channels), block.dtype)
            if tap_y == 0:
                x_ref[first : first + across, :] = blank
                x_ref[first + across : first + area, :] = block[: area - across]
            elif tap_y == 1:
                x_ref[first : first + area, :] = block
            else:
                x_ref[first : first + area - across, :] = block[across:]
                x_ref[first + area - across : first + area, :] = blank
            first += area
    place = lax.rem(lax.broadcasted_iota(jnp.int32, d_refs[0].shape, 1), across)
    for tap_x in range(3):
        for source, ref in enumerate(d_refs):
            block = ref[...]
            if tap_x != 1:
                wide = pltpu.roll(block.astype(jnp.float32), (tap_x - 1) % rows, 1)
                valid = place < across - 1 if tap_x == 0 else place > 0
                block = jnp.where(valid, wide, 0.0).astype(block.dtype)
            d_ref[:, source * rows : (source + 1) * rows] = block
        total = jnp.dot(d_ref[...], x_ref[...], preferred_element_type=jnp.float32) / rows
        columns = slice(tap_x * channels, (tap_x + 1) * channels)
        if len(out_refs) == 2:
            store_split(total, bit, step, *out_refs, 0, columns)
        else:
            out_refs[0][:, columns] = total.astype(jnp.bfloat16)


def kernel_grad(tap_y, xs, ds, shape, bit, own, after):
    channels = shape[3]
    wide, rows = ds[0].shape
    parts = 2 if fused_split(own) else 1
    grads = call(
        functools.partial(kernel_grad_kernel, tap_y, bit, own << (bit - 1), shape, len(xs)),
        f"conv_grad_rows{tap_y}",
        [half((wide // parts, 3 * channels))] * parts,
        (*xs, *ds),
        after,
        scratch=[
            pltpu.VMEM((2 * rows, channels), jnp.bfloat16),
            pltpu.VMEM((wide, 2 * rows), jnp.bfloat16),
        ],
    )
    if parts == 1:
        grads = split_rows(grads[0], bit, own << (bit - 1))
    return grads


def merge_kernel(axis, bit, *refs):
    count = (len(refs) - 2) // 2
    send_ref, keep_ref = refs[-2:]
    mine = my_bit(axis, bit)
    first = 0
    for index in range(count):
        kept, got = refs[2 * index : 2 * index + 2]
        last = first + kept.shape[0]
        for out_ref, side in ((keep_ref, mine), (send_ref, 1 - mine)):
            total = kept[:, side].astype(jnp.float32) + got[:, side].astype(jnp.float32)
            out_ref[first:last] = total.astype(out_ref.dtype)
        first = last


def merge(parts, leading, axis, bit, after=(), name="merge"):
    flat = []
    for kept, got, lead in zip(*zip(*parts), leading):
        for block in (kept, got):
            flat.append(block.reshape((lead, 2, -1) + block.shape[-2:]))
    lead, _, middle, own, wide = flat[0].shape
    out = half((sum(leading), middle, own, wide))
    return call(functools.partial(merge_kernel, axis, bit), name, [out] * 2, flat, after)


def spread_kernel(bit, kept, got, send_ref, keep_ref):
    mine = my_bit("outer", bit)
    sources = kept.shape[0]
    for index, ref in enumerate((kept, got)):
        place = slice(index * sources, (index + 1) * sources)
        keep_ref[place] = ref[:, mine]
        send_ref[place] = ref[:, 1 - mine]


def spread(kept, got, bit, after=()):
    sources, left, own, wide = kept.shape
    out = half((2 * sources, left // 2, own, wide))
    args = [block.reshape(sources, 2, left // 2, own, wide) for block in (kept, got)]
    return call(functools.partial(spread_kernel, bit), "spread", [out] * 2, args, after)


def gram_kernel(offset, *refs):
    kept, got = refs[:2]
    v_ref, out_ref = refs[-2:]
    sources, rows, width = kept.shape
    count = 2 * sources
    levels = count.bit_length() - 1
    vectors = [None] * count
    for index in range(count):
        flips = sum(((index >> k) & 1) << (levels - 1 - k) for k in range(levels))
        vectors[flips] = (kept if index < sources else got)[index % sources].astype(jnp.float32)
    for bit in range(levels):
        mine = my_bit("outer", bit)
        for low in range(count):
            high = low | 1 << bit
            if high != low:
                a, b = vectors[low], vectors[high]
                vectors[low] = jnp.where(mine == 0, a, b)
                vectors[high] = jnp.where(mine == 0, b, a)
    for index, vector in enumerate(vectors):
        v_ref[index] = vector.astype(v_ref.dtype)
    if len(refs) == 5:
        out_ref[...] = refs[2][...]
    else:
        out_ref[...] = jnp.zeros(out_ref.shape, jnp.float32)
    for index, (a, b) in enumerate(pairs_of(count)):
        product = vectors[a] * vectors[b]
        folded = sum(product[:, g : g + LANES] for g in range(0, width, LANES))
        row = offset + index
        out_ref[row : row + 1, :] += jnp.sum(folded, axis=0, keepdims=True)


def gram(kept, got, offset, before, after=()):
    sources, _, own, wide = kept.shape
    args = [block.reshape(sources, own, wide) for block in (kept, got)]
    if before is not None:
        args.append(before)
    return call(
        functools.partial(gram_kernel, offset),
        "gram",
        [half((2 * sources, own, wide)), jax.ShapeDtypeStruct((2 * stat_rows(2 * sources), LANES), jnp.float32)],
        args,
        after,
    )


def pairs_of(count):
    return [(a, b) for a in range(count) for b in range(a, count)]


def stat_rows(count):
    return -(-len(pairs_of(count)) // 8) * 8


def adasum_coefs(table, count):
    def dot(first, second):
        total = 0.0
        for i, u in first.items():
            for j, v in second.items():
                total = total + u * v * table[min(i, j), max(i, j)]
        return total

    held = [{o: jnp.ones((1, LANES), jnp.float32)} for o in range(count)]
    while len(held) > 1:
        merged = []
        for low, high in zip(held[::2], held[1::2]):
            cross = dot(low, high)
            low_coef = 1.0 - cross / (2.0 * (jnp.maximum(dot(low, low), 0.0) + EPS))
            high_coef = 1.0 - cross / (2.0 * (jnp.maximum(dot(high, high), 0.0) + EPS))
            both = {o: low_coef * u for o, u in low.items()}
            both.update({o: high_coef * u for o, u in high.items()})
            merged.append(both)
        held = merged
    return held[0]


def finish_kernel(pieces, *refs):
    stats_ref = refs[0]
    conv_refs = refs[1 : 1 + pieces]
    expand_ref, conv_m_ref, expand_m_ref, conv_out, expand_out = refs[1 + pieces :]
    count, rows, _ = expand_ref.shape

    def apply(offset, v_refs, m_ref, out_ref):
        table = {}
        for index, pair in enumerate(pairs_of(count)):
            lane = stats_ref[offset + index : offset + index + 1, :]
            table[pair] = jnp.broadcast_to(jnp.sum(lane, axis=1, keepdims=True), (1, LANES))
        coefs = adasum_coefs(table, count)
        stride = sum(ref.shape[2] for ref in v_refs) // LANES
        group = 0
        for ref in v_refs:
            for start in range(0, ref.shape[2], LANES):
                total = sum(
                    coefs[o] * ref[o, :, start : start + LANES].astype(jnp.float32) for o in range(count)
                )
                place = pl.ds(group, rows, stride=stride)
                out_ref[place, :] = MOMENTUM * m_ref[place, :] + total
                group += 1

    apply(0, conv_refs, conv_m_ref, conv_out)
    apply(stat_rows(count), (expand_ref,), expand_m_ref, expand_out)


def finish(stats, conv_pieces, expand, conv_momentum, expand_momentum):
    conv_m = conv_momentum.reshape(-1, LANES)
    expand_m = expand_momentum.reshape(-1, LANES)
    conv_new, expand_new = pl.pallas_call(
        functools.partial(finish_kernel, len(conv_pieces)),
        out_shape=(
            jax.ShapeDtypeStruct(conv_m.shape, jnp.float32),
            jax.ShapeDtypeStruct(expand_m.shape, jnp.float32),
        ),
        compiler_params=params(),
        name="finish",
    )(stats, *conv_pieces, expand, conv_m, expand_m)
    return conv_new.reshape(conv_momentum.shape), expand_new.reshape(expand_momentum.shape)


def body(inputs, cotangent, conv_weight, expand_weight, conv_momentum, expand_momentum):
    shape = inputs.shape
    images, height, across, channels = shape
    rows = images * height * across
    wide = cotangent.shape[-1]
    outer_count = lax.axis_size("outer")
    inner_count = lax.axis_size("inner")
    inner_bits = inner_count.bit_length() - 1
    outer_bits = outer_count.bit_length() - 1
    own = conv_weight.shape[1] // (outer_count * inner_count)
    top = outer_bits - 1

    x_own = inputs.reshape(rows, channels)
    cut = images // 2 * height * across
    x_first = exchange(x_own[:cut], "inner", 0)
    x_second = exchange(x_own[cut:], "inner", 0)
    cot = cotangent.reshape(rows, wide)

    hidden, expand = [], []
    for index in range(2):
        block, send, keep = front(index, x_own, conv_weight, cot, shape, 1, own)
        hidden.append(block)
        expand.append((keep, exchange(send, "inner", 1)))
    hidden_grad, d_send, d_own = hidden_gradient(hidden, cot, expand_weight, own, (x_first,))
    d_other = exchange(d_send, "inner", 0)
    input_grad = backward(hidden_grad, conv_weight, x_own, shape).reshape(shape)

    parts = expand
    halves = outer_count // 2
    for bit in range(2, inner_bits):
        lead = halves << (inner_bits - 1 - bit)
        merged = []
        for kept, got in parts:
            shaped = [b.reshape(-1, 2, own, wide) for b in (kept, got)]
            send, keep = merge([shaped], [lead], "inner", bit, name="merge_expand_z")
            merged.append((keep, exchange(send, "inner", bit)))
        parts = merged
    early = [keep for keep, _ in parts]

    def to_owner(send, keep, after):
        got = exchange(send, "outer", top)
        for bit in reversed(range(top)):
            send, keep = spread(keep, got, bit, after)
            got = exchange(send, "outer", bit)
        return keep, got

    conv = []
    for tap_y in range(3):
        after = tuple(early) + (input_grad,) if tap_y == 0 else ()
        send, keep = kernel_grad(tap_y, (x_own, x_first, x_second), (d_own, d_other), shape, 1, own, after)
        conv.append((keep, exchange(send, "inner", 1)))

    shaped = [[b.reshape(-1, own, wide) for b in pair] for pair in parts]
    send, keep = merge(shaped, [halves] * 2, "inner", 0, name="merge_expand_y")
    expand_y = (keep, exchange(send, "inner", 0))

    stats = None
    ready = []
    expand_all = None
    for tap_y, (keep, got) in enumerate(conv):
        for bit in range(2, inner_bits):
            lead = outer_count << (inner_bits - 1 - bit)
            shaped = [b.reshape(-1, own, 3 * channels) for b in (keep, got)]
            after = (expand_y[0],) if tap_y == 0 else ()
            send, keep = merge([shaped], [lead], "inner", bit, after, name="merge_conv_z")
            got = exchange(send, "inner", bit)
        ready.append((keep, got))

    shaped = [b.reshape(-1, own, wide) for b in expand_y]
    send, keep = merge([shaped], [1], "outer", top, name="merge_expand_x")
    kept, got = to_owner(send, keep, ())
    expand_all, stats = gram(kept, got, stat_rows(outer_count), None)

    conv_all = []
    for tap_y, (keep, got) in enumerate(ready):
        shaped = [b.reshape(-1, own, 3 * channels) for b in (keep, got)]
        after = (stats,)
        send, keep = merge([shaped], [1], "outer", top, after, name="merge_conv_x")
        kept, got = to_owner(send, keep, ())
        vectors, stats = gram(kept, got, 0, stats)
        conv_all.append(vectors)

    for axis, bits in (("inner", inner_bits), ("outer", outer_bits)):
        for bit in range(bits):
            stats = stats + exchange(stats, axis, bit)
    conv_new, expand_new = finish(stats, conv_all, expand_all, conv_momentum, expand_momentum)
    return (input_grad, conv_new, expand_new)


def solution(mesh):
    split = P(("outer", "inner"))
    return jax.shard_map(
        body,
        mesh=mesh,
        in_specs=(split, split, P(), P(), split, split),
        out_specs=(split, split, split),
        check_vma=False,
    )
```

time: 147 us -> 128 us (0.87)
  waiting for transfers between devices: 81.4 us -> 58.9 us
  Pallas kernels: 27.9 us -> 36.3 us
  matrix products: 4.75 us -> 0 us
  starting transfers between devices: 23.9 us -> 27.6 us
  other arithmetic: 2.94 us -> 0.02 us
    ppermute x24 -> x27, waiting for transfers between devices: 81.4 us -> 58.9 us  [exchange(): return lax.ppermute(block, axis, [(i, i ^ 1 << bit) for i in range(count)])]
    pallas_call x9 -> x25, Pallas kernels: 26.9 us -> 35.3 us  [call(): pl.pallas_call(run, out_shape=out_shape, in_specs=list(in_specs) + [pl.Bl...]
    dot_general x2 -> x0, matrix products: 4.75 us -> none  [the longest x1 2.39 us: body(): lax.dot_general(hidden_act, grad_rows, (((0,), (0,)), ((), ())), preferre...]
    ppermute x24 -> x27, starting transfers between devices: 23.9 us -> 27.6 us  [exchange(): return lax.ppermute(block, axis, [(i, i ^ 1 << bit) for i in range(count)])]
    convert_element_type x9 -> x0, other arithmetic: 2.57 us -> none  [halve(): (keep.astype(jnp.float32) + got.astype(jnp.float32)).astype(jnp.bfloat16)]
    unnamed x12, local copies, waits for them, and re-layouts: 0.03 us -> 2.47 us
    dynamic_slice x1 -> x0, local copies, waits for them, and re-layouts: 2.31 us -> none  [body(): lax.dynamic_index_in_dim(grad_t, 1 - side, 1, keepdims=False)]
    squeeze x13 -> x0, local copies, waits for them, and re-layouts: 1.5 us -> none  [the longest x9 1.43 us: halve(): send = lax.dynamic_index_in_dim(block, 1 - mine, dim, keepdims=False)]
  transfers between devices with their start and end apart: 24 -> 27, of which waited for: 14 -> 17; matrix products, arithmetic and copies ran while one was open for 6% -> 0% of each run, Pallas kernels for 13% -> 28%
where the time goes in v2:
time: 128 us; the launch traced here: 127 us
  waiting for transfers between devices  58.9 us (46%)
  Pallas kernels  36.3 us (28%)
  starting transfers between devices  27.6 us (22%)
  local copies, waits for them, and re-layouts  3.74 us (3%)
    ppermute x27, waiting for transfers between devices, exchange(): return lax.ppermute(block, axis, [(i, i ^ 1 << bit) for i in range(count)])  58.9 us
    pallas_call x25, Pallas kernels, call(): pl.pallas_call(run, out_shape=out_shape, in_specs=list(in_specs) + [pl.Bl...  35.3 us
    ppermute x27, starting transfers between devices, exchange(): return lax.ppermute(block, axis, [(i, i ^ 1 << bit) for i in range(count)])  27.6 us
  transfers between devices with their start and end apart: 27, of which 17 were waited for; matrix products, arithmetic and copies ran while one was open for 0% of the time, Pallas kernels for 28%

profile of v2, /device:TPU:0, one launch (start us, length us, event | category | flops | bytes accessed | tf_op | source)
XLA Modules:
  0.0 127.5 jit_solution(15749762964030629671)
XLA Ops:
  1.9 3.0 %collective-permute-start = (bf16[512,512]{1,0:T(8,128)(2,1)S(1)}, bf16[512,512]{1,0:T(8,128)(2,1)S(1)}, u32[]{:S(2)}, u32[]{:S(2)}) collective-permute-start(bf16[512,512]{1,0:T(8,128)(2,1)S(1)} %bitcast.109), channel_id=1, source_target_pairs={{0,1},{1,0},{2,3},{3,2},{4,5},{5,4},{6,7},{7,6},{8,9},{9,8},{10,11... | collective-permute-start | bytes 1572872 | tf_op jit(solution)/shard_map/ppermute | solution.py:45
  6.2 7.2 %forward_expand1.1 = (bf16[1024,256]{1,0:T(8,128)(2,1)S(1)}, bf16[128,2048]{1,0:T(8,128)(2,1)S(1)}, bf16[128,2048]{1,0:T(8,128)(2,1)S(1)}) custom-call(bf16[1024,512]{1,0:T(8,128)(2,1)S(1)} %bitcast.52, bf16[4608,512]{1,0:T(8,128)(2,1)} %refs_1_.3, bf16[1024,2048]{1,0:T(8,128)(2,1)} %bitcast.105), custom_call_target="tpu_custom_call" | custom-call | flops 1 | bytes 1 | tf_op jit(solution)/shard_map/forward_expand1/pallas_call | solution.py:28
  15.0 7.4 %forward_expand0.1 = (bf16[1024,256]{1,0:T(8,128)(2,1)S(1)}, bf16[128,2048]{1,0:T(8,128)(2,1)S(1)}, bf16[128,2048]{1,0:T(8,128)(2,1)S(1)}) custom-call(bf16[1024,512]{1,0:T(8,128)(2,1)S(1)} %bitcast.53, bf16[4608,512]{1,0:T(8,128)(2,1)} %refs_1_.3, bf16[1024,2048]{1,0:T(8,128)(2,1)} %bitcast.106), custom_call_target="tpu_custom_call" | custom-call | flops 1 | bytes 1 | tf_op jit(solution)/shard_map/forward_expand0/pallas_call | solution.py:28
  23.1 4.9 %hidden_grad.1 = (bf16[1024,512]{1,0:T(8,128)(2,1)S(1)}, bf16[256,1024]{1,0:T(8,128)(2,1)S(1)}, bf16[256,1024]{1,0:T(8,128)(2,1)S(1)}) custom-call(bf16[1024,256]{1,0:T(8,128)(2,1)S(1)} %get-tuple-element.56.refs_0_, bf16[1024,256]{1,0:T(8,128)(2,1)S(1)} %get-tuple-element.57.refs_1_, bf16[1024,2048]{1,0:T(8,128)(2,1)} %bitcast.107, ...), custom_call_target="tpu_custom_call" | custom-call | flops 1 | bytes 1 | tf_op jit(solution)/shard_map/hidden_grad/pallas_call | solution.py:28
  28.0 1.8 %collective-permute-start.2 = (bf16[256,1024]{1,0:T(8,128)(2,1)S(1)}, bf16[256,1024]{1,0:T(8,128)(2,1)S(1)}, u32[]{:S(2)}, u32[]{:S(2)}) collective-permute-start(bf16[256,1024]{1,0:T(8,128)(2,1)S(1)} %get-tuple-element.60), channel_id=1, source_target_pairs={{0,1},{1,0},{2,3},{3,2},{4,5},{5,4},{6,7},{7,6},{8,9},{9,8},{10,11... | collective-permute-start | bytes 1572872 | tf_op jit(solution)/shard_map/ppermute | solution.py:45
  30.0 2.7 %collective-permute-start.11 = (bf16[2,2,16,2048]{3,2,1,0:T(8,128)(2,1)S(1)}, bf16[2,2,16,2048]{3,2,1,0:T(8,128)(2,1)S(1)}, u32[]{:S(2)}, u32[]{:S(2)}) collective-permute-start(bf16[2,2,16,2048]{3,2,1,0:T(8,128)(2,1)S(1)} %get-tuple-element.78), channel_id=1, source_target_pairs={{0,4},{1,5},{2,6},{3,7},{4,0},{5,1},{6,2},{7,3},{8,12},{9,13},{10,... | collective-permute-start | bytes 786440 | tf_op jit(solution)/shard_map/ppermute | solution.py:45
  32.7 11.0 %collective-permute-done.7 = bf16[128,2048]{1,0:T(8,128)(2,1)S(1)} collective-permute-done((bf16[128,2048]{1,0:T(8,128)(2,1)S(1)}, bf16[128,2048]{1,0:T(8,128)(2,1)S(1)}, u32[]{:S(2)}, u32[]{:S(2)}) %collective-permute-start.7) | collective-permute-done | bytes 524320 | tf_op jit(solution)/shard_map/ppermute | solution.py:45
  45.5 8.4 %conv_backward.1 = bf16[1024,512]{1,0:T(8,128)(2,1)} custom-call(bf16[1024,512]{1,0:T(8,128)(2,1)S(1)} %get-tuple-element.58.refs_0_, bf16[9,512,512]{2,1,0:T(8,128)(2,1)} %bitcast.104, bf16[1024,512]{1,0:T(8,128)(2,1)S(1)} %bitcast.54), custom_call_target="tpu_custom_call" | custom-call | flops 1 | bytes 1 | tf_op jit(solution)/shard_map/conv_backward/pallas_call | solution.py:28
  55.2 1.9 %conv_grad_rows0.1 = (bf16[128,1536]{1,0:T(8,128)(2,1)S(1)}, bf16[128,1536]{1,0:T(8,128)(2,1)S(1)}) custom-call(bf16[1024,512]{1,0:T(8,128)(2,1)S(1)} %bitcast.55, bf16[512,512]{1,0:T(8,128)(2,1)S(1)} %collective-permute-done.refs_4_.refs_1_, bf16[512,512]{1,0:T(8,128)(2,1)S(1)} %collective-permute-done.1.refs_2_, ...), custom_call_target="tpu_custom_call" | custom-call | flops 1 | bytes 1 | tf_op jit(solution)/shard_map/conv_grad_rows0/pallas_call | solution.py:28
  57.1 2.6 %collective-permute-start.9 = (bf16[128,1536]{1,0:T(8,128)(2,1)S(1)}, bf16[128,1536]{1,0:T(8,128)(2,1)S(1)}, u32[]{:S(2)}, u32[]{:S(2)}) collective-permute-start(bf16[128,1536]{1,0:T(8,128)(2,1)S(1)} %get-tuple-element.76), channel_id=1, source_target_pairs={{0,2},{1,3},{2,0},{3,1},{4,6},{5,7},{6,4},{7,5},{8,10},{9,11},{10,... | collective-permute-start | bytes 1179656 | tf_op jit(solution)/shard_map/ppermute | solution.py:45
  60.3 2.1 %conv_grad_rows1.1 = (bf16[128,1536]{1,0:T(8,128)(2,1)S(1)}, bf16[128,1536]{1,0:T(8,128)(2,1)S(1)}) custom-call(bf16[1024,512]{1,0:T(8,128)(2,1)S(1)} %bitcast.56, bf16[512,512]{1,0:T(8,128)(2,1)S(1)} %collective-permute-done.refs_4_.refs_1_, bf16[512,512]{1,0:T(8,128)(2,1)S(1)} %collective-permute-done.1.refs_2_, ...), custom_call_target="tpu_custom_call" | custom-call | flops 1 | bytes 1 | tf_op jit(solution)/shard_map/conv_grad_rows1/pallas_call | solution.py:28
  62.5 3.7 %collective-permute-done.13 = bf16[4,1,16,2048]{3,2,1,0:T(8,128)(2,1)S(1)} collective-permute-done((bf16[4,1,16,2048]{3,2,1,0:T(8,128)(2,1)S(1)}, bf16[4,1,16,2048]{3,2,1,0:T(8,128)(2,1)S(1)}, u32[]{:S(2)}, u32[]{:S(2)}) %collective-permute-start.13) | collective-permute-done | bytes 262176 | tf_op jit(solution)/shard_map/ppermute | solution.py:45
  67.8 4.0 %collective-permute-done.9 = bf16[128,1536]{1,0:T(8,128)(2,1)S(1)} collective-permute-done((bf16[128,1536]{1,0:T(8,128)(2,1)S(1)}, bf16[128,1536]{1,0:T(8,128)(2,1)S(1)}, u32[]{:S(2)}, u32[]{:S(2)}) %collective-permute-start.9) | collective-permute-done | bytes 393248 | tf_op jit(solution)/shard_map/ppermute | solution.py:45
  72.0 1.9 %conv_grad_rows2.1 = (bf16[128,1536]{1,0:T(8,128)(2,1)S(1)}, bf16[128,1536]{1,0:T(8,128)(2,1)S(1)}) custom-call(bf16[1024,512]{1,0:T(8,128)(2,1)S(1)} %bitcast.57, bf16[512,512]{1,0:T(8,128)(2,1)S(1)} %collective-permute-done.refs_4_.refs_1_, bf16[512,512]{1,0:T(8,128)(2,1)S(1)} %collective-permute-done.1.refs_2_, ...), custom_call_target="tpu_custom_call" | custom-call | flops 1 | bytes 1 | tf_op jit(solution)/shard_map/conv_grad_rows2/pallas_call | solution.py:28
  75.6 6.2 %collective-permute-done.12 = bf16[4,1,16,1536]{3,2,1,0:T(8,128)(2,1)S(1)} collective-permute-done((bf16[4,1,16,1536]{3,2,1,0:T(8,128)(2,1)S(1)}, bf16[4,1,16,1536]{3,2,1,0:T(8,128)(2,1)S(1)}, u32[]{:S(2)}, u32[]{:S(2)}) %collective-permute-start.12) | collective-permute-done | bytes 196640 | tf_op jit(solution)/shard_map/ppermute | solution.py:45
  83.5 3.4 %collective-permute-start.6 = (bf16[4,1,16,1536]{3,2,1,0:T(8,128)(2,1)S(1)}, bf16[4,1,16,1536]{3,2,1,0:T(8,128)(2,1)S(1)}, u32[]{:S(2)}, u32[]{:S(2)}) collective-permute-start(bf16[4,1,16,1536]{3,2,1,0:T(8,128)(2,1)S(1)} %get-tuple-element.68), channel_id=1, source_target_pairs={{0,4},{1,5},{2,6},{3,7},{4,0},{5,1},{6,2},{7,3},{8,12},{9,13},{10,... | collective-permute-start | bytes 589832 | tf_op jit(solution)/shard_map/ppermute | solution.py:45
  88.5 4.8 %collective-permute-done.6 = bf16[4,1,16,1536]{3,2,1,0:T(8,128)(2,1)S(1)} collective-permute-done((bf16[4,1,16,1536]{3,2,1,0:T(8,128)(2,1)S(1)}, bf16[4,1,16,1536]{3,2,1,0:T(8,128)(2,1)S(1)}, u32[]{:S(2)}, u32[]{:S(2)}) %collective-permute-start.6) | collective-permute-done | bytes 196640 | tf_op jit(solution)/shard_map/ppermute | solution.py:45
  93.4 1.8 %collective-permute-start.18 = (bf16[1,2,16,1536]{3,2,1,0:T(8,128)(2,1)S(1)}, bf16[1,2,16,1536]{3,2,1,0:T(8,128)(2,1)S(1)}, u32[]{:S(2)}, u32[]{:S(2)}) collective-permute-start(bf16[1,2,16,1536]{3,2,1,0:T(8,128)(2,1)S(1)} %get-tuple-element.94), channel_id=1, source_target_pairs={{0,16},{8,24},{16,0},{24,8},{1,17},{9,25},{17,1},{25,9},{2,18},{10... | collective-permute-start | bytes 294920 | tf_op jit(solution)/shard_map/ppermute | solution.py:45
  99.7 3.4 %collective-permute-done.4 = bf16[4,1,16,1536]{3,2,1,0:T(8,128)(2,1)S(1)} collective-permute-done((bf16[4,1,16,1536]{3,2,1,0:T(8,128)(2,1)S(1)}, bf16[4,1,16,1536]{3,2,1,0:T(8,128)(2,1)S(1)}, u32[]{:S(2)}, u32[]{:S(2)}) %collective-permute-start.4) | collective-permute-done | bytes 196640 | tf_op jit(solution)/shard_map/ppermute | solution.py:45
  103.7 4.1 %collective-permute-done.20 = bf16[1,2,16,1536]{3,2,1,0:T(8,128)(2,1)S(1)} collective-permute-done((bf16[1,2,16,1536]{3,2,1,0:T(8,128)(2,1)S(1)}, bf16[1,2,16,1536]{3,2,1,0:T(8,128)(2,1)S(1)}, u32[]{:S(2)}, u32[]{:S(2)}) %collective-permute-start.20) | collective-permute-done | bytes 98336 | tf_op jit(solution)/shard_map/ppermute | solution.py:45
  109.9 3.3 %collective-permute-done.22 = f32[32,128]{1,0:T(8,128)S(1)} collective-permute-done((f32[32,128]{1,0:T(8,128)S(1)}, f32[32,128]{1,0:T(8,128)S(1)}, u32[]{:S(2)}, u32[]{:S(2)}) %collective-permute-start.22) | collective-permute-done | bytes 16416 | tf_op jit(solution)/shard_map/ppermute | solution.py:45
  113.1 3.7 %collective-permute-done.23 = f32[32,128]{1,0:T(8,128)S(1)} collective-permute-done((f32[32,128]{1,0:T(8,128)S(1)}, f32[32,128]{1,0:T(8,128)S(1)}, u32[]{:S(2)}, u32[]{:S(2)}) %collective-permute-start.23) | collective-permute-done | bytes 16416 | tf_op jit(solution)/shard_map/ppermute | solution.py:45
  117.5 4.1 %collective-permute-done.24 = f32[32,128]{1,0:T(8,128)S(1)} collective-permute-done((f32[32,128]{1,0:T(8,128)S(1)}, f32[32,128]{1,0:T(8,128)S(1)}, u32[]{:S(2)}, u32[]{:S(2)}) %collective-permute-start.24) | collective-permute-done | bytes 16416 | tf_op jit(solution)/shard_map/ppermute | solution.py:45
  123.2 3.2 %collective-permute-done.26 = f32[32,128]{1,0:T(8,128)S(1)} collective-permute-done((f32[32,128]{1,0:T(8,128)S(1)}, f32[32,128]{1,0:T(8,128)S(1)}, u32[]{:S(2)}, u32[]{:S(2)}) %collective-permute-start.26) | collective-permute-done | bytes 16416 | tf_op jit(solution)/shard_map/ppermute | solution.py:45
  (74 shorter events, 26.2 us)
Async XLA Ops:
  1.9 21.2 %collective-permute-start = (bf16[512,512]{1,0:T(8,128)(2,1)S(1)}, bf16[512,512]{1,0:T(8,128)(2,1)S(1)}, u32[]{:S(2)}, u32[]{:S(2)}) collective-permute-start(bf16[512,512]{1,0:T(8,128)(2,1)S(1)} %bitcast.109), channel_id=1, source_target_pairs={{0,1},{1,0},{2,3},{3,2},{4,5},{5,4},{6,7},{7,6},{8,9},{9,8},{10,11... | collective-permute-start | bytes 1572872 | tf_op jit(solution)/shard_map/ppermute | solution.py:45
  13.4 16.5 %collective-permute-start.8 = (bf16[128,2048]{1,0:T(8,128)(2,1)S(1)}, bf16[128,2048]{1,0:T(8,128)(2,1)S(1)}, u32[]{:S(2)}, u32[]{:S(2)}) collective-permute-start(bf16[128,2048]{1,0:T(8,128)(2,1)S(1)} %get-tuple-element.73), channel_id=1, source_target_pairs={{0,2},{1,3},{2,0},{3,1},{4,6},{5,7},{6,4},{7,5},{8,10},{9,11},{10,... | collective-permute-start | bytes 1572872 | tf_op jit(solution)/shard_map/ppermute | solution.py:45
  22.4 21.3 %collective-permute-start.7 = (bf16[128,2048]{1,0:T(8,128)(2,1)S(1)}, bf16[128,2048]{1,0:T(8,128)(2,1)S(1)}, u32[]{:S(2)}, u32[]{:S(2)}) collective-permute-start(bf16[128,2048]{1,0:T(8,128)(2,1)S(1)} %get-tuple-element.70), channel_id=1, source_target_pairs={{0,2},{1,3},{2,0},{3,1},{4,6},{5,7},{6,4},{7,5},{8,10},{9,11},{10,... | collective-permute-start | bytes 1572872 | tf_op jit(solution)/shard_map/ppermute | solution.py:45
  22.9 31.1 %collective-permute-start.1 = (bf16[512,512]{1,0:T(8,128)(2,1)S(1)}, bf16[512,512]{1,0:T(8,128)(2,1)S(1)}, u32[]{:S(2)}, u32[]{:S(2)}) collective-permute-start(bf16[512,512]{1,0:T(8,128)(2,1)S(1)} %bitcast.108), channel_id=1, source_target_pairs={{0,1},{1,0},{2,3},{3,2},{4,5},{5,4},{6,7},{7,6},{8,9},{9,8},{10,11... | collective-permute-start | bytes 1572872 | tf_op jit(solution)/shard_map/ppermute | solution.py:45
  28.0 25.9 %collective-permute-start.2 = (bf16[256,1024]{1,0:T(8,128)(2,1)S(1)}, bf16[256,1024]{1,0:T(8,128)(2,1)S(1)}, u32[]{:S(2)}, u32[]{:S(2)}) collective-permute-start(bf16[256,1024]{1,0:T(8,128)(2,1)S(1)} %get-tuple-element.60), channel_id=1, source_target_pairs={{0,1},{1,0},{2,3},{3,2},{4,5},{5,4},{6,7},{7,6},{8,9},{9,8},{10,11... | collective-permute-start | bytes 1572872 | tf_op jit(solution)/shard_map/ppermute | solution.py:45
  30.0 29.6 %collective-permute-start.11 = (bf16[2,2,16,2048]{3,2,1,0:T(8,128)(2,1)S(1)}, bf16[2,2,16,2048]{3,2,1,0:T(8,128)(2,1)S(1)}, u32[]{:S(2)}, u32[]{:S(2)}) collective-permute-start(bf16[2,2,16,2048]{3,2,1,0:T(8,128)(2,1)S(1)} %get-tuple-element.78), channel_id=1, source_target_pairs={{0,4},{1,5},{2,6},{3,7},{4,0},{5,1},{6,2},{7,3},{8,12},{9,13},{10,... | collective-permute-start | bytes 786440 | tf_op jit(solution)/shard_map/ppermute | solution.py:45
  43.8 15.8 %collective-permute-start.10 = (bf16[2,2,16,2048]{3,2,1,0:T(8,128)(2,1)S(1)}, bf16[2,2,16,2048]{3,2,1,0:T(8,128)(2,1)S(1)}, u32[]{:S(2)}, u32[]{:S(2)}) collective-permute-start(bf16[2,2,16,2048]{3,2,1,0:T(8,128)(2,1)S(1)} %get-tuple-element.77), channel_id=1, source_target_pairs={{0,4},{1,5},{2,6},{3,7},{4,0},{5,1},{6,2},{7,3},{8,12},{9,13},{10,... | collective-permute-start | bytes 786440 | tf_op jit(solution)/shard_map/ppermute | solution.py:45
  57.1 14.7 %collective-permute-start.9 = (bf16[128,1536]{1,0:T(8,128)(2,1)S(1)}, bf16[128,1536]{1,0:T(8,128)(2,1)S(1)}, u32[]{:S(2)}, u32[]{:S(2)}) collective-permute-start(bf16[128,1536]{1,0:T(8,128)(2,1)S(1)} %get-tuple-element.76), channel_id=1, source_target_pairs={{0,2},{1,3},{2,0},{3,1},{4,6},{5,7},{6,4},{7,5},{8,10},{9,11},{10,... | collective-permute-start | bytes 1179656 | tf_op jit(solution)/shard_map/ppermute | solution.py:45
  59.8 6.4 %collective-permute-start.13 = (bf16[4,1,16,2048]{3,2,1,0:T(8,128)(2,1)S(1)}, bf16[4,1,16,2048]{3,2,1,0:T(8,128)(2,1)S(1)}, u32[]{:S(2)}, u32[]{:S(2)}) collective-permute-start(bf16[4,1,16,2048]{3,2,1,0:T(8,128)(2,1)S(1)} %get-tuple-element.82), channel_id=1, source_target_pairs={{0,1},{1,0},{2,3},{3,2},{4,5},{5,4},{6,7},{7,6},{8,9},{9,8},{10,11... | collective-permute-start | bytes 786440 | tf_op jit(solution)/shard_map/ppermute | solution.py:45
  62.4 21.0 %collective-permute-start.5 = (bf16[128,1536]{1,0:T(8,128)(2,1)S(1)}, bf16[128,1536]{1,0:T(8,128)(2,1)S(1)}, u32[]{:S(2)}, u32[]{:S(2)}) collective-permute-start(bf16[128,1536]{1,0:T(8,128)(2,1)S(1)} %get-tuple-element.66), channel_id=1, source_target_pairs={{0,2},{1,3},{2,0},{3,1},{4,6},{5,7},{6,4},{7,5},{8,10},{9,11},{10,... | collective-permute-start | bytes 1179656 | tf_op jit(solution)/shard_map/ppermute | solution.py:45
  66.3 7.7 %collective-permute-start.14 = (bf16[1,2,16,2048]{3,2,1,0:T(8,128)(2,1)S(1)}, bf16[1,2,16,2048]{3,2,1,0:T(8,128)(2,1)S(1)}, u32[]{:S(2)}, u32[]{:S(2)}) collective-permute-start(bf16[1,2,16,2048]{3,2,1,0:T(8,128)(2,1)S(1)} %get-tuple-element.84), channel_id=1, source_target_pairs={{0,16},{8,24},{16,0},{24,8},{1,17},{9,25},{17,1},{25,9},{2,18},{10... | collective-permute-start | bytes 393224 | tf_op jit(solution)/shard_map/ppermute | solution.py:45
  71.9 10.0 %collective-permute-start.12 = (bf16[4,1,16,1536]{3,2,1,0:T(8,128)(2,1)S(1)}, bf16[4,1,16,1536]{3,2,1,0:T(8,128)(2,1)S(1)}, u32[]{:S(2)}, u32[]{:S(2)}) collective-permute-start(bf16[4,1,16,1536]{3,2,1,0:T(8,128)(2,1)S(1)} %get-tuple-element.81), channel_id=1, source_target_pairs={{0,4},{1,5},{2,6},{3,7},{4,0},{5,1},{6,2},{7,3},{8,12},{9,13},{10,... | collective-permute-start | bytes 589832 | tf_op jit(solution)/shard_map/ppermute | solution.py:45
  73.8 21.4 %collective-permute-start.3 = (bf16[128,1536]{1,0:T(8,128)(2,1)S(1)}, bf16[128,1536]{1,0:T(8,128)(2,1)S(1)}, u32[]{:S(2)}, u32[]{:S(2)}) collective-permute-start(bf16[128,1536]{1,0:T(8,128)(2,1)S(1)} %get-tuple-element.62), channel_id=1, source_target_pairs={{0,2},{1,3},{2,0},{3,1},{4,6},{5,7},{6,4},{7,5},{8,10},{9,11},{10,... | collective-permute-start | bytes 1179656 | tf_op jit(solution)/shard_map/ppermute | solution.py:45
  74.0 1.4 %collective-permute-start.15 = (bf16[2,1,16,2048]{3,2,0,1:T(8,128)(2,1)S(1)}, bf16[2,1,16,2048]{3,2,0,1:T(8,128)(2,1)S(1)}, u32[]{:S(2)}, u32[]{:S(2)}) collective-permute-start(bf16[2,1,16,2048]{3,2,0,1:T(8,128)(2,1)S(1)} %bitcast.100), channel_id=1, source_target_pairs={{0,8},{8,0},{16,24},{24,16},{1,9},{9,1},{17,25},{25,17},{2,10},{10... | collective-permute-start | bytes 393224 | tf_op jit(solution)/shard_map/ppermute | solution.py:45
  81.9 5.1 %collective-permute-start.16 = (bf16[1,2,16,1536]{3,2,1,0:T(8,128)(2,1)S(1)}, bf16[1,2,16,1536]{3,2,1,0:T(8,128)(2,1)S(1)}, u32[]{:S(2)}, u32[]{:S(2)}) collective-permute-start(bf16[1,2,16,1536]{3,2,1,0:T(8,128)(2,1)S(1)} %get-tuple-element.89), channel_id=1, source_target_pairs={{0,16},{8,24},{16,0},{24,8},{1,17},{9,25},{17,1},{25,9},{2,18},{10... | collective-permute-start | bytes 294920 | tf_op jit(solution)/shard_map/ppermute | solution.py:45
  83.5 9.8 %collective-permute-start.6 = (bf16[4,1,16,1536]{3,2,1,0:T(8,128)(2,1)S(1)}, bf16[4,1,16,1536]{3,2,1,0:T(8,128)(2,1)S(1)}, u32[]{:S(2)}, u32[]{:S(2)}) collective-permute-start(bf16[4,1,16,1536]{3,2,1,0:T(8,128)(2,1)S(1)} %get-tuple-element.68), channel_id=1, source_target_pairs={{0,4},{1,5},{2,6},{3,7},{4,0},{5,1},{6,2},{7,3},{8,12},{9,13},{10,... | collective-permute-start | bytes 589832 | tf_op jit(solution)/shard_map/ppermute | solution.py:45
  87.0 1.4 %collective-permute-start.17 = (bf16[2,1,16,1536]{3,2,0,1:T(8,128)(2,1)S(1)}, bf16[2,1,16,1536]{3,2,0,1:T(8,128)(2,1)S(1)}, u32[]{:S(2)}, u32[]{:S(2)}) collective-permute-start(bf16[2,1,16,1536]{3,2,0,1:T(8,128)(2,1)S(1)} %bitcast.101), channel_id=1, source_target_pairs={{0,8},{8,0},{16,24},{24,16},{1,9},{9,1},{17,25},{25,17},{2,10},{10... | collective-permute-start | bytes 294920 | tf_op jit(solution)/shard_map/ppermute | solution.py:45
  93.4 4.7 %collective-permute-start.18 = (bf16[1,2,16,1536]{3,2,1,0:T(8,128)(2,1)S(1)}, bf16[1,2,16,1536]{3,2,1,0:T(8,128)(2,1)S(1)}, u32[]{:S(2)}, u32[]{:S(2)}) collective-permute-start(bf16[1,2,16,1536]{3,2,1,0:T(8,128)(2,1)S(1)} %get-tuple-element.94), channel_id=1, source_target_pairs={{0,16},{8,24},{16,0},{24,8},{1,17},{9,25},{17,1},{25,9},{2,18},{10... | collective-permute-start | bytes 294920 | tf_op jit(solution)/shard_map/ppermute | solution.py:45
  95.3 7.7 %collective-permute-start.4 = (bf16[4,1,16,1536]{3,2,1,0:T(8,128)(2,1)S(1)}, bf16[4,1,16,1536]{3,2,1,0:T(8,128)(2,1)S(1)}, u32[]{:S(2)}, u32[]{:S(2)}) collective-permute-start(bf16[4,1,16,1536]{3,2,1,0:T(8,128)(2,1)S(1)} %get-tuple-element.64), channel_id=1, source_target_pairs={{0,4},{1,5},{2,6},{3,7},{4,0},{5,1},{6,2},{7,3},{8,12},{9,13},{10,... | collective-permute-start | bytes 589832 | tf_op jit(solution)/shard_map/ppermute | solution.py:45
  103.1 4.7 %collective-permute-start.20 = (bf16[1,2,16,1536]{3,2,1,0:T(8,128)(2,1)S(1)}, bf16[1,2,16,1536]{3,2,1,0:T(8,128)(2,1)S(1)}, u32[]{:S(2)}, u32[]{:S(2)}) collective-permute-start(bf16[1,2,16,1536]{3,2,1,0:T(8,128)(2,1)S(1)} %get-tuple-element.99), channel_id=1, source_target_pairs={{0,16},{8,24},{16,0},{24,8},{1,17},{9,25},{17,1},{25,9},{2,18},{10... | collective-permute-start | bytes 294920 | tf_op jit(solution)/shard_map/ppermute | solution.py:45
  109.3 3.8 %collective-permute-start.22 = (f32[32,128]{1,0:T(8,128)S(1)}, f32[32,128]{1,0:T(8,128)S(1)}, u32[]{:S(2)}, u32[]{:S(2)}) collective-permute-start(f32[32,128]{1,0:T(8,128)S(1)} %get-tuple-element.102), channel_id=1, source_target_pairs={{0,1},{1,0},{2,3},{3,2},{4,5},{5,4},{6,7},{7,6},{8,9},{9,8},{10,11... | collective-permute-start | bytes 49160 | tf_op jit(solution)/shard_map/ppermute | solution.py:45
  113.1 3.7 %collective-permute-start.23 = (f32[32,128]{1,0:T(8,128)S(1)}, f32[32,128]{1,0:T(8,128)S(1)}, u32[]{:S(2)}, u32[]{:S(2)}) collective-permute-start(f32[32,128]{1,0:T(8,128)S(1)} %add.15), channel_id=1, source_target_pairs={{0,2},{1,3},{2,0},{3,1},{4,6},{5,7},{6,4},{7,5},{8,10},{9,11},{10,... | collective-permute-start | bytes 49160 | tf_op jit(solution)/shard_map/ppermute | solution.py:45
  116.9 4.6 %collective-permute-start.24 = (f32[32,128]{1,0:T(8,128)S(1)}, f32[32,128]{1,0:T(8,128)S(1)}, u32[]{:S(2)}, u32[]{:S(2)}) collective-permute-start(f32[32,128]{1,0:T(8,128)S(1)} %add.16), channel_id=1, source_target_pairs={{0,4},{1,5},{2,6},{3,7},{4,0},{5,1},{6,2},{7,3},{8,12},{9,13},{10,... | collective-permute-start | bytes 49160 | tf_op jit(solution)/shard_map/ppermute | solution.py:45
  122.7 3.7 %collective-permute-start.26 = (f32[32,128]{1,0:T(8,128)S(1)}, f32[32,128]{1,0:T(8,128)S(1)}, u32[]{:S(2)}, u32[]{:S(2)}) collective-permute-start(f32[32,128]{1,0:T(8,128)S(1)} %add.18), channel_id=1, source_target_pairs={{0,16},{8,24},{16,0},{24,8},{1,17},{9,25},{17,1},{25,9},{2,18},{10... | collective-permute-start | bytes 49160 | tf_op jit(solution)/shard_map/ppermute | solution.py:45
  (9 other events, 147.7 us)

commit v3 on v2

--- a/solution.py
+++ b/solution.py
@@ -205,7 +205,8 @@
     return grad, *turned
 
 
-def backward_kernel(shape, d_ref, w_ref, x_ref, out_ref, taps_ref):
+def backward_kernel(shape, d_ref, w_ref, x_ref, out_ref, token_ref, taps_ref):
+    token_ref[...] = jnp.zeros(token_ref.shape, token_ref.dtype)
     images, height, across, channels = shape
     fill_row_taps(d_ref, taps_ref, images, height, across, False)
     block = channels // 2
@@ -226,19 +227,20 @@
         out_ref[:, columns] = jnp.where(keep, total, 0.0).astype(out_ref.dtype)
 
 
-def backward(hidden_grad, weight, x, shape):
+def backward(hidden_grad, weight, x, shape, after):
     rows, channels = x.shape
     wide = weight.shape[1]
     return call(
         functools.partial(backward_kernel, shape),
         "conv_backward",
-        half((rows, channels)),
+        [half((rows, channels)), jax.ShapeDtypeStruct((8, LANES), jnp.float32)],
         (hidden_grad, weight.reshape(9, channels, wide), x),
+        after,
         scratch=[pltpu.VMEM((rows, 3 * wide), jnp.bfloat16)],
     )
 
 
-def kernel_grad_kernel(tap_y, bit, step, shape, x_count, *refs):
+def kernel_grad_kernel(taps, bit, step, shape, x_count, *refs):
     images, height, across, channels = shape
     area = height * across
     x_refs = refs[:x_count]
@@ -246,23 +248,31 @@
     out_refs = refs[x_count + 2 : -2]
     x_ref, d_ref = refs[-2:]
     rows = d_refs[0].shape[1]
-    first = 0
-    for ref in x_refs:
-        for image in range(ref.shape[0] // area):
-            block = ref[image * area : (image + 1) * area, :]
-            block = jnp.maximum(block, jnp.zeros((), block.dtype))
-            blank = jnp.zeros((across, channels), block.dtype)
-            if tap_y == 0:
-                x_ref[first : first + across, :] = blank
-                x_ref[first + across : first + area, :] = block[: area - across]
-            elif tap_y == 1:
-                x_ref[first : first + area, :] = block
-            else:
-                x_ref[first : first + area - across, :] = block[across:]
-                x_ref[first + area - across : first + area, :] = blank
-            first += area
+
+    def fill(tap_y):
+        first = 0
+        for ref in x_refs:
+            for image in range(ref.shape[0] // area):
+                block = ref[image * area : (image + 1) * area, :]
+                block = jnp.maximum(block, jnp.zeros((), block.dtype))
+                blank = jnp.zeros((across, channels), block.dtype)
+                if tap_y == 0:
+                    x_ref[first : first + across, :] = blank
+                    x_ref[first + across : first + area, :] = block[: area - across]
+                elif tap_y == 1:
+                    x_ref[first : first + area, :] = block
+                else:
+                    x_ref[first : first + area - across, :] = block[across:]
+                    x_ref[first + area - across : first + area, :] = blank
+                first += area
+
     place = lax.rem(lax.broadcasted_iota(jnp.int32, d_refs[0].shape, 1), across)
-    for tap_x in range(3):
+    filled = None
+    for index, tap in enumerate(taps):
+        tap_y, tap_x = divmod(tap, 3)
+        if tap_y != filled:
+            fill(tap_y)
+            filled = tap_y
         for source, ref in enumerate(d_refs):
             block = ref[...]
             if tap_x != 1:
@@ -271,21 +281,21 @@
                 block = jnp.where(valid, wide, 0.0).astype(block.dtype)
             d_ref[:, source * rows : (source + 1) * rows] = block
         total = jnp.dot(d_ref[...], x_ref[...], preferred_element_type=jnp.float32) / rows
-        columns = slice(tap_x * channels, (tap_x + 1) * channels)
+        columns = slice(index * channels, (index + 1) * channels)
         if len(out_refs) == 2:
             store_split(total, bit, step, *out_refs, 0, columns)
         else:
             out_refs[0][:, columns] = total.astype(jnp.bfloat16)
 
 
-def kernel_grad(tap_y, xs, ds, shape, bit, own, after):
+def kernel_grad(taps, xs, ds, shape, bit, own, after):
     channels = shape[3]
     wide, rows = ds[0].shape
     parts = 2 if fused_split(own) else 1
     grads = call(
-        functools.partial(kernel_grad_kernel, tap_y, bit, own << (bit - 1), shape, len(xs)),
-        f"conv_grad_rows{tap_y}",
-        [half((wide // parts, 3 * channels))] * parts,
+        functools.partial(kernel_grad_kernel, taps, bit, own << (bit - 1), shape, len(xs)),
+        f"conv_grad_{taps[0]}_{taps[-1]}",
+        [half((wide // parts, len(taps) * channels))] * parts,
         (*xs, *ds),
         after,
         scratch=[
@@ -298,49 +308,71 @@
     return grads
 
 
+def added(kept, got):
+    return kept.astype(jnp.float32) + got.astype(jnp.float32)
+
+
 def merge_kernel(axis, bit, *refs):
-    count = (len(refs) - 2) // 2
     send_ref, keep_ref = refs[-2:]
     mine = my_bit(axis, bit)
     first = 0
-    for index in range(count):
-        kept, got = refs[2 * index : 2 * index + 2]
-        last = first + kept.shape[0]
+    for kept, got in zip(refs[:-2:2], refs[1:-2:2]):
+        columns = slice(first, first + kept.shape[-1])
         for out_ref, side in ((keep_ref, mine), (send_ref, 1 - mine)):
-            total = kept[:, side].astype(jnp.float32) + got[:, side].astype(jnp.float32)
-            out_ref[first:last] = total.astype(out_ref.dtype)
-        first = last
-
-
-def merge(parts, leading, axis, bit, after=(), name="merge"):
+            out_ref[..., columns] = added(kept[:, side], got[:, side]).astype(out_ref.dtype)
+        first = columns.stop
+
+
+def merge_halves_kernel(axis, bit, *refs):
+    send_ref, keep_ref = refs[-2:]
+    mine = my_bit(axis, bit)
+    zero, one = (added(kept[...], got[...]) for kept, got in zip(refs[:-2:2], refs[1:-2:2]))
+    keep_ref[...] = jnp.where(mine == 0, zero, one).astype(keep_ref.dtype)
+    send_ref[...] = jnp.where(mine == 0, one, zero).astype(send_ref.dtype)
+
+
+def merge(parts, lead, axis, bit, name, after=(), halves=False):
+    own = parts[0][0].shape[-2]
+    sides = 1 if halves else 2
     flat = []
-    for kept, got, lead in zip(*zip(*parts), leading):
-        for block in (kept, got):
-            flat.append(block.reshape((lead, 2, -1) + block.shape[-2:]))
-    lead, _, middle, own, wide = flat[0].shape
-    out = half((sum(leading), middle, own, wide))
-    return call(functools.partial(merge_kernel, axis, bit), name, [out] * 2, flat, after)
-
-
-def spread_kernel(bit, kept, got, send_ref, keep_ref):
+    for pair in parts:
+        for block in pair:
+            wide = block.shape[-1]
+            shape = (lead, -1, own, wide) if halves else (lead, 2, block.size // (lead * 2 * own * wide), own, wide)
+            flat.append(block.reshape(shape))
+    middle = flat[0].shape[-3]
+    wide = flat[0].shape[-1] if halves else sum(block.shape[-1] for block in flat[::2])
+    kernel = merge_halves_kernel if halves else merge_kernel
+    out = half((lead, middle, own, wide))
+    send, keep = call(functools.partial(kernel, axis, bit), name, [out] * 2, flat, after)
+    return keep, exchange(send, axis, bit)
+
+
+def spread_kernel(bit, *refs):
+    send_ref, keep_ref = refs[-2:]
     mine = my_bit("outer", bit)
-    sources = kept.shape[0]
-    for index, ref in enumerate((kept, got)):
-        place = slice(index * sources, (index + 1) * sources)
-        keep_ref[place] = ref[:, mine]
-        send_ref[place] = ref[:, 1 - mine]
-
-
-def spread(kept, got, bit, after=()):
-    sources, left, own, wide = kept.shape
-    out = half((2 * sources, left // 2, own, wide))
-    args = [block.reshape(sources, 2, left // 2, own, wide) for block in (kept, got)]
-    return call(functools.partial(spread_kernel, bit), "spread", [out] * 2, args, after)
-
-
-def gram_kernel(offset, *refs):
+    first = 0
+    for kept, got in zip(refs[:-2:2], refs[1:-2:2]):
+        columns = slice(first, first + kept.shape[-1])
+        sources = kept.shape[0]
+        for index, ref in enumerate((kept, got)):
+            place = slice(index * sources, (index + 1) * sources)
+            keep_ref[place, :, :, columns] = ref[:, mine]
+            send_ref[place, :, :, columns] = ref[:, 1 - mine]
+        first = columns.stop
+
+
+def spread(parts, bit, name, after=()):
+    sources, left, own, _ = parts[0][0].shape
+    args = [block.reshape(sources, 2, left // 2, own, -1) for pair in parts for block in pair]
+    out = half((2 * sources, left // 2, own, sum(block.shape[-1] for block in args[::2])))
+    send, keep = call(functools.partial(spread_kernel, bit), name, [out] * 2, args, after)
+    return keep, exchange(send, "outer", bit)
+
+
+def gram_kernel(offset, has_before, last, *refs):
     kept, got = refs[:2]
-    v_ref, out_ref = refs[-2:]
+    v_ref, out_ref = refs[2 + has_before : 4 + has_before]
     sources, rows, width = kept.shape
     count = 2 * sources
     levels = count.bit_length() - 1
@@ -358,7 +390,7 @@
                 vectors[high] = jnp.where(mine == 0, b, a)
     for index, vector in enumerate(vectors):
         v_ref[index] = vector.astype(v_ref.dtype)
-    if len(refs) == 5:
+    if has_before:
         out_ref[...] = refs[2][...]
     else:
         out_ref[...] = jnp.zeros(out_ref.shape, jnp.float32)
@@ -367,20 +399,24 @@
         folded = sum(product[:, g : g + LANES] for g in range(0, width, LANES))
         row = offset + index
         out_ref[row : row + 1, :] += jnp.sum(folded, axis=0, keepdims=True)
-
-
-def gram(kept, got, offset, before, after=()):
-    sources, _, own, wide = kept.shape
-    args = [block.reshape(sources, own, wide) for block in (kept, got)]
+    if last:
+        row_ref = refs[4 + has_before]
+        totals = jnp.sum(out_ref[...], axis=1, keepdims=True)
+        rows = out_ref.shape[0]
+        spot = lax.broadcasted_iota(jnp.int32, (rows, LANES), 1) == lax.broadcasted_iota(jnp.int32, (rows, LANES), 0)
+        line = jnp.sum(jnp.where(spot, totals, 0.0), axis=0, keepdims=True)
+        row_ref[...] = jnp.broadcast_to(line[None], row_ref.shape)
+
+
+def gram(part, offset, before=None, devices=0):
+    sources, _, own, wide = part[0].shape
+    args = [block.reshape(sources, own, wide) for block in part]
     if before is not None:
         args.append(before)
-    return call(
-        functools.partial(gram_kernel, offset),
-        "gram",
-        [half((2 * sources, own, wide)), jax.ShapeDtypeStruct((2 * stat_rows(2 * sources), LANES), jnp.float32)],
-        args,
-        after,
-    )
+    out = [half((2 * sources, own, wide)), jax.ShapeDtypeStruct((2 * stat_rows(2 * sources), LANES), jnp.float32)]
+    if devices:
+        out.append(jax.ShapeDtypeStruct((devices, 1, LANES), jnp.float32))
+    return call(functools.partial(gram_kernel, offset, int(before is not None), devices > 0), "gram", out, args)
 
 
 def pairs_of(count):
@@ -418,12 +454,14 @@
     conv_refs = refs[1 : 1 + pieces]
     expand_ref, conv_m_ref, expand_m_ref, conv_out, expand_out = refs[1 + pieces :]
     count, rows, _ = expand_ref.shape
+    line = jnp.sum(stats_ref[...], axis=0)
+    place_in_row = lax.broadcasted_iota(jnp.int32, line.shape, 1)
 
     def apply(offset, v_refs, m_ref, out_ref):
         table = {}
         for index, pair in enumerate(pairs_of(count)):
-            lane = stats_ref[offset + index : offset + index + 1, :]
-            table[pair] = jnp.broadcast_to(jnp.sum(lane, axis=1, keepdims=True), (1, LANES))
+            value = jnp.sum(jnp.where(place_in_row == offset + index, line, 0.0), axis=1, keepdims=True)
+            table[pair] = jnp.broadcast_to(value, (1, LANES))
         coefs = adasum_coefs(table, count)
         stride = sum(ref.shape[2] for ref in v_refs) // LANES
         group = 0
@@ -468,9 +506,7 @@
     top = outer_bits - 1
 
     x_own = inputs.reshape(rows, channels)
-    cut = images // 2 * height * across
-    x_first = exchange(x_own[:cut], "inner", 0)
-    x_second = exchange(x_own[cut:], "inner", 0)
+    x_other = exchange(x_own, "inner", 0)
     cot = cotangent.reshape(rows, wide)
 
     hidden, expand = [], []
@@ -478,70 +514,66 @@
         block, send, keep = front(index, x_own, conv_weight, cot, shape, 1, own)
         hidden.append(block)
         expand.append((keep, exchange(send, "inner", 1)))
-    hidden_grad, d_send, d_own = hidden_gradient(hidden, cot, expand_weight, own, (x_first,))
+    hidden_grad, d_send, d_own = hidden_gradient(hidden, cot, expand_weight, own, ())
     d_other = exchange(d_send, "inner", 0)
-    input_grad = backward(hidden_grad, conv_weight, x_own, shape).reshape(shape)
-
-    parts = expand
-    halves = outer_count // 2
+
+    lead = outer_count // 2
+    first, second = (tuple(block.reshape(-1, own, wide) for block in part) for part in expand)
+    after = (hidden_grad,)
     for bit in range(2, inner_bits):
-        lead = halves << (inner_bits - 1 - bit)
-        merged = []
-        for kept, got in parts:
-            shaped = [b.reshape(-1, 2, own, wide) for b in (kept, got)]
-            send, keep = merge([shaped], [lead], "inner", bit, name="merge_expand_z")
-            merged.append((keep, exchange(send, "inner", bit)))
-        parts = merged
-    early = [keep for keep, _ in parts]
-
-    def to_owner(send, keep, after):
-        got = exchange(send, "outer", top)
+        first = merge([first], lead << (inner_bits - 1 - bit), "inner", bit, "merge_first_z", after)
+        after = (first[0],)
+    input_grad, token = backward(hidden_grad, conv_weight, x_own, shape, (x_other, *after))
+    second = merge([second], lead << (inner_bits - 2), "inner", 0, "merge_second_y", (token,))
+
+    conv = []
+    after = (second[0],)
+    for taps in ((0, 1, 2, 3), (4, 5, 6), (7, 8)):
+        send, keep = kernel_grad(taps, (x_own, x_other), (d_own, d_other), shape, 1, own, after)
+        conv.append(tuple(b.reshape(-1, own, len(taps) * channels) for b in (keep, exchange(send, "inner", 1))))
+        after = (keep,)
+    first = merge([first], lead, "inner", 0, "merge_first_y", after)
+
+    def along_z(part, lead, name, after):
+        for bit in range(2, inner_bits):
+            part = merge([part], lead << (inner_bits - 1 - bit), "inner", bit, name, after)
+            after = (part[0],)
+        return part
+
+    def along_x(parts, name, after, halves=False):
+        return merge(parts, 1, "outer", top, name, after, halves)
+
+    def along_core(part, name, after):
         for bit in reversed(range(top)):
-            send, keep = spread(keep, got, bit, after)
-            got = exchange(send, "outer", bit)
-        return keep, got
-
-    conv = []
-    for tap_y in range(3):
-        after = tuple(early) + (input_grad,) if tap_y == 0 else ()
-        send, keep = kernel_grad(tap_y, (x_own, x_first, x_second), (d_own, d_other), shape, 1, own, after)
-        conv.append((keep, exchange(send, "inner", 1)))
-
-    shaped = [[b.reshape(-1, own, wide) for b in pair] for pair in parts]
-    send, keep = merge(shaped, [halves] * 2, "inner", 0, name="merge_expand_y")
-    expand_y = (keep, exchange(send, "inner", 0))
-
-    stats = None
-    ready = []
-    expand_all = None
-    for tap_y, (keep, got) in enumerate(conv):
-        for bit in range(2, inner_bits):
-            lead = outer_count << (inner_bits - 1 - bit)
-            shaped = [b.reshape(-1, own, 3 * channels) for b in (keep, got)]
-            after = (expand_y[0],) if tap_y == 0 else ()
-            send, keep = merge([shaped], [lead], "inner", bit, after, name="merge_conv_z")
-            got = exchange(send, "inner", bit)
-        ready.append((keep, got))
-
-    shaped = [b.reshape(-1, own, wide) for b in expand_y]
-    send, keep = merge([shaped], [1], "outer", top, name="merge_expand_x")
-    kept, got = to_owner(send, keep, ())
-    expand_all, stats = gram(kept, got, stat_rows(outer_count), None)
-
-    conv_all = []
-    for tap_y, (keep, got) in enumerate(ready):
-        shaped = [b.reshape(-1, own, 3 * channels) for b in (keep, got)]
-        after = (stats,)
-        send, keep = merge([shaped], [1], "outer", top, after, name="merge_conv_x")
-        kept, got = to_owner(send, keep, ())
-        vectors, stats = gram(kept, got, 0, stats)
-        conv_all.append(vectors)
-
-    for axis, bits in (("inner", inner_bits), ("outer", outer_bits)):
-        for bit in range(bits):
-            stats = stats + exchange(stats, axis, bit)
+            part = spread([part], bit, name, after)
+            after = (part[0],)
+        return part
+
+    at = stat_rows(outer_count)
+    conv[0] = along_z(conv[0], outer_count, "merge_conv0_z", (first[0],))
+    second = along_z(second, lead, "merge_second_z", (conv[0][0],))
+
+    conv[1] = along_z(conv[1], outer_count, "merge_conv1_z", (second[0],))
+    conv[0] = along_x(conv[:1], "merge_conv0_x", (conv[1][0],))
+    expand = along_x([first, second], "merge_expand_x", (conv[0][0],), True)
+
+    conv[2] = along_z(conv[2], outer_count, "merge_conv2_z", (expand[0],))
+    conv[1] = along_x(conv[1:2], "merge_conv1_x", (conv[2][0],))
+    expand = along_core(expand, "spread_expand", (conv[1][0],))
+    conv[0] = along_core(conv[0], "spread_conv0", (expand[0],))
+
+    conv[2] = along_x(conv[2:], "merge_conv2_x", (conv[0][0],))
+    conv[1] = along_core(conv[1], "spread_conv1", (conv[2][0],))
+    expand_all, stats = gram(expand, at)
+    conv[0], stats = gram(conv[0], 0, stats)
+
+    conv[2] = along_core(conv[2], "spread_conv2", (stats,))
+    conv[1], stats = gram(conv[1], 0, stats)
+    conv[2], _, row = gram(conv[2], 0, stats, outer_count * inner_count)
+    stats = lax.all_to_all(row, ("outer", "inner"), 0, 0, tiled=True)
+    conv_all = conv
     conv_new, expand_new = finish(stats, conv_all, expand_all, conv_momentum, expand_momentum)
-    return (input_grad, conv_new, expand_new)
+    return (input_grad.reshape(shape), conv_new, expand_new)
 
 
 def solution(mesh):

time: 128 us -> 114 us (0.89)
  waiting for transfers between devices: 58.9 us -> 39.3 us
  blocking collectives: 0 us -> 8.88 us
  local copies, waits for them, and re-layouts: 3.74 us -> 1.28 us
  starting transfers between devices: 27.6 us -> 26.1 us
    ppermute x27 -> x22, waiting for transfers between devices: 58.9 us -> 39.3 us  [exchange(): return lax.ppermute(block, axis, [(i, i ^ 1 << bit) for i in range(count)])]
    all_to_all x0 -> x1, blocking collectives: none -> 8.88 us  [body(): stats = lax.all_to_all(row, ('outer', 'inner'), 0, 0, tiled=True)]
    ppermute x27 -> x22, starting transfers between devices: 27.6 us -> 26.1 us  [exchange(): return lax.ppermute(block, axis, [(i, i ^ 1 << bit) for i in range(count)])]
    pallas_call x25 -> x26, Pallas kernels: 35.3 us -> 35.9 us  [call(): pl.pallas_call(run, out_shape=out_shape, in_specs=list(in_specs) + [pl.Bl...]
  transfers between devices with their start and end apart: 27 -> 22, of which waited for: 17 -> 11; matrix products, arithmetic and copies ran while one was open for 0% -> 0% of each run, Pallas kernels for 28% -> 29%
where the time goes in v3:
time: 114 us; the launch traced here: 113 us
  waiting for transfers between devices  39.3 us (34%)
  Pallas kernels  37 us (32%)
  starting transfers between devices  26.1 us (23%)
  blocking collectives  8.88 us (8%)
  local copies, waits for them, and re-layouts  1.28 us (1%)
    ppermute x22, waiting for transfers between devices, exchange(): return lax.ppermute(block, axis, [(i, i ^ 1 << bit) for i in range(count)])  39.3 us
    pallas_call x26, Pallas kernels, call(): pl.pallas_call(run, out_shape=out_shape, in_specs=list(in_specs) + [pl.Bl...  35.9 us
    ppermute x22, starting transfers between devices, exchange(): return lax.ppermute(block, axis, [(i, i ^ 1 << bit) for i in range(count)])  26.1 us
    all_to_all x1, blocking collectives, body(): stats = lax.all_to_all(row, ('outer', 'inner'), 0, 0, tiled=True)  8.88 us
  transfers between devices with their start and end apart: 22, of which 11 were waited for; matrix products, arithmetic and copies ran while one was open for 0% of the time, Pallas kernels for 29%

profile of v3, /device:TPU:0, one launch (start us, length us, event | category | flops | bytes accessed | tf_op | source)
XLA Modules:
  0.0 113.4 jit_solution(1488105434506224216)
XLA Ops:
  0.6 3.0 %collective-permute-start = (bf16[1024,512]{1,0:T(8,128)(2,1)}, bf16[1024,512]{1,0:T(8,128)(2,1)S(1)}, u32[]{:S(2)}, u32[]{:S(2)}) collective-permute-start(bf16[1024,512]{1,0:T(8,128)(2,1)} %bitcast.54), channel_id=1, source_target_pairs={{0,1},{1,0},{2,3},{3,2},{4,5},{5,4},{6,7},{7,6},{8,9},{9,8},{10,11... | collective-permute-start | bytes 3145736 | tf_op jit(solution)/shard_map/ppermute | solution.py:45
  4.9 7.2 %forward_expand0.1 = (bf16[1024,256]{1,0:T(8,128)(2,1)S(1)}, bf16[128,2048]{1,0:T(8,128)(2,1)S(1)}, bf16[128,2048]{1,0:T(8,128)(2,1)S(1)}) custom-call(bf16[1024,512]{1,0:T(8,128)(2,1)S(1)} %bitcast.55, bf16[4608,512]{1,0:T(8,128)(2,1)} %refs_1_.3, bf16[1024,2048]{1,0:T(8,128)(2,1)} %bitcast.110), custom_call_target="tpu_custom_call" | custom-call | flops 1 | bytes 1 | tf_op jit(solution)/shard_map/forward_expand0/pallas_call | solution.py:28
  12.1 1.6 %collective-permute-start.1 = (bf16[128,2048]{1,0:T(8,128)(2,1)S(1)}, bf16[128,2048]{1,0:T(8,128)(2,1)S(1)}, u32[]{:S(2)}, u32[]{:S(2)}) collective-permute-start(bf16[128,2048]{1,0:T(8,128)(2,1)S(1)} %get-tuple-element.64), channel_id=1, source_target_pairs={{0,2},{1,3},{2,0},{3,1},{4,6},{5,7},{6,4},{7,5},{8,10},{9,11},{10,... | collective-permute-start | bytes 1572872 | tf_op jit(solution)/shard_map/ppermute | solution.py:45
  13.8 7.4 %forward_expand1.1 = (bf16[1024,256]{1,0:T(8,128)(2,1)S(1)}, bf16[128,2048]{1,0:T(8,128)(2,1)S(1)}, bf16[128,2048]{1,0:T(8,128)(2,1)S(1)}) custom-call(bf16[1024,512]{1,0:T(8,128)(2,1)S(1)} %bitcast.56, bf16[4608,512]{1,0:T(8,128)(2,1)} %refs_1_.3, bf16[1024,2048]{1,0:T(8,128)(2,1)} %bitcast.111), custom_call_target="tpu_custom_call" | custom-call | flops 1 | bytes 1 | tf_op jit(solution)/shard_map/forward_expand1/pallas_call | solution.py:28
  21.6 4.9 %hidden_grad.1 = (bf16[1024,512]{1,0:T(8,128)(2,1)S(1)}, bf16[256,1024]{1,0:T(8,128)(2,1)S(1)}, bf16[256,1024]{1,0:T(8,128)(2,1)S(1)}) custom-call(bf16[1024,256]{1,0:T(8,128)(2,1)S(1)} %get-tuple-element.60.refs_0_, bf16[1024,256]{1,0:T(8,128)(2,1)S(1)} %get-tuple-element.61.refs_1_, bf16[1024,2048]{1,0:T(8,128)(2,1)} %bitcast.112, ...), custom_call_target="tpu_custom_call" | custom-call | flops 1 | bytes 1 | tf_op jit(solution)/shard_map/hidden_grad/pallas_call | solution.py:28
  27.2 8.4 %conv_backward.1 = (bf16[1024,512]{1,0:T(8,128)(2,1)}, f32[8,128]{1,0:T(8,128)S(1)}) custom-call(bf16[1024,512]{1,0:T(8,128)(2,1)S(1)} %get-tuple-element.62.refs_2_.refs_0_, bf16[9,512,512]{2,1,0:T(8,128)(2,1)} %bitcast.109, bf16[1024,512]{1,0:T(8,128)(2,1)S(1)} %bitcast.57, bf16[1024,512]{1,0:T(8,128)(2,1)S(1)} %collective-permute-done.refs_3_.refs_1_, ...), custom_call_target="tpu_custom_call" | custom-call | flops 1 | bytes 1 | tf_op jit(solution)/shard_map/conv_backward/pallas_call | solution.py:28
  36.9 2.6 %collective-permute-done.2.refs_3_ = bf16[256,1024]{1,0:T(8,128)(2,1)S(1)} collective-permute-done((bf16[256,1024]{1,0:T(8,128)(2,1)S(1)}, bf16[256,1024]{1,0:T(8,128)(2,1)S(1)}, u32[]{:S(2)}, u32[]{:S(2)}) %collective-permute-start.2) | collective-permute-done | bytes 524320 | tf_op jit(solution)/shard_map/ppermute | solution.py:45
  39.6 2.5 %conv_grad_0_3.1 = (bf16[128,2048]{1,0:T(8,128)(2,1)S(1)}, bf16[128,2048]{1,0:T(8,128)(2,1)S(1)}) custom-call(bf16[1024,512]{1,0:T(8,128)(2,1)S(1)} %bitcast.58, bf16[1024,512]{1,0:T(8,128)(2,1)S(1)} %collective-permute-done.refs_3_.refs_1_, bf16[256,1024]{1,0:T(8,128)(2,1)S(1)} %get-tuple-element.67.refs_2_, ...), custom_call_target="tpu_custom_call" | custom-call | flops 1 | bytes 1 | tf_op jit(solution)/shard_map/conv_grad_0_3/pallas_call | solution.py:28
  42.0 1.5 %collective-permute-start.8 = (bf16[128,2048]{1,0:T(8,128)(2,1)S(1)}, bf16[128,2048]{1,0:T(8,128)(2,1)S(1)}, u32[]{:S(2)}, u32[]{:S(2)}) collective-permute-start(bf16[128,2048]{1,0:T(8,128)(2,1)S(1)} %get-tuple-element.81), channel_id=1, source_target_pairs={{0,2},{1,3},{2,0},{3,1},{4,6},{5,7},{6,4},{7,5},{8,10},{9,11},{10,... | collective-permute-start | bytes 1572872 | tf_op jit(solution)/shard_map/ppermute | solution.py:45
  43.5 2.6 %collective-permute-start.5 = (bf16[2,2,16,2048]{3,2,1,0:T(8,128)(2,1)S(1)}, bf16[2,2,16,2048]{3,2,1,0:T(8,128)(2,1)S(1)}, u32[]{:S(2)}, u32[]{:S(2)}) collective-permute-start(bf16[2,2,16,2048]{3,2,1,0:T(8,128)(2,1)S(1)} %get-tuple-element.77), channel_id=1, source_target_pairs={{0,4},{1,5},{2,6},{3,7},{4,0},{5,1},{6,2},{7,3},{8,12},{9,13},{10,... | collective-permute-start | bytes 786440 | tf_op jit(solution)/shard_map/ppermute | solution.py:45
  46.1 2.1 %conv_grad_4_6.1 = (bf16[128,1536]{1,0:T(8,128)(2,1)S(1)}, bf16[128,1536]{1,0:T(8,128)(2,1)S(1)}) custom-call(bf16[1024,512]{1,0:T(8,128)(2,1)S(1)} %bitcast.59, bf16[1024,512]{1,0:T(8,128)(2,1)S(1)} %collective-permute-done.refs_3_.refs_1_, bf16[256,1024]{1,0:T(8,128)(2,1)S(1)} %get-tuple-element.67.refs_2_, ...), custom_call_target="tpu_custom_call" | custom-call | flops 1 | bytes 1 | tf_op jit(solution)/shard_map/conv_grad_4_6/pallas_call | solution.py:28
  49.4 1.3 %conv_grad_7_8.1 = (bf16[128,1024]{1,0:T(8,128)(2,1)S(1)}, bf16[128,1024]{1,0:T(8,128)(2,1)S(1)}) custom-call(bf16[1024,512]{1,0:T(8,128)(2,1)S(1)} %bitcast.60, bf16[1024,512]{1,0:T(8,128)(2,1)S(1)} %collective-permute-done.refs_3_.refs_1_, bf16[256,1024]{1,0:T(8,128)(2,1)S(1)} %get-tuple-element.67.refs_2_, ...), custom_call_target="tpu_custom_call" | custom-call | flops 1 | bytes 1 | tf_op jit(solution)/shard_map/conv_grad_7_8/pallas_call | solution.py:28
  50.6 10.9 %collective-permute-done.5 = bf16[2,2,16,2048]{3,2,1,0:T(8,128)(2,1)S(1)} collective-permute-done((bf16[2,2,16,2048]{3,2,1,0:T(8,128)(2,1)S(1)}, bf16[2,2,16,2048]{3,2,1,0:T(8,128)(2,1)S(1)}, u32[]{:S(2)}, u32[]{:S(2)}) %collective-permute-start.5) | collective-permute-done | bytes 262176 | tf_op jit(solution)/shard_map/ppermute | solution.py:45
  62.3 2.9 %collective-permute-start.10 = (bf16[4,1,16,2048]{3,2,1,0:T(8,128)(2,1)S(1)}, bf16[4,1,16,2048]{3,2,1,0:T(8,128)(2,1)S(1)}, u32[]{:S(2)}, u32[]{:S(2)}) collective-permute-start(bf16[4,1,16,2048]{3,2,1,0:T(8,128)(2,1)S(1)} %get-tuple-element.85), channel_id=1, source_target_pairs={{0,4},{1,5},{2,6},{3,7},{4,0},{5,1},{6,2},{7,3},{8,12},{9,13},{10,... | collective-permute-start | bytes 786440 | tf_op jit(solution)/shard_map/ppermute | solution.py:45
  66.1 2.9 %collective-permute-start.9 = (bf16[2,1,16,2048]{3,2,0,1:T(8,128)(2,1)S(1)}, bf16[2,1,16,2048]{3,2,0,1:T(8,128)(2,1)S(1)}, u32[]{:S(2)}, u32[]{:S(2)}) collective-permute-start(bf16[2,1,16,2048]{3,2,0,1:T(8,128)(2,1)S(1)} %bitcast.106), channel_id=1, source_target_pairs={{0,4},{1,5},{2,6},{3,7},{4,0},{5,1},{6,2},{7,3},{8,12},{9,13},{10,... | collective-permute-start | bytes 393224 | tf_op jit(solution)/shard_map/ppermute | solution.py:45
  69.0 11.4 %collective-permute-done.11 = bf16[128,1536]{1,0:T(8,128)(2,1)S(1)} collective-permute-done((bf16[128,1536]{1,0:T(8,128)(2,1)S(1)}, bf16[128,1536]{1,0:T(8,128)(2,1)S(1)}, u32[]{:S(2)}, u32[]{:S(2)}) %collective-permute-start.11) | collective-permute-done | bytes 393248 | tf_op jit(solution)/shard_map/ppermute | solution.py:45
  80.7 2.5 %collective-permute-done.9 = bf16[2,1,16,2048]{3,2,0,1:T(8,128)(2,1)S(1)} collective-permute-done((bf16[2,1,16,2048]{3,2,0,1:T(8,128)(2,1)S(1)}, bf16[2,1,16,2048]{3,2,0,1:T(8,128)(2,1)S(1)}, u32[]{:S(2)}, u32[]{:S(2)}) %collective-permute-start.9) | collective-permute-done | bytes 131104 | tf_op jit(solution)/shard_map/ppermute | solution.py:45
  83.2 1.6 %collective-permute-start.14 = (bf16[1,2,16,2048]{3,2,1,0:T(8,128)(2,1)S(1)}, bf16[1,2,16,2048]{3,2,1,0:T(8,128)(2,1)S(1)}, u32[]{:S(2)}, u32[]{:S(2)}) collective-permute-start(bf16[1,2,16,2048]{3,2,1,0:T(8,128)(2,1)S(1)} %get-tuple-element.93), channel_id=1, source_target_pairs={{0,16},{8,24},{16,0},{24,8},{1,17},{9,25},{17,1},{25,9},{2,18},{10... | collective-permute-start | bytes 393224 | tf_op jit(solution)/shard_map/ppermute | solution.py:45
  85.4 3.5 %collective-permute-start.12 = (bf16[4,1,16,1024]{3,2,1,0:T(8,128)(2,1)S(1)}, bf16[4,1,16,1024]{3,2,1,0:T(8,128)(2,1)S(1)}, u32[]{:S(2)}, u32[]{:S(2)}) collective-permute-start(bf16[4,1,16,1024]{3,2,1,0:T(8,128)(2,1)S(1)} %get-tuple-element.91), channel_id=1, source_target_pairs={{0,4},{1,5},{2,6},{3,7},{4,0},{5,1},{6,2},{7,3},{8,12},{9,13},{10,... | collective-permute-start | bytes 393224 | tf_op jit(solution)/shard_map/ppermute | solution.py:45
  88.9 5.8 %collective-permute-done.15 = bf16[4,1,16,1536]{3,2,1,0:T(8,128)(2,1)S(1)} collective-permute-done((bf16[4,1,16,1536]{3,2,1,0:T(8,128)(2,1)S(1)}, bf16[4,1,16,1536]{3,2,1,0:T(8,128)(2,1)S(1)}, u32[]{:S(2)}, u32[]{:S(2)}) %collective-permute-start.15) | collective-permute-done | bytes 196640 | tf_op jit(solution)/shard_map/ppermute | solution.py:45
  94.8 1.6 %collective-permute-start.20 = (bf16[1,2,16,1536]{3,2,1,0:T(8,128)(2,1)S(1)}, bf16[1,2,16,1536]{3,2,1,0:T(8,128)(2,1)S(1)}, u32[]{:S(2)}, u32[]{:S(2)}) collective-permute-start(bf16[1,2,16,1536]{3,2,1,0:T(8,128)(2,1)S(1)} %get-tuple-element.106), channel_id=1, source_target_pairs={{0,16},{8,24},{16,0},{24,8},{1,17},{9,25},{17,1},{25,9},{2,18},{10... | collective-permute-start | bytes 294920 | tf_op jit(solution)/shard_map/ppermute | solution.py:45
  97.8 1.7 %collective-permute-done.20 = bf16[1,2,16,1536]{3,2,1,0:T(8,128)(2,1)S(1)} collective-permute-done((bf16[1,2,16,1536]{3,2,1,0:T(8,128)(2,1)S(1)}, bf16[1,2,16,1536]{3,2,1,0:T(8,128)(2,1)S(1)}, u32[]{:S(2)}, u32[]{:S(2)}) %collective-permute-start.20) | collective-permute-done | bytes 98336 | tf_op jit(solution)/shard_map/ppermute | solution.py:45
  100.1 1.4 %collective-permute-done.16 = bf16[1,2,16,1024]{3,2,1,0:T(8,128)(2,1)S(1)} collective-permute-done((bf16[1,2,16,1024]{3,2,1,0:T(8,128)(2,1)S(1)}, bf16[1,2,16,1024]{3,2,1,0:T(8,128)(2,1)S(1)}, u32[]{:S(2)}, u32[]{:S(2)}) %collective-permute-start.16) | collective-permute-done | bytes 65568 | tf_op jit(solution)/shard_map/ppermute | solution.py:45
  103.5 8.9 %all_to_all.5.refs_0_ = f32[32,1,128]{2,1,0:T(1,128)S(1)} all-to-all(f32[32,1,128]{2,1,0:T(1,128)S(1)} %get-tuple-element.110), channel_id=1, replica_groups=mesh['outer'=4,'inner'=8] {'outer','inner'}, dimensions={0} | all-to-all | bytes 32768 | tf_op jit(solution)/shard_map/all_to_all | solution.py:573
  (58 shorter events, 12.4 us)
Async XLA Ops:
  0.6 26.5 %collective-permute-start = (bf16[1024,512]{1,0:T(8,128)(2,1)}, bf16[1024,512]{1,0:T(8,128)(2,1)S(1)}, u32[]{:S(2)}, u32[]{:S(2)}) collective-permute-start(bf16[1024,512]{1,0:T(8,128)(2,1)} %bitcast.54), channel_id=1, source_target_pairs={{0,1},{1,0},{2,3},{3,2},{4,5},{5,4},{6,7},{7,6},{8,9},{9,8},{10,11... | collective-permute-start | bytes 3145736 | tf_op jit(solution)/shard_map/ppermute | solution.py:45
  12.1 14.9 %collective-permute-start.1 = (bf16[128,2048]{1,0:T(8,128)(2,1)S(1)}, bf16[128,2048]{1,0:T(8,128)(2,1)S(1)}, u32[]{:S(2)}, u32[]{:S(2)}) collective-permute-start(bf16[128,2048]{1,0:T(8,128)(2,1)S(1)} %get-tuple-element.64), channel_id=1, source_target_pairs={{0,2},{1,3},{2,0},{3,1},{4,6},{5,7},{6,4},{7,5},{8,10},{9,11},{10,... | collective-permute-start | bytes 1572872 | tf_op jit(solution)/shard_map/ppermute | solution.py:45
  21.1 15.7 %collective-permute-start.3 = (bf16[128,2048]{1,0:T(8,128)(2,1)S(1)}, bf16[128,2048]{1,0:T(8,128)(2,1)S(1)}, u32[]{:S(2)}, u32[]{:S(2)}) collective-permute-start(bf16[128,2048]{1,0:T(8,128)(2,1)S(1)} %get-tuple-element.70), channel_id=1, source_target_pairs={{0,2},{1,3},{2,0},{3,1},{4,6},{5,7},{6,4},{7,5},{8,10},{9,11},{10,... | collective-permute-start | bytes 1572872 | tf_op jit(solution)/shard_map/ppermute | solution.py:45
  26.5 13.0 %collective-permute-start.2 = (bf16[256,1024]{1,0:T(8,128)(2,1)S(1)}, bf16[256,1024]{1,0:T(8,128)(2,1)S(1)}, u32[]{:S(2)}, u32[]{:S(2)}) collective-permute-start(bf16[256,1024]{1,0:T(8,128)(2,1)S(1)} %get-tuple-element.68), channel_id=1, source_target_pairs={{0,1},{1,0},{2,3},{3,2},{4,5},{5,4},{6,7},{7,6},{8,9},{9,8},{10,11... | collective-permute-start | bytes 1572872 | tf_op jit(solution)/shard_map/ppermute | solution.py:45
  42.0 20.2 %collective-permute-start.8 = (bf16[128,2048]{1,0:T(8,128)(2,1)S(1)}, bf16[128,2048]{1,0:T(8,128)(2,1)S(1)}, u32[]{:S(2)}, u32[]{:S(2)}) collective-permute-start(bf16[128,2048]{1,0:T(8,128)(2,1)S(1)} %get-tuple-element.81), channel_id=1, source_target_pairs={{0,2},{1,3},{2,0},{3,1},{4,6},{5,7},{6,4},{7,5},{8,10},{9,11},{10,... | collective-permute-start | bytes 1572872 | tf_op jit(solution)/shard_map/ppermute | solution.py:45
  43.5 18.0 %collective-permute-start.5 = (bf16[2,2,16,2048]{3,2,1,0:T(8,128)(2,1)S(1)}, bf16[2,2,16,2048]{3,2,1,0:T(8,128)(2,1)S(1)}, u32[]{:S(2)}, u32[]{:S(2)}) collective-permute-start(bf16[2,2,16,2048]{3,2,1,0:T(8,128)(2,1)S(1)} %get-tuple-element.77), channel_id=1, source_target_pairs={{0,4},{1,5},{2,6},{3,7},{4,0},{5,1},{6,2},{7,3},{8,12},{9,13},{10,... | collective-permute-start | bytes 786440 | tf_op jit(solution)/shard_map/ppermute | solution.py:45
  48.2 32.2 %collective-permute-start.11 = (bf16[128,1536]{1,0:T(8,128)(2,1)S(1)}, bf16[128,1536]{1,0:T(8,128)(2,1)S(1)}, u32[]{:S(2)}, u32[]{:S(2)}) collective-permute-start(bf16[128,1536]{1,0:T(8,128)(2,1)S(1)} %get-tuple-element.86), channel_id=1, source_target_pairs={{0,2},{1,3},{2,0},{3,1},{4,6},{5,7},{6,4},{7,5},{8,10},{9,11},{10,... | collective-permute-start | bytes 1179656 | tf_op jit(solution)/shard_map/ppermute | solution.py:45
  48.8 17.2 %collective-permute-start.7 = (bf16[4,1,16,2048]{3,2,1,0:T(8,128)(2,1)S(1)}, bf16[4,1,16,2048]{3,2,1,0:T(8,128)(2,1)S(1)}, u32[]{:S(2)}, u32[]{:S(2)}) collective-permute-start(bf16[4,1,16,2048]{3,2,1,0:T(8,128)(2,1)S(1)} %get-tuple-element.80), channel_id=1, source_target_pairs={{0,1},{1,0},{2,3},{3,2},{4,5},{5,4},{6,7},{7,6},{8,9},{9,8},{10,11... | collective-permute-start | bytes 786440 | tf_op jit(solution)/shard_map/ppermute | solution.py:45
  61.6 50.8 %copy-start.3 = (f32[1,73728]{1,0:T(1,128)S(1)}, f32[1,73728]{1,0:T(1,128)}, u32[]{:S(2)}) copy-start(f32[1,73728]{1,0:T(1,128)} %param.10) | copy-start | bytes 884740
  61.6 50.8 %copy-start.4 = (f32[1,32768]{1,0:T(1,128)S(1)}, f32[1,32768]{1,0:T(1,128)}, u32[]{:S(2)}) copy-start(f32[1,32768]{1,0:T(1,128)} %param.11) | copy-start | bytes 393220
  62.3 18.2 %collective-permute-start.10 = (bf16[4,1,16,2048]{3,2,1,0:T(8,128)(2,1)S(1)}, bf16[4,1,16,2048]{3,2,1,0:T(8,128)(2,1)S(1)}, u32[]{:S(2)}, u32[]{:S(2)}) collective-permute-start(bf16[4,1,16,2048]{3,2,1,0:T(8,128)(2,1)S(1)} %get-tuple-element.85), channel_id=1, source_target_pairs={{0,4},{1,5},{2,6},{3,7},{4,0},{5,1},{6,2},{7,3},{8,12},{9,13},{10,... | collective-permute-start | bytes 786440 | tf_op jit(solution)/shard_map/ppermute | solution.py:45
  65.2 20.1 %collective-permute-start.4 = (bf16[128,1024]{1,0:T(8,128)(2,1)S(1)}, bf16[128,1024]{1,0:T(8,128)(2,1)S(1)}, u32[]{:S(2)}, u32[]{:S(2)}) collective-permute-start(bf16[128,1024]{1,0:T(8,128)(2,1)S(1)} %get-tuple-element.76), channel_id=1, source_target_pairs={{0,2},{1,3},{2,0},{3,1},{4,6},{5,7},{6,4},{7,5},{8,10},{9,11},{10,... | collective-permute-start | bytes 786440 | tf_op jit(solution)/shard_map/ppermute | solution.py:45
  65.5 15.1 %collective-permute-start.6 = (bf16[2,1,16,2048]{3,2,0,1:T(8,128)(2,1)S(1)}, bf16[2,1,16,2048]{3,2,0,1:T(8,128)(2,1)S(1)}, u32[]{:S(2)}, u32[]{:S(2)}) collective-permute-start(bf16[2,1,16,2048]{3,2,0,1:T(8,128)(2,1)S(1)} %bitcast.103), channel_id=1, source_target_pairs={{0,1},{1,0},{2,3},{3,2},{4,5},{5,4},{6,7},{7,6},{8,9},{9,8},{10,11... | collective-permute-start | bytes 393224 | tf_op jit(solution)/shard_map/ppermute | solution.py:45
  66.1 17.0 %collective-permute-start.9 = (bf16[2,1,16,2048]{3,2,0,1:T(8,128)(2,1)S(1)}, bf16[2,1,16,2048]{3,2,0,1:T(8,128)(2,1)S(1)}, u32[]{:S(2)}, u32[]{:S(2)}) collective-permute-start(bf16[2,1,16,2048]{3,2,0,1:T(8,128)(2,1)S(1)} %bitcast.106), channel_id=1, source_target_pairs={{0,4},{1,5},{2,6},{3,7},{4,0},{5,1},{6,2},{7,3},{8,12},{9,13},{10,... | collective-permute-start | bytes 393224 | tf_op jit(solution)/shard_map/ppermute | solution.py:45
  80.5 14.3 %collective-permute-start.15 = (bf16[4,1,16,1536]{3,2,1,0:T(8,128)(2,1)S(1)}, bf16[4,1,16,1536]{3,2,1,0:T(8,128)(2,1)S(1)}, u32[]{:S(2)}, u32[]{:S(2)}) collective-permute-start(bf16[4,1,16,1536]{3,2,1,0:T(8,128)(2,1)S(1)} %get-tuple-element.94), channel_id=1, source_target_pairs={{0,4},{1,5},{2,6},{3,7},{4,0},{5,1},{6,2},{7,3},{8,12},{9,13},{10,... | collective-permute-start | bytes 589832 | tf_op jit(solution)/shard_map/ppermute | solution.py:45
  83.2 13.2 %collective-permute-start.14 = (bf16[1,2,16,2048]{3,2,1,0:T(8,128)(2,1)S(1)}, bf16[1,2,16,2048]{3,2,1,0:T(8,128)(2,1)S(1)}, u32[]{:S(2)}, u32[]{:S(2)}) collective-permute-start(bf16[1,2,16,2048]{3,2,1,0:T(8,128)(2,1)S(1)} %get-tuple-element.93), channel_id=1, source_target_pairs={{0,16},{8,24},{16,0},{24,8},{1,17},{9,25},{17,1},{25,9},{2,18},{10... | collective-permute-start | bytes 393224 | tf_op jit(solution)/shard_map/ppermute | solution.py:45
  84.8 11.7 %collective-permute-start.13 = (bf16[1,2,16,2048]{3,2,1,0:T(8,128)(2,1)S(1)}, bf16[1,2,16,2048]{3,2,1,0:T(8,128)(2,1)S(1)}, u32[]{:S(2)}, u32[]{:S(2)}) collective-permute-start(bf16[1,2,16,2048]{3,2,1,0:T(8,128)(2,1)S(1)} %get-tuple-element.92), channel_id=1, source_target_pairs={{0,16},{8,24},{16,0},{24,8},{1,17},{9,25},{17,1},{25,9},{2,18},{10... | collective-permute-start | bytes 393224 | tf_op jit(solution)/shard_map/ppermute | solution.py:45
  85.4 11.7 %collective-permute-start.12 = (bf16[4,1,16,1024]{3,2,1,0:T(8,128)(2,1)S(1)}, bf16[4,1,16,1024]{3,2,1,0:T(8,128)(2,1)S(1)}, u32[]{:S(2)}, u32[]{:S(2)}) collective-permute-start(bf16[4,1,16,1024]{3,2,1,0:T(8,128)(2,1)S(1)} %get-tuple-element.91), channel_id=1, source_target_pairs={{0,4},{1,5},{2,6},{3,7},{4,0},{5,1},{6,2},{7,3},{8,12},{9,13},{10,... | collective-permute-start | bytes 393224 | tf_op jit(solution)/shard_map/ppermute | solution.py:45
  94.8 4.7 %collective-permute-start.20 = (bf16[1,2,16,1536]{3,2,1,0:T(8,128)(2,1)S(1)}, bf16[1,2,16,1536]{3,2,1,0:T(8,128)(2,1)S(1)}, u32[]{:S(2)}, u32[]{:S(2)}) collective-permute-start(bf16[1,2,16,1536]{3,2,1,0:T(8,128)(2,1)S(1)} %get-tuple-element.106), channel_id=1, source_target_pairs={{0,16},{8,24},{16,0},{24,8},{1,17},{9,25},{17,1},{25,9},{2,18},{10... | collective-permute-start | bytes 294920 | tf_op jit(solution)/shard_map/ppermute | solution.py:45
  96.4 3.2 %collective-permute-start.18 = (bf16[2,1,16,2048]{3,2,0,1:T(8,128)(2,1)S(1)}, bf16[2,1,16,2048]{3,2,0,1:T(8,128)(2,1)S(1)}, u32[]{:S(2)}, u32[]{:S(2)}) collective-permute-start(bf16[2,1,16,2048]{3,2,0,1:T(8,128)(2,1)S(1)} %bitcast.104), channel_id=1, source_target_pairs={{0,8},{8,0},{16,24},{24,16},{1,9},{9,1},{17,25},{25,17},{2,10},{10... | collective-permute-start | bytes 393224 | tf_op jit(solution)/shard_map/ppermute | solution.py:45
  96.5 3.3 %collective-permute-start.17 = (bf16[2,1,16,2048]{3,2,0,1:T(8,128)(2,1)S(1)}, bf16[2,1,16,2048]{3,2,0,1:T(8,128)(2,1)S(1)}, u32[]{:S(2)}, u32[]{:S(2)}) collective-permute-start(bf16[2,1,16,2048]{3,2,0,1:T(8,128)(2,1)S(1)} %bitcast.105), channel_id=1, source_target_pairs={{0,8},{8,0},{16,24},{24,16},{1,9},{9,1},{17,25},{25,17},{2,10},{10... | collective-permute-start | bytes 393224 | tf_op jit(solution)/shard_map/ppermute | solution.py:45
  97.1 4.3 %collective-permute-start.16 = (bf16[1,2,16,1024]{3,2,1,0:T(8,128)(2,1)S(1)}, bf16[1,2,16,1024]{3,2,1,0:T(8,128)(2,1)S(1)}, u32[]{:S(2)}, u32[]{:S(2)}) collective-permute-start(bf16[1,2,16,1024]{3,2,1,0:T(8,128)(2,1)S(1)} %get-tuple-element.99), channel_id=1, source_target_pairs={{0,16},{8,24},{16,0},{24,8},{1,17},{9,25},{17,1},{25,9},{2,18},{10... | collective-permute-start | bytes 196616 | tf_op jit(solution)/shard_map/ppermute | solution.py:45
  99.5 2.0 %collective-permute-start.21 = (bf16[2,1,16,1536]{3,2,0,1:T(8,128)(2,1)S(1)}, bf16[2,1,16,1536]{3,2,0,1:T(8,128)(2,1)S(1)}, u32[]{:S(2)}, u32[]{:S(2)}) collective-permute-start(bf16[2,1,16,1536]{3,2,0,1:T(8,128)(2,1)S(1)} %bitcast.107), channel_id=1, source_target_pairs={{0,8},{8,0},{16,24},{24,16},{1,9},{9,1},{17,25},{25,17},{2,10},{10... | collective-permute-start | bytes 294920 | tf_op jit(solution)/shard_map/ppermute | solution.py:45
  101.5 1.3 %collective-permute-start.19 = (bf16[2,1,16,1024]{3,2,0,1:T(8,128)(2,1)S(1)}, bf16[2,1,16,1024]{3,2,0,1:T(8,128)(2,1)S(1)}, u32[]{:S(2)}, u32[]{:S(2)}) collective-permute-start(bf16[2,1,16,1024]{3,2,0,1:T(8,128)(2,1)S(1)} %bitcast.108), channel_id=1, source_target_pairs={{0,8},{8,0},{16,24},{24,16},{1,9},{9,1},{17,25},{25,17},{2,10},{10... | collective-permute-start | bytes 196616 | tf_op jit(solution)/shard_map/ppermute | solution.py:45
  (3 other events, 16.3 us)

commit v4 on v3

--- a/solution.py
+++ b/solution.py
@@ -323,17 +323,16 @@
         first = columns.stop
 
 
-def merge_halves_kernel(axis, bit, *refs):
-    send_ref, keep_ref = refs[-2:]
+def merge_halves_kernel(axis, bit, kept, got, send_ref, keep_ref):
     mine = my_bit(axis, bit)
-    zero, one = (added(kept[...], got[...]) for kept, got in zip(refs[:-2:2], refs[1:-2:2]))
+    wide = keep_ref.shape[-1]
+    zero, one = (added(kept[..., columns], got[..., columns]) for columns in (slice(0, wide), slice(wide, 2 * wide)))
     keep_ref[...] = jnp.where(mine == 0, zero, one).astype(keep_ref.dtype)
     send_ref[...] = jnp.where(mine == 0, one, zero).astype(send_ref.dtype)
 
 
 def merge(parts, lead, axis, bit, name, after=(), halves=False):
     own = parts[0][0].shape[-2]
-    sides = 1 if halves else 2
     flat = []
     for pair in parts:
         for block in pair:
@@ -341,11 +340,21 @@
             shape = (lead, -1, own, wide) if halves else (lead, 2, block.size // (lead * 2 * own * wide), own, wide)
             flat.append(block.reshape(shape))
     middle = flat[0].shape[-3]
-    wide = flat[0].shape[-1] if halves else sum(block.shape[-1] for block in flat[::2])
+    wide = sum(block.shape[-1] for block in flat[::2])
+    if halves:
+        wide //= 2
     kernel = merge_halves_kernel if halves else merge_kernel
     out = half((lead, middle, own, wide))
     send, keep = call(functools.partial(kernel, axis, bit), name, [out] * 2, flat, after)
     return keep, exchange(send, axis, bit)
+
+
+def held_kernel(in_ref, out_ref):
+    out_ref[...] = in_ref[...]
+
+
+def held(block, after):
+    return call(held_kernel, "held", half(block.shape), (block,), after)
 
 
 def spread_kernel(bit, *refs):
@@ -518,21 +527,20 @@
     d_other = exchange(d_send, "inner", 0)
 
     lead = outer_count // 2
-    first, second = (tuple(block.reshape(-1, own, wide) for block in part) for part in expand)
-    after = (hidden_grad,)
-    for bit in range(2, inner_bits):
-        first = merge([first], lead << (inner_bits - 1 - bit), "inner", bit, "merge_first_z", after)
-        after = (first[0],)
-    input_grad, token = backward(hidden_grad, conv_weight, x_own, shape, (x_other, *after))
-    second = merge([second], lead << (inner_bits - 2), "inner", 0, "merge_second_y", (token,))
+    expand = [tuple(block.reshape(-1, own, wide) for block in part) for part in expand]
+    input_grad, token = backward(hidden_grad, conv_weight, x_own, shape, (x_other,))
+    expand = merge(expand, lead << (inner_bits - 2), "inner", 0, "merge_expand_y", (token,))
 
     conv = []
-    after = (second[0],)
-    for taps in ((0, 1, 2, 3), (4, 5, 6), (7, 8)):
+    after = (expand[0],)
+    for taps in ((0, 1, 2), (3, 4, 5, 6), (7, 8)):
         send, keep = kernel_grad(taps, (x_own, x_other), (d_own, d_other), shape, 1, own, after)
-        conv.append(tuple(b.reshape(-1, own, len(taps) * channels) for b in (keep, exchange(send, "inner", 1))))
+        conv.append((send.reshape(-1, own, len(taps) * channels), keep.reshape(-1, own, len(taps) * channels)))
         after = (keep,)
-    first = merge([first], lead, "inner", 0, "merge_first_y", after)
+
+    def start(index, after):
+        send, keep = conv[index]
+        conv[index] = (keep, exchange(held(send, after) if after else send, "inner", 1))
 
     def along_z(part, lead, name, after):
         for bit in range(2, inner_bits):
@@ -550,13 +558,16 @@
         return part
 
     at = stat_rows(outer_count)
-    conv[0] = along_z(conv[0], outer_count, "merge_conv0_z", (first[0],))
-    second = along_z(second, lead, "merge_second_z", (conv[0][0],))
-
-    conv[1] = along_z(conv[1], outer_count, "merge_conv1_z", (second[0],))
+    start(0, ())
+    conv[0] = along_z(conv[0], outer_count, "merge_conv0_z", after)
+    expand = along_z(expand, lead, "merge_expand_z", (conv[0][0],))
+
+    start(1, (conv[0][0],))
+    conv[1] = along_z(conv[1], outer_count, "merge_conv1_z", (expand[0],))
     conv[0] = along_x(conv[:1], "merge_conv0_x", (conv[1][0],))
-    expand = along_x([first, second], "merge_expand_x", (conv[0][0],), True)
-
+    expand = along_x([expand], "merge_expand_x", (conv[0][0],), True)
+
+    start(2, (conv[1][0],))
     conv[2] = along_z(conv[2], outer_count, "merge_conv2_z", (expand[0],))
     conv[1] = along_x(conv[1:2], "merge_conv1_x", (conv[2][0],))
     expand = along_core(expand, "spread_expand", (conv[1][0],))

time: 114 us -> 111 us (0.974)
  starting transfers between devices: 26.1 us -> 19.1 us
  waiting for transfers between devices: 39.3 us -> 41.9 us
  blocking collectives: 8.88 us -> 10.9 us
    ppermute x22 -> x20, starting transfers between devices: 26.1 us -> 19.1 us  [exchange(): return lax.ppermute(block, axis, [(i, i ^ 1 << bit) for i in range(count)])]
    ppermute x22 -> x20, waiting for transfers between devices: 39.3 us -> 41.9 us  [exchange(): return lax.ppermute(block, axis, [(i, i ^ 1 << bit) for i in range(count)])]
    all_to_all x1, blocking collectives: 8.88 us -> 10.9 us  [body(): stats = lax.all_to_all(row, ('outer', 'inner'), 0, 0, tiled=True)]
  transfers between devices with their start and end apart: 22 -> 20, of which waited for: 11 -> 11; matrix products, arithmetic and copies ran while one was open for 0% -> 0% of each run, Pallas kernels for 29% -> 30%
where the time goes in v4:
time: 111 us
  waiting for transfers between devices  41.9 us (38%)
  Pallas kernels  36.9 us (33%)
  starting transfers between devices  19.1 us (17%)
  blocking collectives  10.9 us (10%)
  local copies, waits for them, and re-layouts  1.28 us (1%)
    ppermute x20, waiting for transfers between devices, exchange(): return lax.ppermute(block, axis, [(i, i ^ 1 << bit) for i in range(count)])  41.9 us
    pallas_call x26, Pallas kernels, call(): pl.pallas_call(run, out_shape=out_shape, in_specs=list(in_specs) + [pl.Bl...  35.9 us
    ppermute x20, starting transfers between devices, exchange(): return lax.ppermute(block, axis, [(i, i ^ 1 << bit) for i in range(count)])  19.1 us
    all_to_all x1, blocking collectives, body(): stats = lax.all_to_all(row, ('outer', 'inner'), 0, 0, tiled=True)  10.9 us
  transfers between devices with their start and end apart: 20, of which 11 were waited for; matrix products, arithmetic and copies ran while one was open for 0% of the time, Pallas kernels for 30%

profile of v4, /device:TPU:0, one launch (start us, length us, event | category | flops | bytes accessed | tf_op | source)
XLA Modules:
  0.0 110.9 jit_solution(6599222911643909445)
XLA Ops:
  0.6 3.0 %collective-permute-start = (bf16[1024,512]{1,0:T(8,128)(2,1)}, bf16[1024,512]{1,0:T(8,128)(2,1)S(1)}, u32[]{:S(2)}, u32[]{:S(2)}) collective-permute-start(bf16[1024,512]{1,0:T(8,128)(2,1)} %bitcast.52), channel_id=1, source_target_pairs={{0,1},{1,0},{2,3},{3,2},{4,5},{5,4},{6,7},{7,6},{8,9},{9,8},{10,11... | collective-permute-start | bytes 3145736 | tf_op jit(solution)/shard_map/ppermute | solution.py:45
  4.9 7.2 %forward_expand1.1 = (bf16[1024,256]{1,0:T(8,128)(2,1)S(1)}, bf16[128,2048]{1,0:T(8,128)(2,1)S(1)}, bf16[128,2048]{1,0:T(8,128)(2,1)S(1)}) custom-call(bf16[1024,512]{1,0:T(8,128)(2,1)S(1)} %bitcast.53, bf16[4608,512]{1,0:T(8,128)(2,1)} %refs_1_.3, bf16[1024,2048]{1,0:T(8,128)(2,1)} %bitcast.106), custom_call_target="tpu_custom_call" | custom-call | flops 1 | bytes 1 | tf_op jit(solution)/shard_map/forward_expand1/pallas_call | solution.py:28
  12.1 1.6 %collective-permute-start.3 = (bf16[128,2048]{1,0:T(8,128)(2,1)S(1)}, bf16[128,2048]{1,0:T(8,128)(2,1)S(1)}, u32[]{:S(2)}, u32[]{:S(2)}) collective-permute-start(bf16[128,2048]{1,0:T(8,128)(2,1)S(1)} %get-tuple-element.65), channel_id=1, source_target_pairs={{0,2},{1,3},{2,0},{3,1},{4,6},{5,7},{6,4},{7,5},{8,10},{9,11},{10,... | collective-permute-start | bytes 1572872 | tf_op jit(solution)/shard_map/ppermute | solution.py:45
  13.8 7.4 %forward_expand0.1 = (bf16[1024,256]{1,0:T(8,128)(2,1)S(1)}, bf16[128,2048]{1,0:T(8,128)(2,1)S(1)}, bf16[128,2048]{1,0:T(8,128)(2,1)S(1)}) custom-call(bf16[1024,512]{1,0:T(8,128)(2,1)S(1)} %bitcast.54, bf16[4608,512]{1,0:T(8,128)(2,1)} %refs_1_.3, bf16[1024,2048]{1,0:T(8,128)(2,1)} %bitcast.107), custom_call_target="tpu_custom_call" | custom-call | flops 1 | bytes 1 | tf_op jit(solution)/shard_map/forward_expand0/pallas_call | solution.py:28
  21.7 4.8 %hidden_grad.1 = (bf16[1024,512]{1,0:T(8,128)(2,1)S(1)}, bf16[256,1024]{1,0:T(8,128)(2,1)S(1)}, bf16[256,1024]{1,0:T(8,128)(2,1)S(1)}) custom-call(bf16[1024,256]{1,0:T(8,128)(2,1)S(1)} %get-tuple-element.56.refs_0_, bf16[1024,256]{1,0:T(8,128)(2,1)S(1)} %get-tuple-element.57.refs_1_, bf16[1024,2048]{1,0:T(8,128)(2,1)} %bitcast.108, ...), custom_call_target="tpu_custom_call" | custom-call | flops 1 | bytes 1 | tf_op jit(solution)/shard_map/hidden_grad/pallas_call | solution.py:28
  27.0 8.4 %conv_backward.1 = (bf16[1024,512]{1,0:T(8,128)(2,1)}, f32[8,128]{1,0:T(8,128)S(1)}) custom-call(bf16[1024,512]{1,0:T(8,128)(2,1)S(1)} %get-tuple-element.58.refs_0_, bf16[9,512,512]{2,1,0:T(8,128)(2,1)} %bitcast.105, bf16[1024,512]{1,0:T(8,128)(2,1)S(1)} %bitcast.55, bf16[1024,512]{1,0:T(8,128)(2,1)S(1)} %collective-permute-done.refs_3_.refs_1_), custom_call_target="tpu_custom_call" | custom-call | flops 1 | bytes 1 | tf_op jit(solution)/shard_map/conv_backward/pallas_call | solution.py:28
  35.5 1.3 %collective-permute-done.2 = bf16[128,2048]{1,0:T(8,128)(2,1)S(1)} collective-permute-done((bf16[128,2048]{1,0:T(8,128)(2,1)S(1)}, bf16[128,2048]{1,0:T(8,128)(2,1)S(1)}, u32[]{:S(2)}, u32[]{:S(2)}) %collective-permute-start.2) | collective-permute-done | bytes 524320 | tf_op jit(solution)/shard_map/ppermute | solution.py:45
  37.0 2.5 %collective-permute-done.1.refs_3_ = bf16[256,1024]{1,0:T(8,128)(2,1)S(1)} collective-permute-done((bf16[256,1024]{1,0:T(8,128)(2,1)S(1)}, bf16[256,1024]{1,0:T(8,128)(2,1)S(1)}, u32[]{:S(2)}, u32[]{:S(2)}) %collective-permute-start.1) | collective-permute-done | bytes 524320 | tf_op jit(solution)/shard_map/ppermute | solution.py:45
  39.5 1.9 %conv_grad_0_2.1 = (bf16[128,1536]{1,0:T(8,128)(2,1)S(1)}, bf16[128,1536]{1,0:T(8,128)(2,1)S(1)}) custom-call(bf16[1024,512]{1,0:T(8,128)(2,1)S(1)} %bitcast.56, bf16[1024,512]{1,0:T(8,128)(2,1)S(1)} %collective-permute-done.refs_3_.refs_1_, bf16[256,1024]{1,0:T(8,128)(2,1)S(1)} %get-tuple-element.60.refs_2_, ...), custom_call_target="tpu_custom_call" | custom-call | flops 1 | bytes 1 | tf_op jit(solution)/shard_map/conv_grad_0_2/pallas_call | solution.py:28
  41.4 1.5 %collective-permute-start.4 = (bf16[8,16,1536]{2,1,0:T(8,128)(2,1)S(1)}, bf16[8,16,1536]{2,1,0:T(8,128)(2,1)S(1)}, u32[]{:S(2)}, u32[]{:S(2)}) collective-permute-start(bf16[8,16,1536]{2,1,0:T(8,128)(2,1)S(1)} %bitcast.99), channel_id=1, source_target_pairs={{0,2},{1,3},{2,0},{3,1},{4,6},{5,7},{6,4},{7,5},{8,10},{9,11},{10,... | collective-permute-start | bytes 1179656 | tf_op jit(solution)/shard_map/ppermute | solution.py:45
  43.5 2.7 %conv_grad_3_6.1 = (bf16[128,2048]{1,0:T(8,128)(2,1)S(1)}, bf16[128,2048]{1,0:T(8,128)(2,1)S(1)}) custom-call(bf16[1024,512]{1,0:T(8,128)(2,1)S(1)} %bitcast.57, bf16[1024,512]{1,0:T(8,128)(2,1)S(1)} %collective-permute-done.refs_3_.refs_1_, bf16[256,1024]{1,0:T(8,128)(2,1)S(1)} %get-tuple-element.60.refs_2_, ...), custom_call_target="tpu_custom_call" | custom-call | flops 1 | bytes 1 | tf_op jit(solution)/shard_map/conv_grad_3_6/pallas_call | solution.py:28
  46.2 1.3 %conv_grad_7_8.1 = (bf16[128,1024]{1,0:T(8,128)(2,1)S(1)}, bf16[128,1024]{1,0:T(8,128)(2,1)S(1)}) custom-call(bf16[1024,512]{1,0:T(8,128)(2,1)S(1)} %bitcast.58, bf16[1024,512]{1,0:T(8,128)(2,1)S(1)} %collective-permute-done.refs_3_.refs_1_, bf16[256,1024]{1,0:T(8,128)(2,1)S(1)} %get-tuple-element.60.refs_2_, ...), custom_call_target="tpu_custom_call" | custom-call | flops 1 | bytes 1 | tf_op jit(solution)/shard_map/conv_grad_7_8/pallas_call | solution.py:28
  47.5 3.2 %collective-permute-done.4 = bf16[8,16,1536]{2,1,0:T(8,128)(2,1)S(1)} collective-permute-done((bf16[8,16,1536]{2,1,0:T(8,128)(2,1)S(1)}, bf16[8,16,1536]{2,1,0:T(8,128)(2,1)S(1)}, u32[]{:S(2)}, u32[]{:S(2)}) %collective-permute-start.4) | collective-permute-done | bytes 393248 | tf_op jit(solution)/shard_map/ppermute | solution.py:45
  50.8 1.4 %collective-permute-start.5 = (bf16[8,16,2048]{2,1,0:T(8,128)(2,1)S(1)}, bf16[8,16,2048]{2,1,0:T(8,128)(2,1)S(1)}, u32[]{:S(2)}, u32[]{:S(2)}) collective-permute-start(bf16[8,16,2048]{2,1,0:T(8,128)(2,1)S(1)} %held.2), channel_id=1, source_target_pairs={{0,2},{1,3},{2,0},{3,1},{4,6},{5,7},{6,4},{7,5},{8,10},{9,11},{10,... | collective-permute-start | bytes 1572872 | tf_op jit(solution)/shard_map/ppermute | solution.py:45
  52.2 2.3 %collective-permute-done.6 = bf16[4,1,16,4096]{3,2,1,0:T(8,128)(2,1)S(1)} collective-permute-done((bf16[4,1,16,4096]{3,2,1,0:T(8,128)(2,1)S(1)}, bf16[4,1,16,4096]{3,2,1,0:T(8,128)(2,1)S(1)}, u32[]{:S(2)}, u32[]{:S(2)}) %collective-permute-start.6) | collective-permute-done | bytes 524320 | tf_op jit(solution)/shard_map/ppermute | solution.py:45
  54.6 2.6 %collective-permute-start.8 = (bf16[2,1,16,4096]{3,2,0,1:T(8,128)(2,1)S(1)}, bf16[2,1,16,4096]{3,2,0,1:T(8,128)(2,1)S(1)}, u32[]{:S(2)}, u32[]{:S(2)}) collective-permute-start(bf16[2,1,16,4096]{3,2,0,1:T(8,128)(2,1)S(1)} %bitcast.100), channel_id=1, source_target_pairs={{0,4},{1,5},{2,6},{3,7},{4,0},{5,1},{6,2},{7,3},{8,12},{9,13},{10,... | collective-permute-start | bytes 786440 | tf_op jit(solution)/shard_map/ppermute | solution.py:45
  57.6 17.0 %collective-permute-done.5 = bf16[8,16,2048]{2,1,0:T(8,128)(2,1)S(1)} collective-permute-done((bf16[8,16,2048]{2,1,0:T(8,128)(2,1)S(1)}, bf16[8,16,2048]{2,1,0:T(8,128)(2,1)S(1)}, u32[]{:S(2)}, u32[]{:S(2)}) %collective-permute-start.5) | collective-permute-done | bytes 524320 | tf_op jit(solution)/shard_map/ppermute | solution.py:45
  74.9 1.6 %collective-permute-start.13 = (bf16[4,1,16,2048]{3,2,1,0:T(8,128)(2,1)S(1)}, bf16[4,1,16,2048]{3,2,1,0:T(8,128)(2,1)S(1)}, u32[]{:S(2)}, u32[]{:S(2)}) collective-permute-start(bf16[4,1,16,2048]{3,2,1,0:T(8,128)(2,1)S(1)} %get-tuple-element.86), channel_id=1, source_target_pairs={{0,4},{1,5},{2,6},{3,7},{4,0},{5,1},{6,2},{7,3},{8,12},{9,13},{10,... | collective-permute-start | bytes 786440 | tf_op jit(solution)/shard_map/ppermute | solution.py:45
  76.6 1.5 %collective-permute-start.12 = (bf16[1,2,16,2048]{3,2,1,0:T(8,128)(2,1)S(1)}, bf16[1,2,16,2048]{3,2,1,0:T(8,128)(2,1)S(1)}, u32[]{:S(2)}, u32[]{:S(2)}) collective-permute-start(bf16[1,2,16,2048]{3,2,1,0:T(8,128)(2,1)S(1)} %get-tuple-element.85), channel_id=1, source_target_pairs={{0,16},{8,24},{16,0},{24,8},{1,17},{9,25},{17,1},{25,9},{2,18},{10... | collective-permute-start | bytes 393224 | tf_op jit(solution)/shard_map/ppermute | solution.py:45
  78.7 4.9 %collective-permute-done.7 = bf16[8,16,1024]{2,1,0:T(8,128)(2,1)S(1)} collective-permute-done((bf16[8,16,1024]{2,1,0:T(8,128)(2,1)S(1)}, bf16[8,16,1024]{2,1,0:T(8,128)(2,1)S(1)}, u32[]{:S(2)}, u32[]{:S(2)}) %collective-permute-start.7) | collective-permute-done | bytes 262176 | tf_op jit(solution)/shard_map/ppermute | solution.py:45
  83.9 6.3 %collective-permute-done.13 = bf16[4,1,16,2048]{3,2,1,0:T(8,128)(2,1)S(1)} collective-permute-done((bf16[4,1,16,2048]{3,2,1,0:T(8,128)(2,1)S(1)}, bf16[4,1,16,2048]{3,2,1,0:T(8,128)(2,1)S(1)}, u32[]{:S(2)}, u32[]{:S(2)}) %collective-permute-start.13) | collective-permute-done | bytes 262176 | tf_op jit(solution)/shard_map/ppermute | solution.py:45
  90.3 1.6 %collective-permute-start.18 = (bf16[1,2,16,2048]{3,2,1,0:T(8,128)(2,1)S(1)}, bf16[1,2,16,2048]{3,2,1,0:T(8,128)(2,1)S(1)}, u32[]{:S(2)}, u32[]{:S(2)}) collective-permute-start(bf16[1,2,16,2048]{3,2,1,0:T(8,128)(2,1)S(1)} %get-tuple-element.98), channel_id=1, source_target_pairs={{0,16},{8,24},{16,0},{24,8},{1,17},{9,25},{17,1},{25,9},{2,18},{10... | collective-permute-start | bytes 393224 | tf_op jit(solution)/shard_map/ppermute | solution.py:45
  93.2 2.1 %collective-permute-done.18 = bf16[1,2,16,2048]{3,2,1,0:T(8,128)(2,1)S(1)} collective-permute-done((bf16[1,2,16,2048]{3,2,1,0:T(8,128)(2,1)S(1)}, bf16[1,2,16,2048]{3,2,1,0:T(8,128)(2,1)S(1)}, u32[]{:S(2)}, u32[]{:S(2)}) %collective-permute-start.18) | collective-permute-done | bytes 131104 | tf_op jit(solution)/shard_map/ppermute | solution.py:45
  99.0 10.9 %all_to_all.5.refs_0_ = f32[32,1,128]{2,1,0:T(1,128)S(1)} all-to-all(f32[32,1,128]{2,1,0:T(1,128)S(1)} %get-tuple-element.102), channel_id=1, replica_groups=mesh['outer'=4,'inner'=8] {'outer','inner'}, dimensions={0} | all-to-all | bytes 32768 | tf_op jit(solution)/shard_map/all_to_all | solution.py:584
  (54 shorter events, 11.1 us)
Async XLA Ops:
  0.6 26.4 %collective-permute-start = (bf16[1024,512]{1,0:T(8,128)(2,1)}, bf16[1024,512]{1,0:T(8,128)(2,1)S(1)}, u32[]{:S(2)}, u32[]{:S(2)}) collective-permute-start(bf16[1024,512]{1,0:T(8,128)(2,1)} %bitcast.52), channel_id=1, source_target_pairs={{0,1},{1,0},{2,3},{3,2},{4,5},{5,4},{6,7},{7,6},{8,9},{9,8},{10,11... | collective-permute-start | bytes 3145736 | tf_op jit(solution)/shard_map/ppermute | solution.py:45
  12.1 9.5 %copy-start.2 = (bf16[512,2048]{1,0:T(8,128)(2,1)S(1)}, bf16[512,2048]{1,0:T(8,128)(2,1)}, u32[]{:S(2)}) copy-start(bf16[512,2048]{1,0:T(8,128)(2,1)} %refs_3_.1) | copy-start | bytes 6291460
  12.1 23.4 %collective-permute-start.3 = (bf16[128,2048]{1,0:T(8,128)(2,1)S(1)}, bf16[128,2048]{1,0:T(8,128)(2,1)S(1)}, u32[]{:S(2)}, u32[]{:S(2)}) collective-permute-start(bf16[128,2048]{1,0:T(8,128)(2,1)S(1)} %get-tuple-element.65), channel_id=1, source_target_pairs={{0,2},{1,3},{2,0},{3,1},{4,6},{5,7},{6,4},{7,5},{8,10},{9,11},{10,... | collective-permute-start | bytes 1572872 | tf_op jit(solution)/shard_map/ppermute | solution.py:45
  21.1 5.9 %copy-start.1 = (bf16[4,16,16,512]{3,2,1,0:T(8,128)(2,1)S(1)}, bf16[4,16,16,512]{3,2,1,0:T(8,128)(2,1)}, u32[]{:S(2)}) copy-start(bf16[4,16,16,512]{3,2,1,0:T(8,128)(2,1)} %param.6) | copy-start | bytes 3145732
  21.1 15.7 %collective-permute-start.2 = (bf16[128,2048]{1,0:T(8,128)(2,1)S(1)}, bf16[128,2048]{1,0:T(8,128)(2,1)S(1)}, u32[]{:S(2)}, u32[]{:S(2)}) collective-permute-start(bf16[128,2048]{1,0:T(8,128)(2,1)S(1)} %get-tuple-element.63), channel_id=1, source_target_pairs={{0,2},{1,3},{2,0},{3,1},{4,6},{5,7},{6,4},{7,5},{8,10},{9,11},{10,... | collective-permute-start | bytes 1572872 | tf_op jit(solution)/shard_map/ppermute | solution.py:45
  26.5 13.0 %collective-permute-start.1 = (bf16[256,1024]{1,0:T(8,128)(2,1)S(1)}, bf16[256,1024]{1,0:T(8,128)(2,1)S(1)}, u32[]{:S(2)}, u32[]{:S(2)}) collective-permute-start(bf16[256,1024]{1,0:T(8,128)(2,1)S(1)} %get-tuple-element.61), channel_id=1, source_target_pairs={{0,1},{1,0},{2,3},{3,2},{4,5},{5,4},{6,7},{7,6},{8,9},{9,8},{10,11... | collective-permute-start | bytes 1572872 | tf_op jit(solution)/shard_map/ppermute | solution.py:45
  41.4 9.3 %collective-permute-start.4 = (bf16[8,16,1536]{2,1,0:T(8,128)(2,1)S(1)}, bf16[8,16,1536]{2,1,0:T(8,128)(2,1)S(1)}, u32[]{:S(2)}, u32[]{:S(2)}) collective-permute-start(bf16[8,16,1536]{2,1,0:T(8,128)(2,1)S(1)} %bitcast.99), channel_id=1, source_target_pairs={{0,2},{1,3},{2,0},{3,1},{4,6},{5,7},{6,4},{7,5},{8,10},{9,11},{10,... | collective-permute-start | bytes 1179656 | tf_op jit(solution)/shard_map/ppermute | solution.py:45
  42.9 11.6 %collective-permute-start.6 = (bf16[4,1,16,4096]{3,2,1,0:T(8,128)(2,1)S(1)}, bf16[4,1,16,4096]{3,2,1,0:T(8,128)(2,1)S(1)}, u32[]{:S(2)}, u32[]{:S(2)}) collective-permute-start(bf16[4,1,16,4096]{3,2,1,0:T(8,128)(2,1)S(1)} %get-tuple-element.75), channel_id=1, source_target_pairs={{0,1},{1,0},{2,3},{3,2},{4,5},{5,4},{6,7},{7,6},{8,9},{9,8},{10,11... | collective-permute-start | bytes 1572872 | tf_op jit(solution)/shard_map/ppermute | solution.py:45
  50.8 23.8 %collective-permute-start.5 = (bf16[8,16,2048]{2,1,0:T(8,128)(2,1)S(1)}, bf16[8,16,2048]{2,1,0:T(8,128)(2,1)S(1)}, u32[]{:S(2)}, u32[]{:S(2)}) collective-permute-start(bf16[8,16,2048]{2,1,0:T(8,128)(2,1)S(1)} %held.2), channel_id=1, source_target_pairs={{0,2},{1,3},{2,0},{3,1},{4,6},{5,7},{6,4},{7,5},{8,10},{9,11},{10,... | collective-permute-start | bytes 1572872 | tf_op jit(solution)/shard_map/ppermute | solution.py:45
  54.5 55.4 %copy-start.3 = (f32[1,73728]{1,0:T(1,128)S(1)}, f32[1,73728]{1,0:T(1,128)}, u32[]{:S(2)}) copy-start(f32[1,73728]{1,0:T(1,128)} %param.10) | copy-start | bytes 884740
  54.5 55.4 %copy-start.4 = (f32[1,32768]{1,0:T(1,128)S(1)}, f32[1,32768]{1,0:T(1,128)}, u32[]{:S(2)}) copy-start(f32[1,32768]{1,0:T(1,128)} %param.11) | copy-start | bytes 393220
  54.6 21.9 %collective-permute-start.8 = (bf16[2,1,16,4096]{3,2,0,1:T(8,128)(2,1)S(1)}, bf16[2,1,16,4096]{3,2,0,1:T(8,128)(2,1)S(1)}, u32[]{:S(2)}, u32[]{:S(2)}) collective-permute-start(bf16[2,1,16,4096]{3,2,0,1:T(8,128)(2,1)S(1)} %bitcast.100), channel_id=1, source_target_pairs={{0,4},{1,5},{2,6},{3,7},{4,0},{5,1},{6,2},{7,3},{8,12},{9,13},{10,... | collective-permute-start | bytes 786440 | tf_op jit(solution)/shard_map/ppermute | solution.py:45
  57.3 19.2 %collective-permute-start.9 = (bf16[4,1,16,1536]{3,2,1,0:T(8,128)(2,1)S(1)}, bf16[4,1,16,1536]{3,2,1,0:T(8,128)(2,1)S(1)}, u32[]{:S(2)}, u32[]{:S(2)}) collective-permute-start(bf16[4,1,16,1536]{3,2,1,0:T(8,128)(2,1)S(1)} %get-tuple-element.79), channel_id=1, source_target_pairs={{0,4},{1,5},{2,6},{3,7},{4,0},{5,1},{6,2},{7,3},{8,12},{9,13},{10,... | collective-permute-start | bytes 589832 | tf_op jit(solution)/shard_map/ppermute | solution.py:45
  74.8 8.9 %collective-permute-start.7 = (bf16[8,16,1024]{2,1,0:T(8,128)(2,1)S(1)}, bf16[8,16,1024]{2,1,0:T(8,128)(2,1)S(1)}, u32[]{:S(2)}, u32[]{:S(2)}) collective-permute-start(bf16[8,16,1024]{2,1,0:T(8,128)(2,1)S(1)} %held.3), channel_id=1, source_target_pairs={{0,2},{1,3},{2,0},{3,1},{4,6},{5,7},{6,4},{7,5},{8,10},{9,11},{10,... | collective-permute-start | bytes 786440 | tf_op jit(solution)/shard_map/ppermute | solution.py:45
  74.9 15.4 %collective-permute-start.13 = (bf16[4,1,16,2048]{3,2,1,0:T(8,128)(2,1)S(1)}, bf16[4,1,16,2048]{3,2,1,0:T(8,128)(2,1)S(1)}, u32[]{:S(2)}, u32[]{:S(2)}) collective-permute-start(bf16[4,1,16,2048]{3,2,1,0:T(8,128)(2,1)S(1)} %get-tuple-element.86), channel_id=1, source_target_pairs={{0,4},{1,5},{2,6},{3,7},{4,0},{5,1},{6,2},{7,3},{8,12},{9,13},{10,... | collective-permute-start | bytes 786440 | tf_op jit(solution)/shard_map/ppermute | solution.py:45
  76.6 15.2 %collective-permute-start.12 = (bf16[1,2,16,2048]{3,2,1,0:T(8,128)(2,1)S(1)}, bf16[1,2,16,2048]{3,2,1,0:T(8,128)(2,1)S(1)}, u32[]{:S(2)}, u32[]{:S(2)}) collective-permute-start(bf16[1,2,16,2048]{3,2,1,0:T(8,128)(2,1)S(1)} %get-tuple-element.85), channel_id=1, source_target_pairs={{0,16},{8,24},{16,0},{24,8},{1,17},{9,25},{17,1},{25,9},{2,18},{10... | collective-permute-start | bytes 393224 | tf_op jit(solution)/shard_map/ppermute | solution.py:45
  78.1 13.9 %collective-permute-start.11 = (bf16[1,2,16,1536]{3,2,1,0:T(8,128)(2,1)S(1)}, bf16[1,2,16,1536]{3,2,1,0:T(8,128)(2,1)S(1)}, u32[]{:S(2)}, u32[]{:S(2)}) collective-permute-start(bf16[1,2,16,1536]{3,2,1,0:T(8,128)(2,1)S(1)} %get-tuple-element.84), channel_id=1, source_target_pairs={{0,16},{8,24},{16,0},{24,8},{1,17},{9,25},{17,1},{25,9},{2,18},{10... | collective-permute-start | bytes 294920 | tf_op jit(solution)/shard_map/ppermute | solution.py:45
  83.7 8.8 %collective-permute-start.10 = (bf16[4,1,16,1024]{3,2,1,0:T(8,128)(2,1)S(1)}, bf16[4,1,16,1024]{3,2,1,0:T(8,128)(2,1)S(1)}, u32[]{:S(2)}, u32[]{:S(2)}) collective-permute-start(bf16[4,1,16,1024]{3,2,1,0:T(8,128)(2,1)S(1)} %get-tuple-element.83), channel_id=1, source_target_pairs={{0,4},{1,5},{2,6},{3,7},{4,0},{5,1},{6,2},{7,3},{8,12},{9,13},{10,... | collective-permute-start | bytes 393224 | tf_op jit(solution)/shard_map/ppermute | solution.py:45
  90.3 5.0 %collective-permute-start.18 = (bf16[1,2,16,2048]{3,2,1,0:T(8,128)(2,1)S(1)}, bf16[1,2,16,2048]{3,2,1,0:T(8,128)(2,1)S(1)}, u32[]{:S(2)}, u32[]{:S(2)}) collective-permute-start(bf16[1,2,16,2048]{3,2,1,0:T(8,128)(2,1)S(1)} %get-tuple-element.98), channel_id=1, source_target_pairs={{0,16},{8,24},{16,0},{24,8},{1,17},{9,25},{17,1},{25,9},{2,18},{10... | collective-permute-start | bytes 393224 | tf_op jit(solution)/shard_map/ppermute | solution.py:45
  91.9 3.6 %collective-permute-start.16 = (bf16[2,1,16,2048]{3,2,0,1:T(8,128)(2,1)S(1)}, bf16[2,1,16,2048]{3,2,0,1:T(8,128)(2,1)S(1)}, u32[]{:S(2)}, u32[]{:S(2)}) collective-permute-start(bf16[2,1,16,2048]{3,2,0,1:T(8,128)(2,1)S(1)} %bitcast.101), channel_id=1, source_target_pairs={{0,8},{8,0},{16,24},{24,16},{1,9},{9,1},{17,25},{25,17},{2,10},{10... | collective-permute-start | bytes 393224 | tf_op jit(solution)/shard_map/ppermute | solution.py:45
  92.0 3.7 %collective-permute-start.15 = (bf16[2,1,16,1536]{3,2,0,1:T(8,128)(2,1)S(1)}, bf16[2,1,16,1536]{3,2,0,1:T(8,128)(2,1)S(1)}, u32[]{:S(2)}, u32[]{:S(2)}) collective-permute-start(bf16[2,1,16,1536]{3,2,0,1:T(8,128)(2,1)S(1)} %bitcast.103), channel_id=1, source_target_pairs={{0,8},{8,0},{16,24},{24,16},{1,9},{9,1},{17,25},{25,17},{2,10},{10... | collective-permute-start | bytes 294920 | tf_op jit(solution)/shard_map/ppermute | solution.py:45
  92.6 4.3 %collective-permute-start.14 = (bf16[1,2,16,1024]{3,2,1,0:T(8,128)(2,1)S(1)}, bf16[1,2,16,1024]{3,2,1,0:T(8,128)(2,1)S(1)}, u32[]{:S(2)}, u32[]{:S(2)}) collective-permute-start(bf16[1,2,16,1024]{3,2,1,0:T(8,128)(2,1)S(1)} %get-tuple-element.91), channel_id=1, source_target_pairs={{0,16},{8,24},{16,0},{24,8},{1,17},{9,25},{17,1},{25,9},{2,18},{10... | collective-permute-start | bytes 196616 | tf_op jit(solution)/shard_map/ppermute | solution.py:45
  95.3 1.7 %collective-permute-start.19 = (bf16[2,1,16,2048]{3,2,0,1:T(8,128)(2,1)S(1)}, bf16[2,1,16,2048]{3,2,0,1:T(8,128)(2,1)S(1)}, u32[]{:S(2)}, u32[]{:S(2)}) collective-permute-start(bf16[2,1,16,2048]{3,2,0,1:T(8,128)(2,1)S(1)} %bitcast.102), channel_id=1, source_target_pairs={{0,8},{8,0},{16,24},{24,16},{1,9},{9,1},{17,25},{25,17},{2,10},{10... | collective-permute-start | bytes 393224 | tf_op jit(solution)/shard_map/ppermute | solution.py:45
  96.9 1.3 %collective-permute-start.17 = (bf16[2,1,16,1024]{3,2,0,1:T(8,128)(2,1)S(1)}, bf16[2,1,16,1024]{3,2,0,1:T(8,128)(2,1)S(1)}, u32[]{:S(2)}, u32[]{:S(2)}) collective-permute-start(bf16[2,1,16,1024]{3,2,0,1:T(8,128)(2,1)S(1)} %bitcast.104), channel_id=1, source_target_pairs={{0,8},{8,0},{16,24},{24,16},{1,9},{9,1},{17,25},{25,17},{2,10},{10... | collective-permute-start | bytes 196616 | tf_op jit(solution)/shard_map/ppermute | solution.py:45
  (1 other events, 1.3 us)
